TPU v7x, 32 devices: a whole 2x2x4 slice. The times are simulated.
32 devices in a mesh: dp: 8 (over z, y), mp: 4 (over x, core).
Axes of the slice: x: 2, y: 2, z: 4, core: 2. Of those that a mesh axis runs over, the one named last changes fastest.
Arguments:
- queries: bfloat16 [4096, 2048], P('dp', 'mp'), may hold values from -96 to 96
- out_grad: bfloat16 [4096, 2048], P('dp', 'mp'), may hold values from -0.75 to 0.75
- owner: int32 [64, 2], P('dp'), may hold values from 0 to 7, all different within a row; in each aligned block of 8 rows (0 to 7, 8 to 15, ...) at most 2 rows name the same one
- store_row: int32 [64, 2], P('dp'), may hold values from 0 to 1
- store: bfloat16 [16, 128, 4096], P('dp', None, 'mp'), may hold values from -80 to 80
- norm_gain: bfloat16 [4096], P('mp'), may hold values from 0.5 to 2
- w_key: bfloat16 [4096, 2048], P(None, 'mp'), may hold values from -0.09375 to 0.09375
- w_value: bfloat16 [4096, 2048], P(None, 'mp'), may hold values from -0.09375 to 0.09375
Outputs:
- attended: bfloat16 [4096, 2048], P('dp', 'mp')
- query_grad: bfloat16 [4096, 2048], P('dp', 'mp')
- key_weight_grad: float32 [4096, 2048], P('dp', 'mp')
- value_weight_grad: float32 [4096, 2048], P('dp', 'mp')
Inputs may be any that keep to these rules, and one draw needn't show every extreme that they name: Within the 8 spans of one index of dp no owner is named more than 2 times, and in some such block one owner is named exactly 2 times; the 2 neighbours of a span have different owners.
All inputs are finite; a program needn't handle non-finite values.
Results may differ from a plain program's by a relative error of at most 0.03.
The roundings to bfloat16 on the way count: a program that leaves them out, or rounds other values in their place, can miss the bound.
Values may be sent and summed in bfloat16 or wider, within the bound.
No kernel may reach another device: no remote copies, remote signals or barrier semaphores. Data moves between devices by JAX's collectives and lax.ppermute only.
A program may use at most 128 MiB of HBM per device.

v0:
```python
import math

import jax
import jax.numpy as jnp
from jax import lax
from jax.sharding import PartitionSpec as P

HEAD = 128


epsilon = 1e-06


def shards(queries, out_grad, owner, store_row, store, norm_gain, w_key, w_value):
    whole_store, whole_gain = (
        lax.all_gather(store, "mp", axis=2, tiled=True),
        lax.all_gather(norm_gain, "mp", axis=0, tiled=True),
    )
    stored, length, model_width = whole_store.shape
    floats = whole_store.astype(jnp.float32)
    scale_rows = lax.rsqrt(jnp.mean(floats * floats, axis=-1, keepdims=True) + epsilon)
    normed = (
        (floats * scale_rows * whole_gain.astype(jnp.float32))
        .astype(jnp.bfloat16)
        .reshape(stored * length, model_width)
    )
    columns_half = w_key.shape[1]
    key_rows = jnp.dot(normed, w_key, preferred_element_type=jnp.float32).astype(jnp.bfloat16)
    value_rows = jnp.dot(normed, w_value, preferred_element_type=jnp.float32).astype(jnp.bfloat16)
    encoded = jnp.concatenate([key_rows, value_rows], axis=1).reshape(
        stored, length, 2 * columns_half
    )
    spans, neighbours_per = owner.shape
    references = spans * neighbours_per
    peer_count = lax.axis_size("dp")
    own_flat = owner.reshape(references)
    row_flat = store_row.reshape(references)
    global_id = own_flat * stored + row_flat
    earlier = jnp.tril(jnp.ones((references, references), jnp.int32), -1)
    everything = lax.all_gather(encoded, "dp", axis=0, tiled=True)
    context = jnp.take(everything, global_id, axis=0)
    head_size = HEAD
    heads_here = columns_half // head_size
    context_all = context.reshape(spans, neighbours_per * length, 2, heads_here, head_size)
    key_ctx = context_all[:, :, 0]
    value_ctx = context_all[:, :, 1]
    tokens = queries.reshape(spans, -1, heads_here, head_size)
    grads_out = out_grad.reshape(spans, -1, heads_here, head_size)
    inverse_root = 1.0 / math.sqrt(head_size)
    scores = (
        jnp.einsum("cqhd,ckhd->chqk", tokens, key_ctx, preferred_element_type=jnp.float32)
        * inverse_root
    )
    probs = jax.nn.softmax(scores, axis=-1)
    probs_low = probs.astype(jnp.bfloat16)
    attended = (
        jnp.einsum("chqk,ckhd->cqhd", probs_low, value_ctx, preferred_element_type=jnp.float32)
        .astype(jnp.bfloat16)
        .reshape(queries.shape)
    )
    prob_grad = jnp.einsum(
        "cqhd,ckhd->chqk", grads_out, value_ctx, preferred_element_type=jnp.float32
    )
    row_delta = jnp.sum(probs * prob_grad, axis=-1, keepdims=True)
    score_grad = (probs * (prob_grad - row_delta)).astype(jnp.bfloat16)
    query_grad = (
        (
            jnp.einsum("chqk,ckhd->cqhd", score_grad, key_ctx, preferred_element_type=jnp.float32)
            * inverse_root
        )
        .astype(jnp.bfloat16)
        .reshape(queries.shape)
    )
    key_grad = (
        jnp.einsum("chqk,cqhd->ckhd", score_grad, tokens, preferred_element_type=jnp.float32)
        * inverse_root
    )
    value_grad = jnp.einsum(
        "chqk,cqhd->ckhd", probs_low, grads_out, preferred_element_type=jnp.float32
    )
    ref_grads = jnp.stack([key_grad, value_grad], axis=2).reshape(
        references, length, 2 * columns_half
    )
    same_id = (global_id[:, None] == global_id[None, :]).astype(jnp.float32)
    first_use = jnp.sum(same_id * earlier.astype(jnp.float32), axis=1) == 0.0
    summed = jnp.einsum("ij,jtc->itc", same_id, ref_grads, precision=lax.Precision.HIGHEST)
    sent_grads = jnp.where(first_use[:, None, None], summed, 0.0).astype(jnp.bfloat16)
    placement_table = (global_id[:, None] == jnp.arange(peer_count * stored)[None, :]).astype(
        jnp.bfloat16
    )
    dense_grads = jnp.einsum(
        "ir,itc->rtc", placement_table, sent_grads, preferred_element_type=jnp.float32
    )
    row_grad = lax.psum_scatter(
        dense_grads.astype(jnp.bfloat16), "dp", scatter_dimension=0, tiled=True
    )
    row_grad_low = row_grad.reshape(stored * length, 2 * columns_half)
    weight_grad = lax.psum_scatter(
        lax.dot_general(
            normed, row_grad_low, (((0,), (0,)), ((), ())), preferred_element_type=jnp.float32
        ).astype(jnp.bfloat16),
        "dp",
        scatter_dimension=0,
        tiled=True,
    ).astype(jnp.float32)
    return (attended, query_grad, weight_grad[:, :columns_half], weight_grad[:, columns_half:])


def solution(mesh):
    in_specs = (
        P("dp", "mp"),
        P("dp", "mp"),
        P("dp", None),
        P("dp", None),
        P("dp", None, "mp"),
        P("mp"),
        P(None, "mp"),
        P(None, "mp"),
    )
    out_specs = (P("dp", "mp"), P("dp", "mp"), P("dp", "mp"), P("dp", "mp"))
    return jax.shard_map(shards, mesh=mesh, in_specs=in_specs, out_specs=out_specs, check_vma=False)
```

profile of v0, /device:TPU:10, one launch (start us, length us, event | category | flops | bytes accessed | tf_op | source)
XLA Modules:
  0.0 445.6 jit_solution(16867970477390504006)
XLA Ops:
  7.2 0.0 all-gather.3.cloned.1.call-start
  7.2 0.7 all-gather.3.cloned.1.call-update
  7.9 0.0 all-gather.5.cloned.1.call-start
  7.9 5.3 %all_gather.10 = bf16[4096]{0:T(1024)(128)(2,1)S(1)} all-gather(bf16[1024]{0:T(1024)(128)(2,1)} %param.13), channel_id=1, replica_groups=mesh['dp'=8,'mp'=4] {'mp'}, dimensions={0}, use_global_device_ids=true | all-gather | bytes 10240 | tf_op jit(solution)/shard_map/all_gather | solution.py:17
  13.3 19.2 %all-gather.3.cloned.1.call-done = bf16[2,128,4096]{2,1,0:T(8,128)(2,1)} async-done(((bf16[2,128,1024]{2,1,0:T(8,128)(2,1)}), bf16[2,128,4096]{2,1,0:T(8,128)(2,1)}) %all-gather.3.cloned.1.call-update) | async-done | bytes 2097168 | tf_op jit(solution)/shard_map/all_gather | solution.py:16
  32.4 2.2 fusion.1
  34.7 0.0 copy-done.1
  34.7 0.0 copy-start.10
  34.7 0.6 fusion.3
  35.3 1.5 copy-done.10
  36.9 1.2 convolution_convert_fusion
  38.1 0.9 copy-done.11
  39.0 1.3 convolution_convert_fusion.1
  40.3 0.9 pad_maximum_fusion.1
  41.2 0.0 all-gather.5.cloned.1.call-update
  41.2 0.2 reduce-scatter.3.cloned.1.call-start
  41.5 0.0 copy-done.8
  41.5 0.0 copy-done.9
  41.5 0.1 copy.45
  41.6 0.1 add.72
  41.7 0.1 add.70
  41.7 0.0 copy-done.7
  41.7 0.1 reshape.113
  41.9 1.2 reshape.115
  43.1 0.1 fusion.32
  43.2 0.1 broadcast_bitcast_fusion
  43.3 71.8 %all-gather.5.cloned.1.call-done = bf16[16,128,1024]{2,1,0:T(8,128)(2,1)} async-done(((bf16[2,128,1024]{2,1,0:T(8,128)(2,1)}), bf16[16,128,1024]{2,1,0:T(8,128)(2,1)}) %all-gather.5.cloned.1.call-update) | async-done | bytes 4194320 | tf_op jit(solution)/shard_map/all_gather | solution.py:40
  115.1 4.9 %gather_fusion = bf16[16,128,1024]{2,1,0:T(8,128)(2,1)} fusion(bf16[16,128,1024]{2,1,0:T(8,128)(2,1)} %all-gather.5.cloned.1.call-done, s32[1024]{0:T(1024)S(1)} %pad_clamp_fusion), kind=kCustom, calls=%fused_computation | custom fusion | bytes 8388672 | tf_op jit(solution)/shard_map/jit(_take)/gather | solution.py:41
  120.0 7.7 %reshape.129 = bf16[8,256,2,4,128]{4,3,2,1,0:T(4,128)(2,1)} reshape(bf16[16,128,1024]{2,1,0:T(8,128)(2,1)} %gather_fusion) | data formatting | bytes 8388608 | tf_op jit(solution)/shard_map/jit(_take)/gather | solution.py:41
  127.8 2.9 copy_select_fusion
  130.7 0.0 copy-start
  130.7 0.8 fusion.17
  131.5 1.1 copy-done
  132.6 2.0 fusion.51
  134.6 0.0 copy-done.2
  134.6 8.5 %convolution_bitcast_fusion = f32[8,256,1,4,128]{4,1,3,0,2:T(8,128)} fusion(bf16[8,64,4,128]{3,2,1,0:T(4,128)(2,1)S(1)} %reshape.115, f32[8,4,64]{2,1,0:T(4,128)S(1)} %get-tuple-element.8, f32[8,4,256,64]{2,3,1,0:T(8,128)} %copy-done.2), kind=kOutput, calls=%fused_computation.16 | convolution fusion | flops 136841472 | bytes 6823936 | tf_op jit(solution)/shard_map/chqk,cqhd->ckhd/dot_general | solution.py:78
  143.1 3.3 fusion.8
  146.4 0.0 copy-done.3
  146.4 0.7 fusion.10
  147.2 0.0 copy-start.4
  147.2 1.0 copy-done.4
  148.1 0.8 multiply_bitcast_fusion
  148.9 1.4 copy-done.6
  150.3 3.8 pad_maximum_fusion
  154.1 10.3 %copy.55 = f32[8,256,2,4,128]{1,0,4,3,2:T(8,128)} copy(f32[8,256,2,4,128]{4,1,3,0,2:T(8,128)} %pad_maximum_fusion) | data formatting | bytes 16777216 | tf_op jit(solution)/shard_map/stack | solution.py:81
  164.4 8.9 %reshape.117 = f32[16,128,1024]{1,0,2:T(8,128)} reshape(f32[8,256,2,4,128]{1,0,4,3,2:T(8,128)} %copy.55) | data formatting | bytes 16777216 | tf_op jit(solution)/shard_map/reshape | solution.py:81
  173.3 8.8 %copy.57 = f32[16,128,1024]{2,0,1:T(8,128)} copy(f32[16,128,1024]{1,0,2:T(8,128)} %reshape.117) | data formatting | bytes 16777216 | tf_op jit(solution)/shard_map/reshape | solution.py:81
  182.1 6.9 %fusion.33 = bf16[16,128,1024]{2,0,1:T(8,128)(2,1)S(1)} fusion(f32[16,128,1024]{2,0,1:T(8,128)} %copy.57, s32[16]{0:T(128)S(1)} %add.72), kind=kOutput, calls=%fused_computation.56 | convolution fusion | flops 402653440 | bytes 12582976 | tf_op jit(solution)/shard_map/ij,jtc->itc/dot_general | solution.py:86
  189.0 1.3 fusion.7
  190.3 4.3 copy.58
  194.6 0.0 reduce-scatter.3.cloned.1.call-update
  194.6 0.0 reduce-scatter.5.cloned.1.call-start
  194.6 87.1 %reduce-scatter.3.cloned.1.call-done = bf16[2,128,1024]{2,1,0:T(8,128)(2,1)} async-done(((bf16[16,128,1024]{2,1,0:T(8,128)(2,1)}), bf16[2,128,1024]{2,1,0:T(8,128)(2,1)}) %reduce-scatter.3.cloned.1.call-update) | async-done | bytes 524304 | tf_op jit(solution)/shard_map/reduce_scatter | solution.py:94
  281.8 6.7 %bitcast_convert_fusion = bf16[4096,1024]{1,0:T(8,128)(2,1)} fusion(bf16[2,128,4096]{2,1,0:T(8,128)(2,1)S(1)} %fusion.3, bf16[2,128,1024]{2,1,0:T(8,128)(2,1)} %reduce-scatter.3.cloned.1.call-done), kind=kOutput, calls=%fused_computation.2 | convolution fusion | flops 2151677952 | bytes 11010048 | tf_op jit(solution)/shard_map/dot_general | solution.py:99
  288.4 0.0 reduce-scatter.5.cloned.1.call-update
  288.5 0.0 copy-start.5
  288.5 6.6 %fusion.24 = bf16[8,64,4,128]{3,1,2,0:T(8,128)(2,1)S(1)} fusion(bf16[8,256,2,4,128]{4,1,3,0,2:T(8,128)(2,1)} %copy-done, f32[8,4,64]{2,1,0:T(4,128)S(1)} %get-tuple-element.8, f32[8,4,256,64]{2,3,1,0:T(8,128)} %copy-done.2), kind=kOutput, calls=%fused_computation.37 | convolution fusion | flops 137103616 | bytes 6823936 | tf_op jit(solution)/shard_map/chqk,ckhd->cqhd/dot_general | solution.py:57
  295.1 0.4 copy.49
  295.5 0.0 copy-done.5
  295.5 2.3 fusion.23
  297.8 0.4 copy.51
  298.2 1.1 copy_bitcast_fusion
  299.4 136.9 %reduce-scatter.5.cloned.1.call-done = bf16[512,1024]{1,0:T(8,128)(2,1)} async-done(((bf16[4096,1024]{1,0:T(8,128)(2,1)}), bf16[512,1024]{1,0:T(8,128)(2,1)}) %reduce-scatter.5.cloned.1.call-update) | async-done | bytes 1048592 | tf_op jit(solution)/shard_map/reduce_scatter | solution.py:98
  436.3 2.8 fusion.50
  (15 shorter events, 0.1 us)
Async XLA Ops:
  7.2 25.2 %all-gather.3.cloned.1.call-start = ((), (), s32[]{:S(2)}) async-start(), calls=%async_computation.2 | async-start | bytes 2621440 | tf_op jit(solution)/shard_map/all_gather | solution.py:16
  7.9 107.2 %all-gather.5.cloned.1.call-start = ((), (), s32[]{:S(2)}) async-start(), calls=%async_computation.3 | async-start | bytes 4718592 | tf_op jit(solution)/shard_map/all_gather | solution.py:40
  32.4 2.2 copy-start.1
  34.7 2.2 copy-start.10
  36.9 2.2 copy-start.11
  39.0 2.4 copy-start.8
  39.0 2.4 copy-start.9
  39.0 2.7 copy-start.7
  41.2 240.5 %reduce-scatter.3.cloned.1.call-start = ((), (), s32[]{:S(2)}) async-start(), calls=%async_computation.4 | async-start | bytes 4718592 | tf_op jit(solution)/shard_map/reduce_scatter | solution.py:94
  130.7 1.9 copy-start
  132.6 2.0 copy-start.2
  143.1 3.3 copy-start.3
  147.2 1.0 copy-start.4
  148.1 2.2 copy-start.6
  194.6 241.7 %reduce-scatter.5.cloned.1.call-start = ((), (), s32[]{:S(2)}) async-start(), calls=%async_computation.5 | async-start | bytes 9437184 | tf_op jit(solution)/shard_map/reduce_scatter | solution.py:98
  288.5 7.0 %copy-start.5 = (bf16[8,4,64,256]{3,2,1,0:T(8,128)(2,1)S(1)}, bf16[8,4,64,256]{3,2,1,0:T(8,128)(2,1)}, u32[]{:S(2)}) copy-start(bf16[8,4,64,256]{3,2,1,0:T(8,128)(2,1)} %copy-done.4) | copy-start | bytes 3145732
Sparse Core Ops, SparseCore 0:
  9.6 22.7 all-gather.2
  41.4 73.6 all-gather.4
  194.7 87.0 reduce-scatter.2
  288.6 147.6 reduce-scatter.4
where the time goes:
time: 450 us; the launch traced here: 446 us
  waiting for transfers between devices  316 us (70%)
  local copies, waits for them, and re-layouts  57.2 us (13%)
  matrix products  39.7 us (9%)
  between operations  14 us (3%)
  other arithmetic  13.3 us (3%)
  blocking collectives  5.3 us (1%)
    reduce_scatter x1, waiting for transfers between devices, shards(): lax.psum_scatter(lax.dot_general(normed, row_grad_low, (((0,), (0,)), (()...  137 us
    reduce_scatter x1, waiting for transfers between devices, shards(): lax.psum_scatter(dense_grads.astype(jnp.bfloat16), 'dp', scatter_dimensio...  87.1 us
    all_gather x1, waiting for transfers between devices, shards(): everything = lax.all_gather(encoded, 'dp', axis=0, tiled=True)  71.8 us
    all_gather x1, waiting for transfers between devices, shards(): lax.all_gather(store, 'mp', axis=2, tiled=True)  19.2 us
    reshape x2, local copies, waits for them, and re-layouts, shards(): jnp.stack([key_grad, value_grad], axis=2)  17.7 us
    gather x2, local copies, waits for them, and re-layouts, shards(): context = jnp.take(everything, global_id, axis=0)  12.7 us
    another operation x1, local copies, waits for them, and re-layouts, shards(): jnp.stack([key_grad, value_grad], axis=2)  10.3 us
  transfers between devices with their start and end apart: 4, of which 4 were waited for; matrix products, arithmetic and copies ran while one was open for 3% of the time, Pallas kernels for 0%

commit v1 on v0

--- a/solution.py
+++ b/solution.py
@@ -1,17 +1,554 @@
+import functools
 import math
 
 import jax
 import jax.numpy as jnp
 from jax import lax
+from jax.experimental import pallas as pl
+from jax.experimental.pallas import tpu as pltpu
 from jax.sharding import PartitionSpec as P
 
 HEAD = 128
+TILE = 16
 
 
 epsilon = 1e-06
 
-
-def shards(queries, out_grad, owner, store_row, store, norm_gain, w_key, w_value):
+def params(mebibytes):
+    return pltpu.CompilerParams(vmem_limit_bytes=mebibytes * 1024 * 1024)
+
+
+VMEM = pl.BlockSpec(memory_space=pltpu.VMEM)
+SMEM = pl.BlockSpec(memory_space=pltpu.SMEM)
+ANY = pl.BlockSpec(memory_space=pl.ANY)
+HBM = pl.BlockSpec(memory_space=pltpu.HBM)
+
+
+def column(head):
+    return pl.ds(pl.multiple_of(head * HEAD, HEAD), HEAD)
+
+
+def pack_kernel(chain, slots, place, owner, store_row, queries, out_grad, store, gain, *refs):
+    packed, (bundle, sems, sem) = refs[:chain], refs[chain:]
+    tokens, rows = queries.shape[0], store.shape[0]
+    named, spans = owner.shape
+    copies = [pltpu.make_async_copy(store, bundle.at[pl.ds(0, rows), :], sem)] + [
+        pltpu.make_async_copy(
+            source.at[:, column(place[0] ^ r)],
+            packed[r].at[pl.ds(side * tokens, tokens), :],
+            sems.at[r, side],
+        )
+        for r in range(chain)
+        for side, source in enumerate((queries, out_grad))
+    ]
+    for copy in copies:
+        copy.start()
+    bundle[pl.ds(rows, TILE), :] = jnp.broadcast_to(gain[...].reshape(1, store.shape[1]), (TILE, store.shape[1]))
+    line = lax.broadcasted_iota(jnp.int32, (spans * named, HEAD), 0)
+    block = jnp.zeros((spans * named, HEAD), jnp.int32)
+    for i in range(spans * named):
+        spot = (i % named, i // named)
+        block = jnp.where(line == i, owner[spot] * slots + store_row[spot], block)
+    block = block.astype(jnp.float32).astype(jnp.bfloat16)
+    for r in range(chain):
+        packed[r][pl.ds(2 * tokens, spans * named), :] = block
+    for copy in copies:
+        copy.wait()
+
+
+def unpack_kernel(chain, place, *refs):
+    parts, (attended, query_grad) = refs[:chain - 1], refs[chain - 1:]
+    for r, part in enumerate(parts):
+        attended[:, column(place[0] ^ r)] = part[0]
+        query_grad[:, column(place[0] ^ r)] = part[1]
+
+
+MASKS = (0, 3, 1, 2)
+
+
+def mask(m):
+    return sum(jnp.where(m == i, x, 0) for i, x in enumerate(MASKS))
+
+
+def project_kernel(chain, features, place, w_key, w_value, *refs):
+    shards = len(refs) - chain - 4
+    states, refs = refs[:shards], refs[shards:]
+    encoded, (normed_own, normed, weights, sems) = refs[:chain], refs[chain:]
+    copies = [
+        pltpu.make_async_copy(
+            source.at[:, column(place[0] ^ r)],
+            weights.at[r, :, pl.ds(side * HEAD, HEAD)],
+            sems.at[r, side],
+        )
+        for r in range(chain)
+        for side, source in enumerate((w_key, w_value))
+    ]
+    for copy in copies:
+        copy.start()
+    m = place[2]
+    rows, width = normed_own.shape
+    gain = [x[pl.ds(rows, TILE), :].astype(jnp.float32) for x in states]
+
+    def norm_tile(i, carry):
+        part = pl.ds(pl.multiple_of(i * TILE, TILE), TILE)
+        square = jnp.zeros((TILE, 1), jnp.float32)
+        for x in states:
+            floats = x[part, :].astype(jnp.float32)
+            square += jnp.sum(floats * floats, axis=-1, keepdims=True)
+        scale = lax.rsqrt(square / features + epsilon)
+        for q, x in enumerate(states):
+            low = (x[part, :].astype(jnp.float32) * scale * gain[q]).astype(jnp.bfloat16)
+            normed[part, pl.ds(pl.multiple_of((m ^ q) * width, width), width)] = low
+        return carry
+
+    lax.fori_loop(0, rows // TILE, norm_tile, 0, unroll=2)
+    block = place[0] ^ mask(m)
+    normed_own[...] = normed[:, pl.ds(pl.multiple_of(block * width, width), width)]
+    for r in range(chain):
+        copies[2 * r].wait()
+        copies[2 * r + 1].wait()
+        encoded[r][...] = jnp.dot(
+            normed[...], weights[r], preferred_element_type=jnp.float32
+        ).astype(jnp.bfloat16)
+
+
+def dot_t(left, right):
+    return lax.dot_general(
+        left, right, (((1,), (1,)), ((), ())), preferred_element_type=jnp.float32
+    )
+
+
+def dot_0(left, right):
+    return lax.dot_general(
+        left, right, (((0,), (0,)), ((), ())), preferred_element_type=jnp.float32
+    )
+
+
+def attend_kernel(chain, spans, slots, length, place, *refs):
+    asked, refs = refs[:chain], refs[chain:]
+    near, far, refs = refs[:chain], refs[chain:2 * chain], refs[2 * chain:]
+    given, again, refs = refs[:chain], refs[chain], refs[chain + 1:]
+    kept, sent, context, grads, scores, prob_grads, lows, score_grads, lines, ids, sem = refs
+    a, y = place[0], place[1]
+    tokens = given[0].shape[1]
+    span_len = tokens // spans
+    pairs = spans // 2
+    width = 2 * span_len
+    named = 2 * spans
+    inverse_root = 1.0 / math.sqrt(HEAD)
+    for r in range(chain):
+        lines[r] = asked[r][pl.ds(2 * tokens, named), :].astype(jnp.float32).astype(jnp.int32)
+    copy = pltpu.make_async_copy(lines, ids, sem)
+    copy.start()
+    for r in range(chain):
+        first = (a ^ r) * 2 * slots
+        for s in range(slots):
+            context[first + y * slots + s] = near[r][pl.ds(s * length, length), :]
+            context[first + (1 - y) * slots + s] = far[r][pl.ds(s * length, length), :]
+    grads[...] = jnp.zeros_like(grads)
+    copy.wait()
+
+    def fetch(r, c):
+        rows = [[ids[r, 4 * c + 2 * h + n, 0] for n in range(2)] for h in range(2)]
+        key = [jnp.concatenate([context[i, :, :HEAD] for i in row], axis=0) for row in rows]
+        value = [jnp.concatenate([context[i, :, HEAD:] for i in row], axis=0) for row in rows]
+        query = asked[r][pl.ds(pl.multiple_of(c * width, width), width), :]
+        grad = asked[r][pl.ds(pl.multiple_of(tokens + c * width, width), width), :]
+        return rows, key, value, query, grad
+
+    def products(c, carry):
+        first = lax.broadcasted_iota(jnp.int32, (2 * length, width), 1) < span_len
+        for r in range(chain):
+            rows, key, value, query, grad = fetch(r, c)
+            scores[r, c] = jnp.where(first, dot_t(key[0], query), dot_t(key[1], query))
+            prob_grads[r, c] = jnp.where(first, dot_t(value[0], grad), dot_t(value[1], grad))
+        return carry
+
+    lax.fori_loop(0, pairs, products, 0)
+
+    def soften(c, carry):
+        for r in range(chain):
+            score = scores[r, c] * inverse_root
+            powers = jnp.exp(score - jnp.max(score, axis=0, keepdims=True))
+            probs = powers * (1.0 / jnp.sum(powers, axis=0, keepdims=True))
+            lows[r, c] = probs.astype(jnp.bfloat16)
+            prob_grad = prob_grads[r, c]
+            delta = jnp.sum(probs * prob_grad, axis=0, keepdims=True)
+            score_grads[r, c] = (probs * (prob_grad - delta)).astype(jnp.bfloat16)
+        return carry
+
+    lax.fori_loop(0, pairs, soften, 0)
+
+    def results(c, carry):
+        upper = lax.broadcasted_iota(jnp.int32, (width, HEAD), 0) < span_len
+        both = pl.ds(pl.multiple_of(c * width, width), width)
+        for r in range(chain):
+            rows, key, value, query, grad = fetch(r, c)
+            low, score_grad = lows[r, c], score_grads[r, c]
+            for h in range(2):
+                mine = upper if h == 0 else jnp.logical_not(upper)
+                key_part = jnp.dot(
+                    score_grad,
+                    jnp.where(mine, query, jnp.zeros_like(query)),
+                    preferred_element_type=jnp.float32,
+                )
+                value_part = jnp.dot(
+                    low,
+                    jnp.where(mine, grad, jnp.zeros_like(grad)),
+                    preferred_element_type=jnp.float32,
+                )
+                for n in range(2):
+                    part = slice(n * length, (n + 1) * length)
+                    grads[rows[h][n], :, :HEAD] += key_part[part]
+                    grads[rows[h][n], :, HEAD:] += value_part[part]
+            attended = jnp.where(upper, dot_0(low, value[0]), dot_0(low, value[1]))
+            query_grad = jnp.where(upper, dot_0(score_grad, key[0]), dot_0(score_grad, key[1]))
+            given[r][0, both, :] = attended.astype(jnp.bfloat16)
+            given[r][1, both, :] = (query_grad * inverse_root).astype(jnp.bfloat16)
+        return carry
+
+    lax.fori_loop(0, pairs, results, 0)
+    again[...] = given[chain - 1][...]
+    for member in range(chain):
+        for s in range(slots):
+            part = pl.ds(s * length, length)
+            own = member * 2 * slots + y * slots + s
+            other = member * 2 * slots + (1 - y) * slots + s
+            kept[member, part, :HEAD] = grads[own, :, :HEAD] * inverse_root
+            kept[member, part, HEAD:] = grads[own, :, HEAD:]
+            sent[member, part, :HEAD] = (grads[other, :, :HEAD] * inverse_root).astype(jnp.bfloat16)
+            sent[member, part, HEAD:] = grads[other, :, HEAD:].astype(jnp.bfloat16)
+
+
+def turn_kernel(*refs):
+    count = len(refs) // 2
+    for share, result in zip(refs[:count], refs[count:]):
+        half = result.shape[1]
+        for side in range(2):
+            result[side] = share[:, side * half:(side + 1) * half].T
+
+
+def inner(place):
+    return (place[0] == 1) | (place[0] == 2)
+
+
+def weigh_kernel(chain, wants, place, *refs):
+    shares, refs = refs[:chain], refs[chain + 1:]
+    sources, targets = refs[:-len(wants)], refs[-len(wants):]
+
+    def multiply(row_grad):
+        for want, target in zip(wants, targets):
+            half = place[1] if want else 1 - place[1]
+            total = sum(
+                jnp.dot(
+                    shares[q][half],
+                    row_grad[place[0] ^ mask(place[2] ^ q)],
+                    preferred_element_type=jnp.float32,
+                )
+                for q in range(chain)
+            )
+            target[...] = total.astype(target.dtype)
+
+    if len(sources) == 1:
+        multiply(sources[0])
+    else:
+        pl.when(inner(place))(lambda: multiply(sources[0]))
+        pl.when(jnp.logical_not(inner(place)))(lambda: multiply(sources[1]))
+
+
+def collect_kernel(chain, place, *refs):
+    count = chain - 1
+    kept, received, (key_grad, value_grad) = refs[:count], refs[count:2 * count], refs[2 * count:]
+    a = place[0]
+    turned = inner(place).astype(jnp.int32)
+    for r, head in enumerate((a, a ^ 1, a ^ (2 + turned))):
+        total = kept[r][...] + received[r][...].astype(jnp.float32)
+        key_grad[:, column(head)] = total[:, :HEAD]
+        value_grad[:, column(head)] = total[:, HEAD:]
+
+
+def finish_kernel(chain, place, kept, received, near, far, *refs):
+    targets, (total, sems) = refs[4:8], refs[8:]
+    apart = inner(place)
+
+    def write(part):
+        copies = [
+            pltpu.make_async_copy(
+                part.at[side], targets[side].at[:, column(place[0] ^ (chain - 1))], sems.at[side]
+            )
+            for side in range(2)
+        ]
+        for copy in copies:
+            copy.start()
+        total[...] = kept[...] + received[...].astype(jnp.float32)
+        copies += [
+            pltpu.make_async_copy(
+                total.at[:, pl.ds(side * HEAD, HEAD)],
+                targets[2 + side].at[:, column(place[0] ^ (3 - apart.astype(jnp.int32)))],
+                sems.at[2 + side],
+            )
+            for side in range(2)
+        ]
+        for copy in copies[2:]:
+            copy.start()
+        for copy in copies:
+            copy.wait()
+
+    pl.when(apart)(lambda: write(near))
+    pl.when(jnp.logical_not(apart))(lambda: write(far))
+
+
+def sum_kernel(kept, received, *refs):
+    total = refs[-1]
+    total[...] = (kept[...] + received[...].astype(jnp.float32)).astype(jnp.bfloat16)
+
+
+def estimate(us):
+    return pl.CostEstimate(
+        flops=int(us * 1e9), bytes_accessed=int(us * 3.5e6), transcendentals=0
+    )
+
+
+def gate(arrays, tokens):
+    n = len(arrays)
+    return pl.pallas_call(
+        lambda *refs: None,
+        out_shape=[jax.ShapeDtypeStruct(x.shape, x.dtype) for x in arrays],
+        in_specs=[ANY] * (n + len(tokens)),
+        out_specs=[ANY] * n,
+        input_output_aliases={i: i for i in range(n)},
+        compiler_params=params(1),
+        cost_estimate=estimate(0.5),
+        name="gate",
+    )(*arrays, *tokens)
+
+
+def chained(queries, out_grad, owner, store_row, store, norm_gain, w_key, w_value):
+    stored, length, width = store.shape
+    spans, neighbours_per = owner.shape
+    peers, groups = lax.axis_size("dp"), lax.axis_size("mp")
+    chain = peers // 2
+    tokens = queries.shape[0]
+    rows = stored * length
+    features = w_key.shape[0]
+    position, m = lax.axis_index("dp"), lax.axis_index("mp")
+    place = jnp.stack([position // 2, position % 2, m]).astype(jnp.int32)
+
+    def held(x):
+        return pltpu.with_memory_space_constraint(x, pltpu.HBM)
+
+    def along(x, r):
+        return lax.ppermute(x, "dp", [(i, i ^ (2 * r)) for i in range(peers)])
+
+    def hop(x, pairs):
+        return lax.ppermute(
+            x, "dp", [(2 * i + y, 2 * j + y) for i, j in pairs for y in range(2)]
+        )
+
+    def across(x):
+        return lax.ppermute(x, "dp", [(i, i ^ 1) for i in range(peers)])
+
+    def beside(x, q):
+        return lax.ppermute(x, "mp", [(i, i ^ q) for i in range(groups)])
+
+    *packed, mine = pl.pallas_call(
+        functools.partial(pack_kernel, chain, stored),
+        out_shape=[
+            jax.ShapeDtypeStruct((2 * tokens + spans * neighbours_per, HEAD), queries.dtype)
+        ] * chain
+        + [jax.ShapeDtypeStruct((rows + TILE, width), store.dtype)],
+        in_specs=[SMEM] * 3 + [HBM] * 3 + [VMEM],
+        out_specs=[VMEM] * (chain + 1),
+        scratch_shapes=[pltpu.SemaphoreType.DMA((chain, 2)), pltpu.SemaphoreType.DMA],
+        compiler_params=params(8),
+        cost_estimate=estimate(1),
+        name="pack",
+    )(
+        place,
+        held(owner.T),
+        held(store_row.T),
+        held(queries),
+        held(out_grad),
+        held(store.reshape(rows, width)),
+        held(norm_gain),
+    )
+    arrived = [beside(mine, q) for q in range(2, groups, 2)]
+    swapped = beside(mine, 1)
+    asked = [packed[0]] + [along(packed[r], r) for r in range(1, chain - 1)]
+    *arrived, late = gate(arrived + [packed[chain - 1]], asked[1:])
+    asked.append(along(late, chain - 1))
+    states = [mine, swapped]
+    for x in arrived:
+        states += [x, beside(x, 1)]
+
+    *encoded, normed_own = pl.pallas_call(
+        functools.partial(project_kernel, chain, features),
+        out_shape=[jax.ShapeDtypeStruct((rows, 2 * HEAD), jnp.bfloat16)] * chain
+        + [jax.ShapeDtypeStruct((rows, width), jnp.bfloat16)],
+        in_specs=[SMEM, HBM, HBM] + [VMEM] * groups,
+        out_specs=[VMEM] * (chain + 1),
+        scratch_shapes=[
+            pltpu.VMEM((rows, features), jnp.bfloat16),
+            pltpu.VMEM((chain, features, 2 * HEAD), jnp.bfloat16),
+            pltpu.SemaphoreType.DMA((chain, 2)),
+        ],
+        compiler_params=params(24),
+        cost_estimate=estimate(6),
+        name="project",
+    )(place, held(w_key), held(w_value), *states)
+
+    near = [encoded[0]] + [along(encoded[r], r) for r in range(1, chain)]
+    far = [across(x) for x in near]
+
+    (normed_own,) = gate([normed_own], near)
+    turned = lax.ppermute(
+        normed_own,
+        ("dp", "mp"),
+        [
+            (i * groups + j, (i ^ (2 * MASKS[j])) * groups + j)
+            for i in range(peers)
+            for j in range(groups)
+        ],
+    )
+
+    side_by_side = (chain, spans // 2, neighbours_per * length, 2 * tokens // spans)
+    *given, again, kept, sent = pl.pallas_call(
+        functools.partial(attend_kernel, chain, spans, stored, length),
+        out_shape=[jax.ShapeDtypeStruct((2, tokens, HEAD), queries.dtype)] * (chain + 1)
+        + [
+            jax.ShapeDtypeStruct((chain, rows, 2 * HEAD), jnp.float32),
+            jax.ShapeDtypeStruct((chain, rows, 2 * HEAD), jnp.bfloat16),
+        ],
+        in_specs=[SMEM] + [VMEM] * (3 * chain),
+        out_specs=[VMEM] * (chain + 3),
+        scratch_shapes=[
+            pltpu.VMEM((peers * stored, length, 2 * HEAD), jnp.bfloat16),
+            pltpu.VMEM((peers * stored, length, 2 * HEAD), jnp.float32),
+            pltpu.VMEM(side_by_side, jnp.float32),
+            pltpu.VMEM(side_by_side, jnp.float32),
+            pltpu.VMEM(side_by_side, jnp.bfloat16),
+            pltpu.VMEM(side_by_side, jnp.bfloat16),
+            pltpu.VMEM((chain, spans * neighbours_per, HEAD), jnp.int32),
+            pltpu.SMEM((chain, spans * neighbours_per, HEAD), jnp.int32),
+            pltpu.SemaphoreType.DMA,
+        ],
+        compiler_params=params(28),
+        cost_estimate=estimate(14),
+        name="attend",
+    )(place, *asked, *near, *far)
+
+    received = across(sent)
+    returned = [given[0]] + [along(given[r], r) for r in range(1, chain - 1)]
+    row_grad = pl.pallas_call(
+        sum_kernel,
+        out_shape=jax.ShapeDtypeStruct((chain, rows, 2 * HEAD), jnp.bfloat16),
+        in_specs=[VMEM, VMEM, ANY, ANY, ANY],
+        out_specs=VMEM,
+        compiler_params=params(8),
+        cost_estimate=estimate(1),
+        name="sum",
+    )(kept, received, returned[1], returned[2], turned)
+    middle, outward, ahead = ((1, 2), (2, 1)), ((2, 3), (1, 0)), ((0, 1), (3, 2))
+    beyond, inward = along(row_grad, 1), hop(row_grad, middle)
+    onward = hop(beyond, middle)
+    row_grads = [
+        [row_grad],
+        [beyond],
+        [inward, hop(inward, outward)],
+        [onward, hop(onward, outward)],
+    ]
+
+    shares = [turned, beside(turned, 1)]
+    for q in range(2, groups, 2):
+        x = beside(turned, q)
+        shares += [x, beside(x, 1)]
+    shares = pl.pallas_call(
+        turn_kernel,
+        out_shape=[jax.ShapeDtypeStruct((2, width // 2, rows), jnp.bfloat16)] * groups,
+        in_specs=[VMEM] * groups,
+        out_specs=[VMEM] * groups,
+        compiler_params=params(8),
+        cost_estimate=estimate(0.1),
+        name="turn",
+    )(*shares)
+
+    def weigh(sources, wants, token):
+        types = [jnp.float32 if want else jnp.bfloat16 for want in wants]
+        return pl.pallas_call(
+            functools.partial(weigh_kernel, chain, wants),
+            out_shape=[jax.ShapeDtypeStruct((width // 2, 2 * HEAD), t) for t in types],
+            in_specs=[SMEM] + [VMEM] * groups + [ANY] + [VMEM] * len(sources),
+            out_specs=[VMEM] * len(wants),
+            compiler_params=params(12),
+            cost_estimate=estimate(len(wants)),
+            name="weigh",
+        )(place, *shares, token, *sources)
+
+    (again,) = gate([again], [beyond])
+    passing = hop(again, ahead)
+
+    kept, received, token = [], [], place
+    for sources in row_grads[:-1]:
+        own, other = weigh(sources, (True, False), token)
+        kept.append(own)
+        received.append(across(other))
+        token = received[-2] if len(received) > 1 else own
+        if len(kept) == 2:
+            late, passing = gate([given[-1], passing], [onward, own])
+            returned.append(hop(late, middle))
+            passing = hop(passing, middle)
+    (other,) = weigh(row_grads[-1], (False,), token)
+    received.append(across(other))
+    (own,) = weigh(row_grads[-1], (True,), other)
+    kept.append(own)
+    (passing,) = gate([passing], [other])
+    returned.append(hop(passing, outward))
+    answers = [jax.ShapeDtypeStruct(queries.shape, queries.dtype)] * 2
+    attended, query_grad = pl.pallas_call(
+        functools.partial(unpack_kernel, chain),
+        out_shape=answers,
+        in_specs=[SMEM] + [VMEM] * (chain - 1),
+        out_specs=[VMEM] * 2,
+        compiler_params=params(8),
+        cost_estimate=estimate(2),
+        name="unpack",
+    )(place, *returned[:chain - 1])
+    results = [jax.ShapeDtypeStruct((width // 2, chain * HEAD), jnp.float32)] * 2
+    key_grad, value_grad = pl.pallas_call(
+        functools.partial(collect_kernel, chain),
+        out_shape=results,
+        in_specs=[SMEM] + [VMEM] * (2 * chain - 2),
+        out_specs=[VMEM] * 2,
+        compiler_params=params(12),
+        cost_estimate=estimate(2),
+        name="collect",
+    )(place, *kept[:-1], *received[:-1])
+    return pl.pallas_call(
+        functools.partial(finish_kernel, chain),
+        out_shape=answers + results,
+        in_specs=[SMEM] + [VMEM] * 4 + [ANY] * 4,
+        out_specs=[ANY] * 4,
+        scratch_shapes=[
+            pltpu.VMEM((width // 2, 2 * HEAD), jnp.float32),
+            pltpu.SemaphoreType.DMA((4,)),
+        ],
+        input_output_aliases={5 + i: i for i in range(4)},
+        compiler_params=params(4),
+        cost_estimate=estimate(1),
+        name="finish",
+    )(
+        place,
+        kept[-1],
+        received[-1],
+        *returned[chain - 1:],
+        attended,
+        query_grad,
+        key_grad,
+        value_grad,
+    )
+
+
+def gathered(queries, out_grad, owner, store_row, store, norm_gain, w_key, w_value):
     whole_store, whole_gain = (
         lax.all_gather(store, "mp", axis=2, tiled=True),
         lax.all_gather(norm_gain, "mp", axis=0, tiled=True),
@@ -118,4 +655,11 @@
         P(None, "mp"),
     )
     out_specs = (P("dp", "mp"), P("dp", "mp"), P("dp", "mp"), P("dp", "mp"))
+    def shards(*args):
+        peers, groups = lax.axis_size("dp"), lax.axis_size("mp")
+        heads_here = args[6].shape[1] // HEAD
+        if peers == 2 * heads_here == 2 * groups == 8:
+            return chained(*args)
+        return gathered(*args)
+
     return jax.shard_map(shards, mesh=mesh, in_specs=in_specs, out_specs=out_specs, check_vma=False)

time: 450 us -> 124 us (0.28)
  waiting for transfers between devices: 316 us -> 52.7 us
  local copies, waits for them, and re-layouts: 57.2 us -> 0 us
  matrix products: 39.7 us -> 0 us
  starting transfers between devices: 0.34 us -> 40 us
  Pallas kernels: 0 us -> 28.9 us
  other arithmetic: 13.3 us -> 0.08 us
  between operations: 14 us -> 0.94 us
  blocking collectives: 5.3 us -> 0 us
    reduce_scatter x2 -> x0, waiting for transfers between devices: 224 us -> none  [the longest x1 137 us: shards(): lax.psum_scatter(lax.dot_general(normed, row_grad_low, (((0,), (0,)), (()...]
    all_gather x2 -> x0, waiting for transfers between devices: 91 us -> none  [the longest x1 71.8 us: shards(): everything = lax.all_gather(encoded, 'dp', axis=0, tiled=True)]
    ppermute x0 -> x33, waiting for transfers between devices: none -> 52.7 us  [the longest x9 40.3 us: along(): return lax.ppermute(x, 'dp', [(i, i ^ 2 * r) for i in range(peers)])]
    ppermute x0 -> x33, starting transfers between devices: none -> 40 us  [the longest x8 16.1 us: hop(): lax.ppermute(x, 'dp', [(2 * i + y, 2 * j + y) for i, j in pairs for y in...]
    dot_general x11 -> x0, matrix products: 39.7 us -> none  [the longest x1 8.47 us: shards(): jnp.einsum('chqk,cqhd->ckhd', probs_low, grads_out, preferred_element_typ...]
    pallas_call x0 -> x18, Pallas kernels: none -> 28.9 us  [the longest x1 7.81 us: chained(): pl.pallas_call(functools.partial(attend_kernel, chain, spans, stored, len...]
    reshape x5 -> x0, local copies, waits for them, and re-layouts: 20.1 us -> none  [the longest x2 17.7 us: shards(): jnp.stack([key_grad, value_grad], axis=2)]
    gather x2 -> x0, local copies, waits for them, and re-layouts: 12.7 us -> none  [shards(): context = jnp.take(everything, global_id, axis=0)]
  transfers between devices with their start and end apart: 4 -> 33, of which waited for: 4 -> 13; matrix products, arithmetic and copies ran while one was open for 3% -> 0% of each run, Pallas kernels for 0% -> 21%
where the time goes in v1:
time: 124 us; the launch traced here: 123 us
  waiting for transfers between devices  52.7 us (42%)
  starting transfers between devices  40 us (32%)
  Pallas kernels  28.9 us (23%)
    ppermute x9, waiting for transfers between devices, along(): return lax.ppermute(x, 'dp', [(i, i ^ 2 * r) for i in range(peers)])  40.3 us
    ppermute x8, starting transfers between devices, hop(): lax.ppermute(x, 'dp', [(2 * i + y, 2 * j + y) for i, j in pairs for y in...  16.1 us
    ppermute x9, starting transfers between devices, across(): return lax.ppermute(x, 'dp', [(i, i ^ 1) for i in range(peers)])  11 us
    ppermute x9, starting transfers between devices, along(): return lax.ppermute(x, 'dp', [(i, i ^ 2 * r) for i in range(peers)])  9.87 us
    pallas_call x1, Pallas kernels, chained(): pl.pallas_call(functools.partial(attend_kernel, chain, spans, stored, len...  7.81 us
    pallas_call x1, Pallas kernels, chained(): pl.pallas_call(functools.partial(project_kernel, chain, features), out_sh...  7.09 us
    ppermute x8, waiting for transfers between devices, hop(): lax.ppermute(x, 'dp', [(2 * i + y, 2 * j + y) for i, j in pairs for y in...  6.67 us
    pallas_call x5, Pallas kernels, weigh(): pl.pallas_call(functools.partial(weigh_kernel, chain, wants), out_shape=[...  5.8 us
  transfers between devices with their start and end apart: 33, of which 13 were waited for; matrix products, arithmetic and copies ran while one was open for 0% of the time, Pallas kernels for 21%

profile of v1, /device:TPU:10, one launch (start us, length us, event | category | flops | bytes accessed | tf_op | source)
XLA Modules:
  0.0 122.6 jit_solution(1594796209575444555)
XLA Ops:
  0.6 0.1 pad_add_fusion.place.refs_4_
  0.7 2.3 %pack.1 = (bf16[1040,128]{1,0:T(8,128)(2,1)S(1)}, bf16[1040,128]{1,0:T(8,128)(2,1)S(1)}, bf16[1040,128]{1,0:T(8,128)(2,1)S(1)}, bf16[1040,128]{1,0:T(8,128)(2,1)S(1)}, bf16[272,1024]{1,0:T(8,128)(2,1)S(1)}) custom-call(s32[3]{0:T(128)S(1)} %pad_add_fusion.place.refs_4_, s32[2,8]{1,0:T(2,128)} %bitcast.7, s32[2,8]{1,0:T(2,128)} %bitcast.8, ...), custom_call_target="tpu_custom_call" | custom-call | flops 1000000000 | bytes 3500000 | tf_op jit(solution)/shard_map/pack/pallas_call | solution.py:354
  3.0 0.6 collective-permute-start.1
  3.6 0.0 collective-permute-start.2
  3.6 3.0 %collective-permute-start.3 = (bf16[1040,128]{1,0:T(8,128)(2,1)S(1)}, bf16[1040,128]{1,0:T(8,128)(2,1)S(1)}, u32[]{:S(2)}, u32[]{:S(2)}) collective-permute-start(bf16[1040,128]{1,0:T(8,128)(2,1)S(1)} %get-tuple-element.42), channel_id=1, source_target_pairs={{0,16},{4,20},{8,24},{12,28},{16,0},{20,4},{24,8},{28,12},{1,17},{... | collective-permute-start | bytes 798728 | tf_op jit(solution)/shard_map/ppermute | solution.py:341
  6.6 0.0 collective-permute-start
  6.6 8.2 %collective-permute-done.2.refs_2_.refs_1_ = bf16[1040,128]{1,0:T(8,128)(2,1)S(1)} collective-permute-done((bf16[1040,128]{1,0:T(8,128)(2,1)S(1)}, bf16[1040,128]{1,0:T(8,128)(2,1)S(1)}, u32[]{:S(2)}, u32[]{:S(2)}) %collective-permute-start.2) | collective-permute-done | bytes 266272 | tf_op jit(solution)/shard_map/ppermute | solution.py:341
  14.8 3.4 %collective-permute-done.3.refs_3_.refs_2_ = bf16[1040,128]{1,0:T(8,128)(2,1)S(1)} collective-permute-done((bf16[1040,128]{1,0:T(8,128)(2,1)S(1)}, bf16[1040,128]{1,0:T(8,128)(2,1)S(1)}, u32[]{:S(2)}, u32[]{:S(2)}) %collective-permute-start.3) | collective-permute-done | bytes 266272 | tf_op jit(solution)/shard_map/ppermute | solution.py:341
  18.3 0.0 collective-permute-done.1.refs_0_
  18.3 0.7 collective-permute-start.12
  19.0 0.0 collective-permute-done.refs_1_
  19.0 1.2 collective-permute-done.4.refs_3_
  20.2 7.1 %project.1 = (bf16[256,256]{1,0:T(8,128)(2,1)S(1)}, bf16[256,256]{1,0:T(8,128)(2,1)S(1)}, bf16[256,256]{1,0:T(8,128)(2,1)S(1)}, bf16[256,256]{1,0:T(8,128)(2,1)S(1)}, bf16[256,1024]{1,0:T(8,128)(2,1)S(1)}) custom-call(s32[3]{0:T(128)S(1)} %pad_add_fusion.place.refs_4_, bf16[4096,512]{1,0:T(8,128)(2,1)} %w_key.1, bf16[4096,512]{1,0:T(8,128)(2,1)} %w_value.1, ...), custom_call_target="tpu_custom_call" | custom-call | flops 6000000000 | bytes 21000000 | tf_op jit(solution)/shard_map/project/pallas_call | solution.py:384
  27.3 2.2 %collective-permute-start.5 = (bf16[256,256]{1,0:T(8,128)(2,1)S(1)}, bf16[256,256]{1,0:T(8,128)(2,1)S(1)}, u32[]{:S(2)}, u32[]{:S(2)}) collective-permute-start(bf16[256,256]{1,0:T(8,128)(2,1)S(1)} %get-tuple-element.46), channel_id=1, source_target_pairs={{0,8},{4,12},{8,0},{12,4},{16,24},{20,28},{24,16},{28,20},{1,9},{5... | collective-permute-start | bytes 393224 | tf_op jit(solution)/shard_map/ppermute | solution.py:341
  29.6 0.5 collective-permute-start.6
  30.1 1.0 collective-permute-start.7
  31.1 1.5 %collective-permute-start.13 = (bf16[256,256]{1,0:T(8,128)(2,1)S(1)}, bf16[256,256]{1,0:T(8,128)(2,1)S(1)}, u32[]{:S(2)}, u32[]{:S(2)}) collective-permute-start(bf16[256,256]{1,0:T(8,128)(2,1)S(1)} %get-tuple-element.45.refs_1_.refs_4_), channel_id=1, source_target_pairs={{0,4},{4,0},{8,12},{12,8},{16,20},{20,16},{24,28},{28,24},{1,5},{5... | collective-permute-start | bytes 393224 | tf_op jit(solution)/shard_map/ppermute | solution.py:349
  32.6 1.2 collective-permute-done.5.refs_2_.refs_5_
  33.9 1.5 %collective-permute-start.14 = (bf16[256,256]{1,0:T(8,128)(2,1)S(1)}, bf16[256,256]{1,0:T(8,128)(2,1)S(1)}, u32[]{:S(2)}, u32[]{:S(2)}) collective-permute-start(bf16[256,256]{1,0:T(8,128)(2,1)S(1)} %collective-permute-done.5.refs_2_.refs_5_), channel_id=1, source_target_pairs={{0,4},{4,0},{8,12},{12,8},{16,20},{20,16},{24,28},{28,24},{1,5},{5... | collective-permute-start | bytes 393224 | tf_op jit(solution)/shard_map/ppermute | solution.py:349
  35.4 4.5 %collective-permute-done.6.refs_3_.refs_6_ = bf16[256,256]{1,0:T(8,128)(2,1)S(1)} collective-permute-done((bf16[256,256]{1,0:T(8,128)(2,1)S(1)}, bf16[256,256]{1,0:T(8,128)(2,1)S(1)}, u32[]{:S(2)}, u32[]{:S(2)}) %collective-permute-start.6) | collective-permute-done | bytes 131104 | tf_op jit(solution)/shard_map/ppermute | solution.py:341
  39.9 1.5 %collective-permute-start.15 = (bf16[256,256]{1,0:T(8,128)(2,1)S(1)}, bf16[256,256]{1,0:T(8,128)(2,1)S(1)}, u32[]{:S(2)}, u32[]{:S(2)}) collective-permute-start(bf16[256,256]{1,0:T(8,128)(2,1)S(1)} %collective-permute-done.6.refs_3_.refs_6_), channel_id=1, source_target_pairs={{0,4},{4,0},{8,12},{12,8},{16,20},{20,16},{24,28},{28,24},{1,5},{5... | collective-permute-start | bytes 393224 | tf_op jit(solution)/shard_map/ppermute | solution.py:349
  41.4 2.7 %collective-permute-done.7.refs_4_.refs_7_ = bf16[256,256]{1,0:T(8,128)(2,1)S(1)} collective-permute-done((bf16[256,256]{1,0:T(8,128)(2,1)S(1)}, bf16[256,256]{1,0:T(8,128)(2,1)S(1)}, u32[]{:S(2)}, u32[]{:S(2)}) %collective-permute-start.7) | collective-permute-done | bytes 131104 | tf_op jit(solution)/shard_map/ppermute | solution.py:341
  44.0 1.5 %collective-permute-start.16 = (bf16[256,256]{1,0:T(8,128)(2,1)S(1)}, bf16[256,256]{1,0:T(8,128)(2,1)S(1)}, u32[]{:S(2)}, u32[]{:S(2)}) collective-permute-start(bf16[256,256]{1,0:T(8,128)(2,1)S(1)} %collective-permute-done.7.refs_4_.refs_7_), channel_id=1, source_target_pairs={{0,4},{4,0},{8,12},{12,8},{16,20},{20,16},{24,28},{28,24},{1,5},{5... | collective-permute-start | bytes 393224 | tf_op jit(solution)/shard_map/ppermute | solution.py:349
  45.6 1.9 %collective-permute-start.8 = (bf16[256,1024]{1,0:T(8,128)(2,1)S(1)}, bf16[256,1024]{1,0:T(8,128)(2,1)S(1)}, u32[]{:S(2)}, u32[]{:S(2)}) collective-permute-start(bf16[256,1024]{1,0:T(8,128)(2,1)S(1)} %gate.6), channel_id=1, source_target_pairs={{0,0},{1,25},{2,10},{3,19},{4,4},{5,29},{6,14},{7,23},{8,8},{9,17}... | collective-permute-start | bytes 1572872 | tf_op jit(solution)/shard_map/ppermute | solution.py:404
  47.5 0.0 collective-permute-done.13.refs_8_
  47.5 0.0 collective-permute-done.14.refs_9_
  47.5 1.6 %collective-permute-done.16.refs_11_ = bf16[256,256]{1,0:T(8,128)(2,1)S(1)} collective-permute-done((bf16[256,256]{1,0:T(8,128)(2,1)S(1)}, bf16[256,256]{1,0:T(8,128)(2,1)S(1)}, u32[]{:S(2)}, u32[]{:S(2)}) %collective-permute-start.16) | collective-permute-done | bytes 131104 | tf_op jit(solution)/shard_map/ppermute | solution.py:349
  49.1 7.8 %attend.1 = (bf16[2,512,128]{2,1,0:T(8,128)(2,1)S(1)}, bf16[2,512,128]{2,1,0:T(8,128)(2,1)S(1)}, bf16[2,512,128]{2,1,0:T(8,128)(2,1)S(1)}, bf16[2,512,128]{2,1,0...) custom-call(s32[3]{0:T(128)S(1)} %pad_add_fusion.place.refs_4_, ...), custom_call_target="tpu_custom_call" | custom-call | flops 14000000000 | bytes 49000000 | tf_op jit(solution)/shard_map/attend/pallas_call | solution.py:415
  56.9 1.6 %collective-permute-start.17 = (bf16[4,256,256]{2,1,0:T(8,128)(2,1)S(1)}, bf16[4,256,256]{2,1,0:T(8,128)(2,1)S(1)}, u32[]{:S(2)}, u32[]{:S(2)}) collective-permute-start(bf16[4,256,256]{2,1,0:T(8,128)(2,1)S(1)} %get-tuple-element.56), channel_id=1, source_target_pairs={{0,4},{4,0},{8,12},{12,8},{16,20},{20,16},{24,28},{28,24},{1,5},{5... | collective-permute-start | bytes 1572872 | tf_op jit(solution)/shard_map/ppermute | solution.py:349
  58.5 1.5 %collective-permute-start.18 = (bf16[2,512,128]{2,1,0:T(8,128)(2,1)S(1)}, bf16[2,512,128]{2,1,0:T(8,128)(2,1)S(1)}, u32[]{:S(2)}, u32[]{:S(2)}) collective-permute-start(bf16[2,512,128]{2,1,0:T(8,128)(2,1)S(1)} %get-tuple-element.57), channel_id=1, source_target_pairs={{0,8},{4,12},{8,0},{12,4},{16,24},{20,28},{24,16},{28,20},{1,9},{5... | collective-permute-start | bytes 786440 | tf_op jit(solution)/shard_map/ppermute | solution.py:341
  60.0 0.8 collective-permute-start.19
  60.8 1.4 %collective-permute-done.8.refs_0_.refs_2_ = bf16[256,1024]{1,0:T(8,128)(2,1)S(1)} collective-permute-done((bf16[256,1024]{1,0:T(8,128)(2,1)S(1)}, bf16[256,1024]{1,0:T(8,128)(2,1)S(1)}, u32[]{:S(2)}, u32[]{:S(2)}) %collective-permute-start.8) | collective-permute-done | bytes 524320 | tf_op jit(solution)/shard_map/ppermute | solution.py:404
  62.2 0.0 collective-permute-start.10
  62.2 7.7 %collective-permute-done.18.refs_0_.refs_1_ = bf16[2,512,128]{2,1,0:T(8,128)(2,1)S(1)} collective-permute-done((bf16[2,512,128]{2,1,0:T(8,128)(2,1)S(1)}, bf16[2,512,128]{2,1,0:T(8,128)(2,1)S(1)}, u32[]{:S(2)}, u32[]{:S(2)}) %collective-permute-start.18) | collective-permute-done | bytes 262176 | tf_op jit(solution)/shard_map/ppermute | solution.py:341
  69.9 2.9 %collective-permute-done.19.refs_1_.refs_2_ = bf16[2,512,128]{2,1,0:T(8,128)(2,1)S(1)} collective-permute-done((bf16[2,512,128]{2,1,0:T(8,128)(2,1)S(1)}, bf16[2,512,128]{2,1,0:T(8,128)(2,1)S(1)}, u32[]{:S(2)}, u32[]{:S(2)}) %collective-permute-start.19) | collective-permute-done | bytes 262176 | tf_op jit(solution)/shard_map/ppermute | solution.py:341
  72.8 0.0 collective-permute-done.17.received
  72.8 0.1 sum.1.refs_5_
  72.9 0.1 collective-permute-start.20
  73.0 2.7 %collective-permute-start.30 = (bf16[4,256,256]{2,1,0:T(8,128)(2,1)S(1)}, bf16[4,256,256]{2,1,0:T(8,128)(2,1)S(1)}, u32[]{:S(2)}, u32[]{:S(2)}) collective-permute-start(bf16[4,256,256]{2,1,0:T(8,128)(2,1)S(1)} %sum.1.refs_5_), channel_id=1, source_target_pairs={{8,16},{12,20},{16,8},{20,12},{9,17},{13,21},{17,9},{21,13},{10,18... | collective-permute-start | bytes 1572872 | tf_op jit(solution)/shard_map/ppermute | solution.py:344
  75.7 0.1 collective-permute-start.9
  75.8 0.5 collective-permute-start.11
  76.3 9.8 %collective-permute-done.20.refs_5_.refs_1_ = bf16[4,256,256]{2,1,0:T(8,128)(2,1)S(1)} collective-permute-done((bf16[4,256,256]{2,1,0:T(8,128)(2,1)S(1)}, bf16[4,256,256]{2,1,0:T(8,128)(2,1)S(1)}, u32[]{:S(2)}, u32[]{:S(2)}) %collective-permute-start.20) | collective-permute-done | bytes 524320 | tf_op jit(solution)/shard_map/ppermute | solution.py:341
  86.1 2.3 %collective-permute-start.22 = (bf16[4,256,256]{2,1,0:T(8,128)(2,1)S(1)}, bf16[4,256,256]{2,1,0:T(8,128)(2,1)S(1)}, u32[]{:S(2)}, u32[]{:S(2)}) collective-permute-start(bf16[4,256,256]{2,1,0:T(8,128)(2,1)S(1)} %collective-permute-done.20.refs_5_.refs_1_), channel_id=1, source_target_pairs={{8,16},{12,20},{16,8},{20,12},{9,17},{13,21},{17,9},{21,13},{10,18... | collective-permute-start | bytes 1572872 | tf_op jit(solution)/shard_map/ppermute | solution.py:344
  88.4 1.3 %collective-permute-start.31 = (bf16[4,256,256]{2,1,0:T(8,128)(2,1)S(1)}, bf16[4,256,256]{2,1,0:T(8,128)(2,1)S(1)}, u32[]{:S(2)}, u32[]{:S(2)}) collective-permute-start(bf16[4,256,256]{2,1,0:T(8,128)(2,1)S(1)} %collective-permute-done.30.refs_5_), channel_id=1, source_target_pairs={{16,24},{20,28},{8,0},{12,4},{17,25},{21,29},{9,1},{13,5},{18,26},... | collective-permute-start | bytes 1572872 | tf_op jit(solution)/shard_map/ppermute | solution.py:344
  89.7 1.3 %collective-permute-start.25 = (bf16[2,512,128]{2,1,0:T(8,128)(2,1)S(1)}, bf16[2,512,128]{2,1,0:T(8,128)(2,1)S(1)}, u32[]{:S(2)}, u32[]{:S(2)}) collective-permute-start(bf16[2,512,128]{2,1,0:T(8,128)(2,1)S(1)} %gate.7), channel_id=1, source_target_pairs={{0,8},{4,12},{24,16},{28,20},{1,9},{5,13},{25,17},{29,21},{2,10},{... | collective-permute-start | bytes 786440 | tf_op jit(solution)/shard_map/ppermute | solution.py:344
  91.0 0.6 turn.1
  91.7 1.3 %weigh.5 = (f32[512,256]{1,0:T(8,128)S(1)}, bf16[512,256]{1,0:T(8,128)(2,1)S(1)}) custom-call(s32[3]{0:T(128)S(1)} %pad_add_fusion.place.refs_4_, bf16[2,512,256]{2,1,0:T(8,128)(2,1)S(1)} %get-tuple-element.49.refs_0_, bf16[2,512,256]{2,1,0:T(8,128)(2,1)S(1)} %get-tuple-element.50.refs_1_, bf16[2,512,256]{2,1,0:T(8,128)(2,1)S(1)} %get-tuple-element.51.refs_2_, ...), custom_call_target="tpu_custom_call" | custom-call | flops 2000000000 | bytes 7000000 | tf_op jit(solution)/shard_map/weigh/pallas_call | solution.py:477
  92.9 0.6 collective-permute-start.29
  93.5 6.6 %collective-permute-done.22.refs_5_.refs_2_ = bf16[4,256,256]{2,1,0:T(8,128)(2,1)S(1)} collective-permute-done((bf16[4,256,256]{2,1,0:T(8,128)(2,1)S(1)}, bf16[4,256,256]{2,1,0:T(8,128)(2,1)S(1)}, u32[]{:S(2)}, u32[]{:S(2)}) %collective-permute-start.22) | collective-permute-done | bytes 524320 | tf_op jit(solution)/shard_map/ppermute | solution.py:344
  100.1 1.3 %collective-permute-start.23 = (bf16[4,256,256]{2,1,0:T(8,128)(2,1)S(1)}, bf16[4,256,256]{2,1,0:T(8,128)(2,1)S(1)}, u32[]{:S(2)}, u32[]{:S(2)}) collective-permute-start(bf16[4,256,256]{2,1,0:T(8,128)(2,1)S(1)} %collective-permute-done.22.refs_5_.refs_2_), channel_id=1, source_target_pairs={{16,24},{20,28},{8,0},{12,4},{17,25},{21,29},{9,1},{13,5},{18,26},... | collective-permute-start | bytes 1572872 | tf_op jit(solution)/shard_map/ppermute | solution.py:344
  101.5 1.3 %weigh.6 = (f32[512,256]{1,0:T(8,128)S(1)}, bf16[512,256]{1,0:T(8,128)(2,1)S(1)}) custom-call(s32[3]{0:T(128)S(1)} %pad_add_fusion.place.refs_4_, bf16[2,512,256]{2,1,0:T(8,128)(2,1)S(1)} %get-tuple-element.49.refs_0_, bf16[2,512,256]{2,1,0:T(8,128)(2,1)S(1)} %get-tuple-element.50.refs_1_, bf16[2,512,256]{2,1,0:T(8,128)(2,1)S(1)} %get-tuple-element.51.refs_2_, ...), custom_call_target="tpu_custom_call" | custom-call | flops 2000000000 | bytes 7000000 | tf_op jit(solution)/shard_map/weigh/pallas_call | solution.py:477
  102.7 0.6 collective-permute-start.21
  103.3 2.2 %collective-permute-start.27 = (bf16[2,512,128]{2,1,0:T(8,128)(2,1)S(1)}, bf16[2,512,128]{2,1,0:T(8,128)(2,1)S(1)}, u32[]{:S(2)}, u32[]{:S(2)}) collective-permute-start(bf16[2,512,128]{2,1,0:T(8,128)(2,1)S(1)} %get-tuple-element.65), channel_id=1, source_target_pairs={{8,16},{12,20},{16,8},{20,12},{9,17},{13,21},{17,9},{21,13},{10,18... | collective-permute-start | bytes 786440 | tf_op jit(solution)/shard_map/ppermute | solution.py:344
  105.5 1.3 %weigh.9 = (f32[512,256]{1,0:T(8,128)S(1)}, bf16[512,256]{1,0:T(8,128)(2,1)S(1)}) custom-call(s32[3]{0:T(128)S(1)} %pad_add_fusion.place.refs_4_, bf16[2,512,256]{2,1,0:T(8,128)(2,1)S(1)} %get-tuple-element.49.refs_0_, bf16[2,512,256]{2,1,0:T(8,128)(2,1)S(1)} %get-tuple-element.50.refs_1_, bf16[2,512,256]{2,1,0:T(8,128)(2,1)S(1)} %get-tuple-element.51.refs_2_, ...), custom_call_target="tpu_custom_call" | custom-call | flops 2000000000 | bytes 7000000 | tf_op jit(solution)/shard_map/weigh/pallas_call | solution.py:477
  106.8 1.6 %collective-permute-start.32 = (bf16[512,256]{1,0:T(8,128)(2,1)S(1)}, bf16[512,256]{1,0:T(8,128)(2,1)S(1)}, u32[]{:S(2)}, u32[]{:S(2)}) collective-permute-start(bf16[512,256]{1,0:T(8,128)(2,1)S(1)} %get-tuple-element.71), channel_id=1, source_target_pairs={{0,4},{4,0},{8,12},{12,8},{16,20},{20,16},{24,28},{28,24},{1,5},{5... | collective-permute-start | bytes 786440 | tf_op jit(solution)/shard_map/ppermute | solution.py:349
  108.4 1.6 %unpack.1 = (bf16[512,512]{1,0:T(8,128)(2,1)}, bf16[512,512]{1,0:T(8,128)(2,1)}) custom-call(s32[3]{0:T(128)S(1)} %pad_add_fusion.place.refs_4_, bf16[2,512,128]{2,1,0:T(8,128)(2,1)S(1)} %get-tuple-element.66.refs_0_, bf16[2,512,128]{2,1,0:T(8,128)(2,1)S(1)} %collective-permute-done.18.refs_0_.refs_1_, ...), custom_call_target="tpu_custom_call" | custom-call | flops 2000000000 | bytes 7000000 | tf_op jit(solution)/shard_map/unpack/pallas_call | solution.py:507
  110.0 3.6 %collective-permute-start.26 = (bf16[2,512,128]{2,1,0:T(8,128)(2,1)S(1)}, bf16[2,512,128]{2,1,0:T(8,128)(2,1)S(1)}, u32[]{:S(2)}, u32[]{:S(2)}) collective-permute-start(bf16[2,512,128]{2,1,0:T(8,128)(2,1)S(1)} %get-tuple-element.64), channel_id=1, source_target_pairs={{8,16},{12,20},{16,8},{20,12},{9,17},{13,21},{17,9},{21,13},{10,18... | collective-permute-start | bytes 786440 | tf_op jit(solution)/shard_map/ppermute | solution.py:344
  113.7 1.0 weigh.7.refs_4_.refs_1_
  114.7 0.6 collective-permute-start.24
  115.3 1.3 %collective-permute-start.28 = (bf16[2,512,128]{2,1,0:T(8,128)(2,1)S(1)}, bf16[2,512,128]{2,1,0:T(8,128)(2,1)S(1)}, u32[]{:S(2)}, u32[]{:S(2)}) collective-permute-start(bf16[2,512,128]{2,1,0:T(8,128)(2,1)S(1)} %gate.9), channel_id=1, source_target_pairs={{16,24},{20,28},{8,0},{12,4},{17,25},{21,29},{9,1},{13,5},{18,26},... | collective-permute-start | bytes 786440 | tf_op jit(solution)/shard_map/ppermute | solution.py:344
  116.6 2.1 %collect.1 = (f32[512,512]{1,0:T(8,128)}, f32[512,512]{1,0:T(8,128)}) custom-call(s32[3]{0:T(128)S(1)} %pad_add_fusion.place.refs_4_, f32[512,256]{1,0:T(8,128)S(1)} %get-tuple-element.59.refs_4_.refs_0_, f32[512,256]{1,0:T(8,128)S(1)} %get-tuple-element.63.refs_3_.refs_1_, f32[512,256]{1,0:T(8,128)S(1)} %get-tuple-element.70.refs_2_, ...), custom_call_target="tpu_custom_call" | custom-call | flops 2000000000 | bytes 7000000 | tf_op jit(solution)/shard_map/collect/pallas_call | solution.py:517
  118.7 1.0 weigh.8.kept
  119.7 1.4 %collective-permute-done.24.received = bf16[512,256]{1,0:T(8,128)(2,1)S(1)} collective-permute-done((bf16[512,256]{1,0:T(8,128)(2,1)S(1)}, bf16[512,256]{1,0:T(8,128)(2,1)S(1)}, u32[]{:S(2)}, u32[]{:S(2)}) %collective-permute-start.24) | collective-permute-done | bytes 262176 | tf_op jit(solution)/shard_map/ppermute | solution.py:349
  121.1 1.5 %finish.1 = (bf16[512,512]{1,0:T(8,128)(2,1)}, bf16[512,512]{1,0:T(8,128)(2,1)}, f32[512,512]{1,0:T(8,128)}, f32[512,512]{1,0:T(8,128)}) custom-call(s32[3]{0:T(128)S(1)} %pad_add_fusion.place.refs_4_, f32[512,256]{1,0:T(8,128)S(1)} %weigh.8.kept, ...), custom_call_target="tpu_custom_call", output_to_operand_aliasing={{0}: (5, {}), {1}: (6, {}), {2}: (7, {}), {3}: (8, {})} | custom-call | flops 1000000000 | bytes 3500000 | tf_op jit(solution)/shard_map/finish/pallas_call | solution.py:526
  (21 shorter events, 0.0 us)
Async XLA Ops:
  3.0 15.3 %collective-permute-start.1 = (bf16[272,1024]{1,0:T(8,128)(2,1)S(1)}, bf16[272,1024]{1,0:T(8,128)(2,1)S(1)}, u32[]{:S(2)}, u32[]{:S(2)}) collective-permute-start(bf16[272,1024]{1,0:T(8,128)(2,1)S(1)} %get-tuple-element.39.refs_0_), channel_id=1, source_target_pairs={{0,2},{1,3},{2,0},{3,1},{4,6},{5,7},{6,4},{7,5},{8,10},{9,11},{10,... | collective-permute-start | bytes 1671176 | tf_op jit(solution)/shard_map/ppermute | solution.py:352
  3.6 11.2 %collective-permute-start.2 = (bf16[1040,128]{1,0:T(8,128)(2,1)S(1)}, bf16[1040,128]{1,0:T(8,128)(2,1)S(1)}, u32[]{:S(2)}, u32[]{:S(2)}) collective-permute-start(bf16[1040,128]{1,0:T(8,128)(2,1)S(1)} %get-tuple-element.41), channel_id=1, source_target_pairs={{0,8},{4,12},{8,0},{12,4},{16,24},{20,28},{24,16},{28,20},{1,9},{5... | collective-permute-start | bytes 798728 | tf_op jit(solution)/shard_map/ppermute | solution.py:341
  3.6 14.7 %collective-permute-start.3 = (bf16[1040,128]{1,0:T(8,128)(2,1)S(1)}, bf16[1040,128]{1,0:T(8,128)(2,1)S(1)}, u32[]{:S(2)}, u32[]{:S(2)}) collective-permute-start(bf16[1040,128]{1,0:T(8,128)(2,1)S(1)} %get-tuple-element.42), channel_id=1, source_target_pairs={{0,16},{4,20},{8,24},{12,28},{16,0},{20,4},{24,8},{28,12},{1,17},{... | collective-permute-start | bytes 798728 | tf_op jit(solution)/shard_map/ppermute | solution.py:341
  6.6 12.4 %collective-permute-start = (bf16[272,1024]{1,0:T(8,128)(2,1)S(1)}, bf16[272,1024]{1,0:T(8,128)(2,1)S(1)}, u32[]{:S(2)}, u32[]{:S(2)}) collective-permute-start(bf16[272,1024]{1,0:T(8,128)(2,1)S(1)} %get-tuple-element.39.refs_0_), channel_id=1, source_target_pairs={{0,1},{1,0},{2,3},{3,2},{4,5},{5,4},{6,7},{7,6},{8,9},{9,8},{10,11... | collective-permute-start | bytes 1671176 | tf_op jit(solution)/shard_map/ppermute | solution.py:352
  18.3 2.0 %collective-permute-start.4 = (bf16[272,1024]{1,0:T(8,128)(2,1)S(1)}, bf16[272,1024]{1,0:T(8,128)(2,1)S(1)}, u32[]{:S(2)}, u32[]{:S(2)}) collective-permute-start(bf16[272,1024]{1,0:T(8,128)(2,1)S(1)} %get-tuple-element.43.refs_2_), channel_id=1, source_target_pairs={{0,1},{1,0},{2,3},{3,2},{4,5},{5,4},{6,7},{7,6},{8,9},{9,8},{10,11... | collective-permute-start | bytes 1671176 | tf_op jit(solution)/shard_map/ppermute | solution.py:352
  18.3 27.3 %collective-permute-start.12 = (bf16[1040,128]{1,0:T(8,128)(2,1)S(1)}, bf16[1040,128]{1,0:T(8,128)(2,1)S(1)}, u32[]{:S(2)}, u32[]{:S(2)}) collective-permute-start(bf16[1040,128]{1,0:T(8,128)(2,1)S(1)} %get-tuple-element.54), channel_id=1, source_target_pairs={{0,24},{4,28},{8,16},{12,20},{16,8},{20,12},{24,0},{28,4},{1,25},{... | collective-permute-start | bytes 798728 | tf_op jit(solution)/shard_map/ppermute | solution.py:341
  27.3 6.5 %collective-permute-start.5 = (bf16[256,256]{1,0:T(8,128)(2,1)S(1)}, bf16[256,256]{1,0:T(8,128)(2,1)S(1)}, u32[]{:S(2)}, u32[]{:S(2)}) collective-permute-start(bf16[256,256]{1,0:T(8,128)(2,1)S(1)} %get-tuple-element.46), channel_id=1, source_target_pairs={{0,8},{4,12},{8,0},{12,4},{16,24},{20,28},{24,16},{28,20},{1,9},{5... | collective-permute-start | bytes 393224 | tf_op jit(solution)/shard_map/ppermute | solution.py:341
  29.6 10.3 %collective-permute-start.6 = (bf16[256,256]{1,0:T(8,128)(2,1)S(1)}, bf16[256,256]{1,0:T(8,128)(2,1)S(1)}, u32[]{:S(2)}, u32[]{:S(2)}) collective-permute-start(bf16[256,256]{1,0:T(8,128)(2,1)S(1)} %get-tuple-element.47), channel_id=1, source_target_pairs={{0,16},{4,20},{8,24},{12,28},{16,0},{20,4},{24,8},{28,12},{1,17},{... | collective-permute-start | bytes 393224 | tf_op jit(solution)/shard_map/ppermute | solution.py:341
  30.1 14.0 %collective-permute-start.7 = (bf16[256,256]{1,0:T(8,128)(2,1)S(1)}, bf16[256,256]{1,0:T(8,128)(2,1)S(1)}, u32[]{:S(2)}, u32[]{:S(2)}) collective-permute-start(bf16[256,256]{1,0:T(8,128)(2,1)S(1)} %get-tuple-element.48), channel_id=1, source_target_pairs={{0,24},{4,28},{8,16},{12,20},{16,8},{20,12},{24,0},{28,4},{1,25},{... | collective-permute-start | bytes 393224 | tf_op jit(solution)/shard_map/ppermute | solution.py:341
  31.1 16.4 %collective-permute-start.13 = (bf16[256,256]{1,0:T(8,128)(2,1)S(1)}, bf16[256,256]{1,0:T(8,128)(2,1)S(1)}, u32[]{:S(2)}, u32[]{:S(2)}) collective-permute-start(bf16[256,256]{1,0:T(8,128)(2,1)S(1)} %get-tuple-element.45.refs_1_.refs_4_), channel_id=1, source_target_pairs={{0,4},{4,0},{8,12},{12,8},{16,20},{20,16},{24,28},{28,24},{1,5},{5... | collective-permute-start | bytes 393224 | tf_op jit(solution)/shard_map/ppermute | solution.py:349
  33.9 13.6 %collective-permute-start.14 = (bf16[256,256]{1,0:T(8,128)(2,1)S(1)}, bf16[256,256]{1,0:T(8,128)(2,1)S(1)}, u32[]{:S(2)}, u32[]{:S(2)}) collective-permute-start(bf16[256,256]{1,0:T(8,128)(2,1)S(1)} %collective-permute-done.5.refs_2_.refs_5_), channel_id=1, source_target_pairs={{0,4},{4,0},{8,12},{12,8},{16,20},{20,16},{24,28},{28,24},{1,5},{5... | collective-permute-start | bytes 393224 | tf_op jit(solution)/shard_map/ppermute | solution.py:349
  39.9 7.6 %collective-permute-start.15 = (bf16[256,256]{1,0:T(8,128)(2,1)S(1)}, bf16[256,256]{1,0:T(8,128)(2,1)S(1)}, u32[]{:S(2)}, u32[]{:S(2)}) collective-permute-start(bf16[256,256]{1,0:T(8,128)(2,1)S(1)} %collective-permute-done.6.refs_3_.refs_6_), channel_id=1, source_target_pairs={{0,4},{4,0},{8,12},{12,8},{16,20},{20,16},{24,28},{28,24},{1,5},{5... | collective-permute-start | bytes 393224 | tf_op jit(solution)/shard_map/ppermute | solution.py:349
  44.0 5.1 %collective-permute-start.16 = (bf16[256,256]{1,0:T(8,128)(2,1)S(1)}, bf16[256,256]{1,0:T(8,128)(2,1)S(1)}, u32[]{:S(2)}, u32[]{:S(2)}) collective-permute-start(bf16[256,256]{1,0:T(8,128)(2,1)S(1)} %collective-permute-done.7.refs_4_.refs_7_), channel_id=1, source_target_pairs={{0,4},{4,0},{8,12},{12,8},{16,20},{20,16},{24,28},{28,24},{1,5},{5... | collective-permute-start | bytes 393224 | tf_op jit(solution)/shard_map/ppermute | solution.py:349
  45.6 16.6 %collective-permute-start.8 = (bf16[256,1024]{1,0:T(8,128)(2,1)S(1)}, bf16[256,1024]{1,0:T(8,128)(2,1)S(1)}, u32[]{:S(2)}, u32[]{:S(2)}) collective-permute-start(bf16[256,1024]{1,0:T(8,128)(2,1)S(1)} %gate.6), channel_id=1, source_target_pairs={{0,0},{1,25},{2,10},{3,19},{4,4},{5,29},{6,14},{7,23},{8,8},{9,17}... | collective-permute-start | bytes 1572872 | tf_op jit(solution)/shard_map/ppermute | solution.py:404
  56.9 15.9 %collective-permute-start.17 = (bf16[4,256,256]{2,1,0:T(8,128)(2,1)S(1)}, bf16[4,256,256]{2,1,0:T(8,128)(2,1)S(1)}, u32[]{:S(2)}, u32[]{:S(2)}) collective-permute-start(bf16[4,256,256]{2,1,0:T(8,128)(2,1)S(1)} %get-tuple-element.56), channel_id=1, source_target_pairs={{0,4},{4,0},{8,12},{12,8},{16,20},{20,16},{24,28},{28,24},{1,5},{5... | collective-permute-start | bytes 1572872 | tf_op jit(solution)/shard_map/ppermute | solution.py:349
  58.5 11.4 %collective-permute-start.18 = (bf16[2,512,128]{2,1,0:T(8,128)(2,1)S(1)}, bf16[2,512,128]{2,1,0:T(8,128)(2,1)S(1)}, u32[]{:S(2)}, u32[]{:S(2)}) collective-permute-start(bf16[2,512,128]{2,1,0:T(8,128)(2,1)S(1)} %get-tuple-element.57), channel_id=1, source_target_pairs={{0,8},{4,12},{8,0},{12,4},{16,24},{20,28},{24,16},{28,20},{1,9},{5... | collective-permute-start | bytes 786440 | tf_op jit(solution)/shard_map/ppermute | solution.py:341
  60.0 12.8 %collective-permute-start.19 = (bf16[2,512,128]{2,1,0:T(8,128)(2,1)S(1)}, bf16[2,512,128]{2,1,0:T(8,128)(2,1)S(1)}, u32[]{:S(2)}, u32[]{:S(2)}) collective-permute-start(bf16[2,512,128]{2,1,0:T(8,128)(2,1)S(1)} %get-tuple-element.58), channel_id=1, source_target_pairs={{0,16},{4,20},{8,24},{12,28},{16,0},{20,4},{24,8},{28,12},{1,17},{... | collective-permute-start | bytes 786440 | tf_op jit(solution)/shard_map/ppermute | solution.py:341
  62.2 13.6 %collective-permute-start.10 = (bf16[256,1024]{1,0:T(8,128)(2,1)S(1)}, bf16[256,1024]{1,0:T(8,128)(2,1)S(1)}, u32[]{:S(2)}, u32[]{:S(2)}) collective-permute-start(bf16[256,1024]{1,0:T(8,128)(2,1)S(1)} %collective-permute-done.8.refs_0_.refs_2_), channel_id=1, source_target_pairs={{0,2},{1,3},{2,0},{3,1},{4,6},{5,7},{6,4},{7,5},{8,10},{9,11},{10,... | collective-permute-start | bytes 1572872 | tf_op jit(solution)/shard_map/ppermute | solution.py:352
  72.9 13.2 %collective-permute-start.20 = (bf16[4,256,256]{2,1,0:T(8,128)(2,1)S(1)}, bf16[4,256,256]{2,1,0:T(8,128)(2,1)S(1)}, u32[]{:S(2)}, u32[]{:S(2)}) collective-permute-start(bf16[4,256,256]{2,1,0:T(8,128)(2,1)S(1)} %sum.1.refs_5_), channel_id=1, source_target_pairs={{0,8},{4,12},{8,0},{12,4},{16,24},{20,28},{24,16},{28,20},{1,9},{5... | collective-permute-start | bytes 1572872 | tf_op jit(solution)/shard_map/ppermute | solution.py:341
  73.0 15.4 %collective-permute-start.30 = (bf16[4,256,256]{2,1,0:T(8,128)(2,1)S(1)}, bf16[4,256,256]{2,1,0:T(8,128)(2,1)S(1)}, u32[]{:S(2)}, u32[]{:S(2)}) collective-permute-start(bf16[4,256,256]{2,1,0:T(8,128)(2,1)S(1)} %sum.1.refs_5_), channel_id=1, source_target_pairs={{8,16},{12,20},{16,8},{20,12},{9,17},{13,21},{17,9},{21,13},{10,18... | collective-permute-start | bytes 1572872 | tf_op jit(solution)/shard_map/ppermute | solution.py:344
  75.7 15.3 %collective-permute-start.9 = (bf16[256,1024]{1,0:T(8,128)(2,1)S(1)}, bf16[256,1024]{1,0:T(8,128)(2,1)S(1)}, u32[]{:S(2)}, u32[]{:S(2)}) collective-permute-start(bf16[256,1024]{1,0:T(8,128)(2,1)S(1)} %collective-permute-done.8.refs_0_.refs_2_), channel_id=1, source_target_pairs={{0,1},{1,0},{2,3},{3,2},{4,5},{5,4},{6,7},{7,6},{8,9},{9,8},{10,11... | collective-permute-start | bytes 1572872 | tf_op jit(solution)/shard_map/ppermute | solution.py:352
  75.8 15.2 %collective-permute-start.11 = (bf16[256,1024]{1,0:T(8,128)(2,1)S(1)}, bf16[256,1024]{1,0:T(8,128)(2,1)S(1)}, u32[]{:S(2)}, u32[]{:S(2)}) collective-permute-start(bf16[256,1024]{1,0:T(8,128)(2,1)S(1)} %collective-permute-done.10.refs_2_), channel_id=1, source_target_pairs={{0,1},{1,0},{2,3},{3,2},{4,5},{5,4},{6,7},{7,6},{8,9},{9,8},{10,11... | collective-permute-start | bytes 1572872 | tf_op jit(solution)/shard_map/ppermute | solution.py:352
  86.1 14.1 %collective-permute-start.22 = (bf16[4,256,256]{2,1,0:T(8,128)(2,1)S(1)}, bf16[4,256,256]{2,1,0:T(8,128)(2,1)S(1)}, u32[]{:S(2)}, u32[]{:S(2)}) collective-permute-start(bf16[4,256,256]{2,1,0:T(8,128)(2,1)S(1)} %collective-permute-done.20.refs_5_.refs_1_), channel_id=1, source_target_pairs={{8,16},{12,20},{16,8},{20,12},{9,17},{13,21},{17,9},{21,13},{10,18... | collective-permute-start | bytes 1572872 | tf_op jit(solution)/shard_map/ppermute | solution.py:344
  88.4 17.1 %collective-permute-start.31 = (bf16[4,256,256]{2,1,0:T(8,128)(2,1)S(1)}, bf16[4,256,256]{2,1,0:T(8,128)(2,1)S(1)}, u32[]{:S(2)}, u32[]{:S(2)}) collective-permute-start(bf16[4,256,256]{2,1,0:T(8,128)(2,1)S(1)} %collective-permute-done.30.refs_5_), channel_id=1, source_target_pairs={{16,24},{20,28},{8,0},{12,4},{17,25},{21,29},{9,1},{13,5},{18,26},... | collective-permute-start | bytes 1572872 | tf_op jit(solution)/shard_map/ppermute | solution.py:344
  89.7 13.6 %collective-permute-start.25 = (bf16[2,512,128]{2,1,0:T(8,128)(2,1)S(1)}, bf16[2,512,128]{2,1,0:T(8,128)(2,1)S(1)}, u32[]{:S(2)}, u32[]{:S(2)}) collective-permute-start(bf16[2,512,128]{2,1,0:T(8,128)(2,1)S(1)} %gate.7), channel_id=1, source_target_pairs={{0,8},{4,12},{24,16},{28,20},{1,9},{5,13},{25,17},{29,21},{2,10},{... | collective-permute-start | bytes 786440 | tf_op jit(solution)/shard_map/ppermute | solution.py:344
  92.9 12.6 %collective-permute-start.29 = (bf16[512,256]{1,0:T(8,128)(2,1)S(1)}, bf16[512,256]{1,0:T(8,128)(2,1)S(1)}, u32[]{:S(2)}, u32[]{:S(2)}) collective-permute-start(bf16[512,256]{1,0:T(8,128)(2,1)S(1)} %get-tuple-element.69), channel_id=1, source_target_pairs={{0,4},{4,0},{8,12},{12,8},{16,20},{20,16},{24,28},{28,24},{1,5},{5... | collective-permute-start | bytes 786440 | tf_op jit(solution)/shard_map/ppermute | solution.py:349
  100.1 13.5 %collective-permute-start.23 = (bf16[4,256,256]{2,1,0:T(8,128)(2,1)S(1)}, bf16[4,256,256]{2,1,0:T(8,128)(2,1)S(1)}, u32[]{:S(2)}, u32[]{:S(2)}) collective-permute-start(bf16[4,256,256]{2,1,0:T(8,128)(2,1)S(1)} %collective-permute-done.22.refs_5_.refs_2_), channel_id=1, source_target_pairs={{16,24},{20,28},{8,0},{12,4},{17,25},{21,29},{9,1},{13,5},{18,26},... | collective-permute-start | bytes 1572872 | tf_op jit(solution)/shard_map/ppermute | solution.py:344
  102.7 10.9 %collective-permute-start.21 = (bf16[512,256]{1,0:T(8,128)(2,1)S(1)}, bf16[512,256]{1,0:T(8,128)(2,1)S(1)}, u32[]{:S(2)}, u32[]{:S(2)}) collective-permute-start(bf16[512,256]{1,0:T(8,128)(2,1)S(1)} %get-tuple-element.60), channel_id=1, source_target_pairs={{0,4},{4,0},{8,12},{12,8},{16,20},{20,16},{24,28},{28,24},{1,5},{5... | collective-permute-start | bytes 786440 | tf_op jit(solution)/shard_map/ppermute | solution.py:349
  103.3 12.0 %collective-permute-start.27 = (bf16[2,512,128]{2,1,0:T(8,128)(2,1)S(1)}, bf16[2,512,128]{2,1,0:T(8,128)(2,1)S(1)}, u32[]{:S(2)}, u32[]{:S(2)}) collective-permute-start(bf16[2,512,128]{2,1,0:T(8,128)(2,1)S(1)} %get-tuple-element.65), channel_id=1, source_target_pairs={{8,16},{12,20},{16,8},{20,12},{9,17},{13,21},{17,9},{21,13},{10,18... | collective-permute-start | bytes 786440 | tf_op jit(solution)/shard_map/ppermute | solution.py:344
  106.8 9.8 %collective-permute-start.32 = (bf16[512,256]{1,0:T(8,128)(2,1)S(1)}, bf16[512,256]{1,0:T(8,128)(2,1)S(1)}, u32[]{:S(2)}, u32[]{:S(2)}) collective-permute-start(bf16[512,256]{1,0:T(8,128)(2,1)S(1)} %get-tuple-element.71), channel_id=1, source_target_pairs={{0,4},{4,0},{8,12},{12,8},{16,20},{20,16},{24,28},{28,24},{1,5},{5... | collective-permute-start | bytes 786440 | tf_op jit(solution)/shard_map/ppermute | solution.py:349
  110.0 9.7 %collective-permute-start.26 = (bf16[2,512,128]{2,1,0:T(8,128)(2,1)S(1)}, bf16[2,512,128]{2,1,0:T(8,128)(2,1)S(1)}, u32[]{:S(2)}, u32[]{:S(2)}) collective-permute-start(bf16[2,512,128]{2,1,0:T(8,128)(2,1)S(1)} %get-tuple-element.64), channel_id=1, source_target_pairs={{8,16},{12,20},{16,8},{20,12},{9,17},{13,21},{17,9},{21,13},{10,18... | collective-permute-start | bytes 786440 | tf_op jit(solution)/shard_map/ppermute | solution.py:344
  114.7 6.4 %collective-permute-start.24 = (bf16[512,256]{1,0:T(8,128)(2,1)S(1)}, bf16[512,256]{1,0:T(8,128)(2,1)S(1)}, u32[]{:S(2)}, u32[]{:S(2)}) collective-permute-start(bf16[512,256]{1,0:T(8,128)(2,1)S(1)} %weigh.7.refs_4_.refs_1_), channel_id=1, source_target_pairs={{0,4},{4,0},{8,12},{12,8},{16,20},{20,16},{24,28},{28,24},{1,5},{5... | collective-permute-start | bytes 786440 | tf_op jit(solution)/shard_map/ppermute | solution.py:349
  115.3 5.9 %collective-permute-start.28 = (bf16[2,512,128]{2,1,0:T(8,128)(2,1)S(1)}, bf16[2,512,128]{2,1,0:T(8,128)(2,1)S(1)}, u32[]{:S(2)}, u32[]{:S(2)}) collective-permute-start(bf16[2,512,128]{2,1,0:T(8,128)(2,1)S(1)} %gate.9), channel_id=1, source_target_pairs={{16,24},{20,28},{8,0},{12,4},{17,25},{21,29},{9,1},{13,5},{18,26},... | collective-permute-start | bytes 786440 | tf_op jit(solution)/shard_map/ppermute | solution.py:344

commit v2 on v1

--- a/solution.py
+++ b/solution.py
@@ -208,7 +208,8 @@
         return carry
 
     lax.fori_loop(0, pairs, results, 0)
-    again[...] = given[chain - 1][...]
+    again[:, pl.ds(0, tokens), :] = given[chain - 1][...]
+    again[:, pl.ds(tokens, TILE), :] = jnp.zeros((2, TILE, HEAD), jnp.bfloat16)
     for member in range(chain):
         for s in range(slots):
             part = pl.ds(s * length, length)
@@ -274,7 +275,9 @@
     def write(part):
         copies = [
             pltpu.make_async_copy(
-                part.at[side], targets[side].at[:, column(place[0] ^ (chain - 1))], sems.at[side]
+                part.at[side, pl.ds(0, targets[side].shape[0]), :],
+                targets[side].at[:, column(place[0] ^ (chain - 1))],
+                sems.at[side],
             )
             for side in range(2)
         ]
@@ -414,7 +417,8 @@
     side_by_side = (chain, spans // 2, neighbours_per * length, 2 * tokens // spans)
     *given, again, kept, sent = pl.pallas_call(
         functools.partial(attend_kernel, chain, spans, stored, length),
-        out_shape=[jax.ShapeDtypeStruct((2, tokens, HEAD), queries.dtype)] * (chain + 1)
+        out_shape=[jax.ShapeDtypeStruct((2, tokens, HEAD), queries.dtype)] * chain
+        + [jax.ShapeDtypeStruct((2, tokens + TILE, HEAD), queries.dtype)]
         + [
             jax.ShapeDtypeStruct((chain, rows, 2 * HEAD), jnp.float32),
             jax.ShapeDtypeStruct((chain, rows, 2 * HEAD), jnp.bfloat16),
@@ -494,15 +498,16 @@
         received.append(across(other))
         token = received[-2] if len(received) > 1 else own
         if len(kept) == 2:
-            late, passing = gate([given[-1], passing], [onward, own])
-            returned.append(hop(late, middle))
+            (passing,) = gate([passing], [onward, own])
             passing = hop(passing, middle)
-    (other,) = weigh(row_grads[-1], (False,), token)
+    (passing,) = gate([passing], [received[1]])
+    (other,) = weigh(row_grads[-1], (False,), passing)
+    far = hop(passing, outward)
+    (late,) = gate([given[-1]], [other])
+    near = hop(late, middle)
     received.append(across(other))
     (own,) = weigh(row_grads[-1], (True,), other)
     kept.append(own)
-    (passing,) = gate([passing], [other])
-    returned.append(hop(passing, outward))
     answers = [jax.ShapeDtypeStruct(queries.shape, queries.dtype)] * 2
     attended, query_grad = pl.pallas_call(
         functools.partial(unpack_kernel, chain),
@@ -540,7 +545,8 @@
         place,
         kept[-1],
         received[-1],
-        *returned[chain - 1:],
+        near,
+        far,
         attended,
         query_grad,
         key_grad,

time: 124 us -> 126 us (1.016)
  waiting for transfers between devices: 52.7 us -> 56.1 us
    ppermute x8, waiting for transfers between devices: 6.67 us -> 9.59 us  [hop(): lax.ppermute(x, 'dp', [(2 * i + y, 2 * j + y) for i, j in pairs for y in...]
    ppermute x8, starting transfers between devices: 16.1 us -> 14.6 us  [hop(): lax.ppermute(x, 'dp', [(2 * i + y, 2 * j + y) for i, j in pairs for y in...]
  transfers between devices with their start and end apart: 33 -> 33, of which waited for: 13 -> 14; matrix products, arithmetic and copies ran while one was open for 0% -> 0% of each run, Pallas kernels for 21% -> 20%
where the time goes in v2:
time: 126 us; the launch traced here: 125 us
  waiting for transfers between devices  56.1 us (45%)
  starting transfers between devices  39.2 us (31%)
  Pallas kernels  28.9 us (23%)
    ppermute x9, waiting for transfers between devices, along(): return lax.ppermute(x, 'dp', [(i, i ^ 2 * r) for i in range(peers)])  40.3 us
    ppermute x8, starting transfers between devices, hop(): lax.ppermute(x, 'dp', [(2 * i + y, 2 * j + y) for i, j in pairs for y in...  14.6 us
    ppermute x9, starting transfers between devices, across(): return lax.ppermute(x, 'dp', [(i, i ^ 1) for i in range(peers)])  11.7 us
    ppermute x9, starting transfers between devices, along(): return lax.ppermute(x, 'dp', [(i, i ^ 2 * r) for i in range(peers)])  9.87 us
    ppermute x8, waiting for transfers between devices, hop(): lax.ppermute(x, 'dp', [(2 * i + y, 2 * j + y) for i, j in pairs for y in...  9.59 us
    pallas_call x1, Pallas kernels, chained(): pl.pallas_call(functools.partial(attend_kernel, chain, spans, stored, len...  7.81 us
    pallas_call x1, Pallas kernels, chained(): pl.pallas_call(functools.partial(project_kernel, chain, features), out_sh...  7.09 us
    pallas_call x5, Pallas kernels, weigh(): pl.pallas_call(functools.partial(weigh_kernel, chain, wants), out_shape=[...  5.8 us
  transfers between devices with their start and end apart: 33, of which 14 were waited for; matrix products, arithmetic and copies ran while one was open for 0% of the time, Pallas kernels for 20%

profile of v2, /device:TPU:10, one launch (start us, length us, event | category | flops | bytes accessed | tf_op | source)
XLA Modules:
  0.0 125.3 jit_solution(13263807428218088184)
XLA Ops:
  0.6 0.1 pad_add_fusion.place.refs_4_
  0.7 2.3 %pack.1 = (bf16[1040,128]{1,0:T(8,128)(2,1)S(1)}, bf16[1040,128]{1,0:T(8,128)(2,1)S(1)}, bf16[1040,128]{1,0:T(8,128)(2,1)S(1)}, bf16[1040,128]{1,0:T(8,128)(2,1)S(1)}, bf16[272,1024]{1,0:T(8,128)(2,1)S(1)}) custom-call(s32[3]{0:T(128)S(1)} %pad_add_fusion.place.refs_4_, s32[2,8]{1,0:T(2,128)} %bitcast.7, s32[2,8]{1,0:T(2,128)} %bitcast.8, ...), custom_call_target="tpu_custom_call" | custom-call | flops 1000000000 | bytes 3500000 | tf_op jit(solution)/shard_map/pack/pallas_call | solution.py:357
  3.0 0.6 collective-permute-start.1
  3.6 3.0 %collective-permute-start.3 = (bf16[1040,128]{1,0:T(8,128)(2,1)S(1)}, bf16[1040,128]{1,0:T(8,128)(2,1)S(1)}, u32[]{:S(2)}, u32[]{:S(2)}) collective-permute-start(bf16[1040,128]{1,0:T(8,128)(2,1)S(1)} %get-tuple-element.40), channel_id=1, source_target_pairs={{0,16},{4,20},{8,24},{12,28},{16,0},{20,4},{24,8},{28,12},{1,17},{... | collective-permute-start | bytes 798728 | tf_op jit(solution)/shard_map/ppermute | solution.py:344
  6.6 0.0 collective-permute-start
  6.6 8.2 %collective-permute-done.2.refs_2_.refs_1_ = bf16[1040,128]{1,0:T(8,128)(2,1)S(1)} collective-permute-done((bf16[1040,128]{1,0:T(8,128)(2,1)S(1)}, bf16[1040,128]{1,0:T(8,128)(2,1)S(1)}, u32[]{:S(2)}, u32[]{:S(2)}) %collective-permute-start.2) | collective-permute-done | bytes 266272 | tf_op jit(solution)/shard_map/ppermute | solution.py:344
  14.8 3.4 %collective-permute-done.3.refs_3_.refs_2_ = bf16[1040,128]{1,0:T(8,128)(2,1)S(1)} collective-permute-done((bf16[1040,128]{1,0:T(8,128)(2,1)S(1)}, bf16[1040,128]{1,0:T(8,128)(2,1)S(1)}, u32[]{:S(2)}, u32[]{:S(2)}) %collective-permute-start.3) | collective-permute-done | bytes 266272 | tf_op jit(solution)/shard_map/ppermute | solution.py:344
  18.3 0.0 collective-permute-done.1.refs_0_
  18.3 0.7 collective-permute-start.12
  19.0 0.0 collective-permute-done.refs_1_
  19.0 1.2 collective-permute-done.4.refs_3_
  20.2 7.1 %project.1 = (bf16[256,256]{1,0:T(8,128)(2,1)S(1)}, bf16[256,256]{1,0:T(8,128)(2,1)S(1)}, bf16[256,256]{1,0:T(8,128)(2,1)S(1)}, bf16[256,256]{1,0:T(8,128)(2,1)S(1)}, bf16[256,1024]{1,0:T(8,128)(2,1)S(1)}) custom-call(s32[3]{0:T(128)S(1)} %pad_add_fusion.place.refs_4_, bf16[4096,512]{1,0:T(8,128)(2,1)} %w_key.1, bf16[4096,512]{1,0:T(8,128)(2,1)} %w_value.1, ...), custom_call_target="tpu_custom_call" | custom-call | flops 6000000000 | bytes 21000000 | tf_op jit(solution)/shard_map/project/pallas_call | solution.py:387
  27.3 2.2 %collective-permute-start.5 = (bf16[256,256]{1,0:T(8,128)(2,1)S(1)}, bf16[256,256]{1,0:T(8,128)(2,1)S(1)}, u32[]{:S(2)}, u32[]{:S(2)}) collective-permute-start(bf16[256,256]{1,0:T(8,128)(2,1)S(1)} %get-tuple-element.44), channel_id=1, source_target_pairs={{0,8},{4,12},{8,0},{12,4},{16,24},{20,28},{24,16},{28,20},{1,9},{5... | collective-permute-start | bytes 393224 | tf_op jit(solution)/shard_map/ppermute | solution.py:344
  29.6 0.5 collective-permute-start.6
  30.1 1.0 collective-permute-start.7
  31.1 1.5 %collective-permute-start.13 = (bf16[256,256]{1,0:T(8,128)(2,1)S(1)}, bf16[256,256]{1,0:T(8,128)(2,1)S(1)}, u32[]{:S(2)}, u32[]{:S(2)}) collective-permute-start(bf16[256,256]{1,0:T(8,128)(2,1)S(1)} %get-tuple-element.43.refs_1_.refs_4_), channel_id=1, source_target_pairs={{0,4},{4,0},{8,12},{12,8},{16,20},{20,16},{24,28},{28,24},{1,5},{5... | collective-permute-start | bytes 393224 | tf_op jit(solution)/shard_map/ppermute | solution.py:352
  32.6 1.2 collective-permute-done.5.refs_2_.refs_5_
  33.9 1.5 %collective-permute-start.14 = (bf16[256,256]{1,0:T(8,128)(2,1)S(1)}, bf16[256,256]{1,0:T(8,128)(2,1)S(1)}, u32[]{:S(2)}, u32[]{:S(2)}) collective-permute-start(bf16[256,256]{1,0:T(8,128)(2,1)S(1)} %collective-permute-done.5.refs_2_.refs_5_), channel_id=1, source_target_pairs={{0,4},{4,0},{8,12},{12,8},{16,20},{20,16},{24,28},{28,24},{1,5},{5... | collective-permute-start | bytes 393224 | tf_op jit(solution)/shard_map/ppermute | solution.py:352
  35.4 4.5 %collective-permute-done.6.refs_3_.refs_6_ = bf16[256,256]{1,0:T(8,128)(2,1)S(1)} collective-permute-done((bf16[256,256]{1,0:T(8,128)(2,1)S(1)}, bf16[256,256]{1,0:T(8,128)(2,1)S(1)}, u32[]{:S(2)}, u32[]{:S(2)}) %collective-permute-start.6) | collective-permute-done | bytes 131104 | tf_op jit(solution)/shard_map/ppermute | solution.py:344
  39.9 1.5 %collective-permute-start.15 = (bf16[256,256]{1,0:T(8,128)(2,1)S(1)}, bf16[256,256]{1,0:T(8,128)(2,1)S(1)}, u32[]{:S(2)}, u32[]{:S(2)}) collective-permute-start(bf16[256,256]{1,0:T(8,128)(2,1)S(1)} %collective-permute-done.6.refs_3_.refs_6_), channel_id=1, source_target_pairs={{0,4},{4,0},{8,12},{12,8},{16,20},{20,16},{24,28},{28,24},{1,5},{5... | collective-permute-start | bytes 393224 | tf_op jit(solution)/shard_map/ppermute | solution.py:352
  41.4 2.7 %collective-permute-done.7.refs_4_.refs_7_ = bf16[256,256]{1,0:T(8,128)(2,1)S(1)} collective-permute-done((bf16[256,256]{1,0:T(8,128)(2,1)S(1)}, bf16[256,256]{1,0:T(8,128)(2,1)S(1)}, u32[]{:S(2)}, u32[]{:S(2)}) %collective-permute-start.7) | collective-permute-done | bytes 131104 | tf_op jit(solution)/shard_map/ppermute | solution.py:344
  44.0 1.5 %collective-permute-start.16 = (bf16[256,256]{1,0:T(8,128)(2,1)S(1)}, bf16[256,256]{1,0:T(8,128)(2,1)S(1)}, u32[]{:S(2)}, u32[]{:S(2)}) collective-permute-start(bf16[256,256]{1,0:T(8,128)(2,1)S(1)} %collective-permute-done.7.refs_4_.refs_7_), channel_id=1, source_target_pairs={{0,4},{4,0},{8,12},{12,8},{16,20},{20,16},{24,28},{28,24},{1,5},{5... | collective-permute-start | bytes 393224 | tf_op jit(solution)/shard_map/ppermute | solution.py:352
  45.6 0.0 collective-permute-done.12.refs_3_
  45.6 1.9 %collective-permute-start.8 = (bf16[256,1024]{1,0:T(8,128)(2,1)S(1)}, bf16[256,1024]{1,0:T(8,128)(2,1)S(1)}, u32[]{:S(2)}, u32[]{:S(2)}) collective-permute-start(bf16[256,1024]{1,0:T(8,128)(2,1)S(1)} %gate.7), channel_id=1, source_target_pairs={{0,0},{1,25},{2,10},{3,19},{4,4},{5,29},{6,14},{7,23},{8,8},{9,17}... | collective-permute-start | bytes 1572872 | tf_op jit(solution)/shard_map/ppermute | solution.py:407
  47.5 0.0 collective-permute-done.13.refs_8_
  47.5 0.0 collective-permute-done.15.refs_10_
  47.5 1.6 %collective-permute-done.16.refs_11_ = bf16[256,256]{1,0:T(8,128)(2,1)S(1)} collective-permute-done((bf16[256,256]{1,0:T(8,128)(2,1)S(1)}, bf16[256,256]{1,0:T(8,128)(2,1)S(1)}, u32[]{:S(2)}, u32[]{:S(2)}) %collective-permute-start.16) | collective-permute-done | bytes 131104 | tf_op jit(solution)/shard_map/ppermute | solution.py:352
  49.1 7.8 %attend.1 = (bf16[2,512,128]{2,1,0:T(8,128)(2,1)S(1)}, bf16[2,512,128]{2,1,0:T(8,128)(2,1)S(1)}, bf16[2,512,128]{2,1,0:T(8,128)(2,1)S(1)}, bf16[2,512,128]{2,1,0...) custom-call(s32[3]{0:T(128)S(1)} %pad_add_fusion.place.refs_4_, ...), custom_call_target="tpu_custom_call" | custom-call | flops 14000000000 | bytes 49000000 | tf_op jit(solution)/shard_map/attend/pallas_call | solution.py:418
  56.9 1.6 %collective-permute-start.17 = (bf16[4,256,256]{2,1,0:T(8,128)(2,1)S(1)}, bf16[4,256,256]{2,1,0:T(8,128)(2,1)S(1)}, u32[]{:S(2)}, u32[]{:S(2)}) collective-permute-start(bf16[4,256,256]{2,1,0:T(8,128)(2,1)S(1)} %get-tuple-element.55), channel_id=1, source_target_pairs={{0,4},{4,0},{8,12},{12,8},{16,20},{20,16},{24,28},{28,24},{1,5},{5... | collective-permute-start | bytes 1572872 | tf_op jit(solution)/shard_map/ppermute | solution.py:352
  58.5 1.5 %collective-permute-start.18 = (bf16[2,512,128]{2,1,0:T(8,128)(2,1)S(1)}, bf16[2,512,128]{2,1,0:T(8,128)(2,1)S(1)}, u32[]{:S(2)}, u32[]{:S(2)}) collective-permute-start(bf16[2,512,128]{2,1,0:T(8,128)(2,1)S(1)} %get-tuple-element.56), channel_id=1, source_target_pairs={{0,8},{4,12},{8,0},{12,4},{16,24},{20,28},{24,16},{28,20},{1,9},{5... | collective-permute-start | bytes 786440 | tf_op jit(solution)/shard_map/ppermute | solution.py:344
  60.0 0.8 collective-permute-start.19
  60.8 1.5 %collective-permute-done.8.refs_0_.refs_2_ = bf16[256,1024]{1,0:T(8,128)(2,1)S(1)} collective-permute-done((bf16[256,1024]{1,0:T(8,128)(2,1)S(1)}, bf16[256,1024]{1,0:T(8,128)(2,1)S(1)}, u32[]{:S(2)}, u32[]{:S(2)}) %collective-permute-start.8) | collective-permute-done | bytes 524320 | tf_op jit(solution)/shard_map/ppermute | solution.py:407
  62.2 7.7 %collective-permute-done.18.refs_0_.refs_1_ = bf16[2,512,128]{2,1,0:T(8,128)(2,1)S(1)} collective-permute-done((bf16[2,512,128]{2,1,0:T(8,128)(2,1)S(1)}, bf16[2,512,128]{2,1,0:T(8,128)(2,1)S(1)}, u32[]{:S(2)}, u32[]{:S(2)}) %collective-permute-start.18) | collective-permute-done | bytes 262176 | tf_op jit(solution)/shard_map/ppermute | solution.py:344
  69.9 2.9 %collective-permute-done.19.refs_1_.refs_2_ = bf16[2,512,128]{2,1,0:T(8,128)(2,1)S(1)} collective-permute-done((bf16[2,512,128]{2,1,0:T(8,128)(2,1)S(1)}, bf16[2,512,128]{2,1,0:T(8,128)(2,1)S(1)}, u32[]{:S(2)}, u32[]{:S(2)}) %collective-permute-start.19) | collective-permute-done | bytes 262176 | tf_op jit(solution)/shard_map/ppermute | solution.py:344
  72.8 0.0 collective-permute-done.17.received
  72.8 0.1 sum.1.refs_5_
  72.9 0.1 collective-permute-start.20
  73.0 2.7 %collective-permute-start.30 = (bf16[4,256,256]{2,1,0:T(8,128)(2,1)S(1)}, bf16[4,256,256]{2,1,0:T(8,128)(2,1)S(1)}, u32[]{:S(2)}, u32[]{:S(2)}) collective-permute-start(bf16[4,256,256]{2,1,0:T(8,128)(2,1)S(1)} %sum.1.refs_5_), channel_id=1, source_target_pairs={{8,16},{12,20},{16,8},{20,12},{9,17},{13,21},{17,9},{21,13},{10,18... | collective-permute-start | bytes 1572872 | tf_op jit(solution)/shard_map/ppermute | solution.py:347
  75.7 0.1 collective-permute-start.9
  75.8 0.5 collective-permute-start.11
  76.3 9.8 %collective-permute-done.20.refs_1_.refs_5_ = bf16[4,256,256]{2,1,0:T(8,128)(2,1)S(1)} collective-permute-done((bf16[4,256,256]{2,1,0:T(8,128)(2,1)S(1)}, bf16[4,256,256]{2,1,0:T(8,128)(2,1)S(1)}, u32[]{:S(2)}, u32[]{:S(2)}) %collective-permute-start.20) | collective-permute-done | bytes 524320 | tf_op jit(solution)/shard_map/ppermute | solution.py:344
  86.1 2.3 %collective-permute-start.22 = (bf16[4,256,256]{2,1,0:T(8,128)(2,1)S(1)}, bf16[4,256,256]{2,1,0:T(8,128)(2,1)S(1)}, u32[]{:S(2)}, u32[]{:S(2)}) collective-permute-start(bf16[4,256,256]{2,1,0:T(8,128)(2,1)S(1)} %collective-permute-done.20.refs_1_.refs_5_), channel_id=1, source_target_pairs={{8,16},{12,20},{16,8},{20,12},{9,17},{13,21},{17,9},{21,13},{10,18... | collective-permute-start | bytes 1572872 | tf_op jit(solution)/shard_map/ppermute | solution.py:347
  88.4 1.3 %collective-permute-start.31 = (bf16[4,256,256]{2,1,0:T(8,128)(2,1)S(1)}, bf16[4,256,256]{2,1,0:T(8,128)(2,1)S(1)}, u32[]{:S(2)}, u32[]{:S(2)}) collective-permute-start(bf16[4,256,256]{2,1,0:T(8,128)(2,1)S(1)} %collective-permute-done.30.refs_5_), channel_id=1, source_target_pairs={{16,24},{20,28},{8,0},{12,4},{17,25},{21,29},{9,1},{13,5},{18,26},... | collective-permute-start | bytes 1572872 | tf_op jit(solution)/shard_map/ppermute | solution.py:347
  89.7 1.3 %collective-permute-start.21 = (bf16[2,528,128]{2,1,0:T(8,128)(2,1)S(1)}, bf16[2,528,128]{2,1,0:T(8,128)(2,1)S(1)}, u32[]{:S(2)}, u32[]{:S(2)}) collective-permute-start(bf16[2,528,128]{2,1,0:T(8,128)(2,1)S(1)} %gate.8), channel_id=1, source_target_pairs={{0,8},{4,12},{24,16},{28,20},{1,9},{5,13},{25,17},{29,21},{2,10},{... | collective-permute-start | bytes 811016 | tf_op jit(solution)/shard_map/ppermute | solution.py:347
  91.0 0.6 turn.1
  91.6 1.3 %weigh.5 = (f32[512,256]{1,0:T(8,128)S(1)}, bf16[512,256]{1,0:T(8,128)(2,1)S(1)}) custom-call(s32[3]{0:T(128)S(1)} %pad_add_fusion.place.refs_4_, bf16[2,512,256]{2,1,0:T(8,128)(2,1)S(1)} %get-tuple-element.47.refs_0_, bf16[2,512,256]{2,1,0:T(8,128)(2,1)S(1)} %get-tuple-element.48.refs_1_, bf16[2,512,256]{2,1,0:T(8,128)(2,1)S(1)} %get-tuple-element.49.refs_2_, ...), custom_call_target="tpu_custom_call" | custom-call | flops 2000000000 | bytes 7000000 | tf_op jit(solution)/shard_map/weigh/pallas_call | solution.py:481
  92.9 0.6 collective-permute-start.29
  93.5 6.7 %collective-permute-done.22.refs_1_.refs_5_ = bf16[4,256,256]{2,1,0:T(8,128)(2,1)S(1)} collective-permute-done((bf16[4,256,256]{2,1,0:T(8,128)(2,1)S(1)}, bf16[4,256,256]{2,1,0:T(8,128)(2,1)S(1)}, u32[]{:S(2)}, u32[]{:S(2)}) %collective-permute-start.22) | collective-permute-done | bytes 524320 | tf_op jit(solution)/shard_map/ppermute | solution.py:347
  100.1 1.3 %collective-permute-start.25 = (bf16[4,256,256]{2,1,0:T(8,128)(2,1)S(1)}, bf16[4,256,256]{2,1,0:T(8,128)(2,1)S(1)}, u32[]{:S(2)}, u32[]{:S(2)}) collective-permute-start(bf16[4,256,256]{2,1,0:T(8,128)(2,1)S(1)} %collective-permute-done.22.refs_1_.refs_5_), channel_id=1, source_target_pairs={{16,24},{20,28},{8,0},{12,4},{17,25},{21,29},{9,1},{13,5},{18,26},... | collective-permute-start | bytes 1572872 | tf_op jit(solution)/shard_map/ppermute | solution.py:347
  101.5 1.3 %weigh.6 = (f32[512,256]{1,0:T(8,128)S(1)}, bf16[512,256]{1,0:T(8,128)(2,1)S(1)}) custom-call(s32[3]{0:T(128)S(1)} %pad_add_fusion.place.refs_4_, bf16[2,512,256]{2,1,0:T(8,128)(2,1)S(1)} %get-tuple-element.47.refs_0_, bf16[2,512,256]{2,1,0:T(8,128)(2,1)S(1)} %get-tuple-element.48.refs_1_, bf16[2,512,256]{2,1,0:T(8,128)(2,1)S(1)} %get-tuple-element.49.refs_2_, ...), custom_call_target="tpu_custom_call" | custom-call | flops 2000000000 | bytes 7000000 | tf_op jit(solution)/shard_map/weigh/pallas_call | solution.py:481
  102.7 0.6 collective-permute-start.24
  103.3 2.2 %collective-permute-start.23 = (bf16[2,528,128]{2,1,0:T(8,128)(2,1)S(1)}, bf16[2,528,128]{2,1,0:T(8,128)(2,1)S(1)}, u32[]{:S(2)}, u32[]{:S(2)}) collective-permute-start(bf16[2,528,128]{2,1,0:T(8,128)(2,1)S(1)} %gate.9), channel_id=1, source_target_pairs={{8,16},{12,20},{16,8},{20,12},{9,17},{13,21},{17,9},{21,13},{10,18... | collective-permute-start | bytes 811016 | tf_op jit(solution)/shard_map/ppermute | solution.py:347
  105.5 1.3 %weigh.9 = (f32[512,256]{1,0:T(8,128)S(1)}, bf16[512,256]{1,0:T(8,128)(2,1)S(1)}) custom-call(s32[3]{0:T(128)S(1)} %pad_add_fusion.place.refs_4_, bf16[2,512,256]{2,1,0:T(8,128)(2,1)S(1)} %get-tuple-element.47.refs_0_, bf16[2,512,256]{2,1,0:T(8,128)(2,1)S(1)} %get-tuple-element.48.refs_1_, bf16[2,512,256]{2,1,0:T(8,128)(2,1)S(1)} %get-tuple-element.49.refs_2_, ...), custom_call_target="tpu_custom_call" | custom-call | flops 2000000000 | bytes 7000000 | tf_op jit(solution)/shard_map/weigh/pallas_call | solution.py:481
  106.8 1.6 %collective-permute-start.32 = (bf16[512,256]{1,0:T(8,128)(2,1)S(1)}, bf16[512,256]{1,0:T(8,128)(2,1)S(1)}, u32[]{:S(2)}, u32[]{:S(2)}) collective-permute-start(bf16[512,256]{1,0:T(8,128)(2,1)S(1)} %get-tuple-element.67), channel_id=1, source_target_pairs={{0,4},{4,0},{8,12},{12,8},{16,20},{20,16},{24,28},{28,24},{1,5},{5... | collective-permute-start | bytes 786440 | tf_op jit(solution)/shard_map/ppermute | solution.py:352
  108.4 1.6 %unpack.1 = (bf16[512,512]{1,0:T(8,128)(2,1)}, bf16[512,512]{1,0:T(8,128)(2,1)}) custom-call(s32[3]{0:T(128)S(1)} %pad_add_fusion.place.refs_4_, bf16[2,512,128]{2,1,0:T(8,128)(2,1)S(1)} %get-tuple-element.62.refs_0_, bf16[2,512,128]{2,1,0:T(8,128)(2,1)S(1)} %collective-permute-done.18.refs_0_.refs_1_, ...), custom_call_target="tpu_custom_call" | custom-call | flops 2000000000 | bytes 7000000 | tf_op jit(solution)/shard_map/unpack/pallas_call | solution.py:512
  110.0 1.9 %collective-permute-done.24.refs_1_.refs_4_ = bf16[512,256]{1,0:T(8,128)(2,1)S(1)} collective-permute-done((bf16[512,256]{1,0:T(8,128)(2,1)S(1)}, bf16[512,256]{1,0:T(8,128)(2,1)S(1)}, u32[]{:S(2)}, u32[]{:S(2)}) %collective-permute-start.24) | collective-permute-done | bytes 262176 | tf_op jit(solution)/shard_map/ppermute | solution.py:352
  112.0 1.3 %collective-permute-start.28 = (bf16[2,528,128]{2,1,0:T(8,128)(2,1)S(1)}, bf16[2,528,128]{2,1,0:T(8,128)(2,1)S(1)}, u32[]{:S(2)}, u32[]{:S(2)}) collective-permute-start(bf16[2,528,128]{2,1,0:T(8,128)(2,1)S(1)} %gate.10.refs_4_), channel_id=1, source_target_pairs={{16,24},{20,28},{8,0},{12,4},{17,25},{21,29},{9,1},{13,5},{18,26},... | collective-permute-start | bytes 811016 | tf_op jit(solution)/shard_map/ppermute | solution.py:347
  113.3 1.0 weigh.7.refs_4_.refs_1_
  114.3 1.3 %collective-permute-start.26 = (bf16[512,256]{1,0:T(8,128)(2,1)S(1)}, bf16[512,256]{1,0:T(8,128)(2,1)S(1)}, u32[]{:S(2)}, u32[]{:S(2)}) collective-permute-start(bf16[512,256]{1,0:T(8,128)(2,1)S(1)} %weigh.7.refs_4_.refs_1_), channel_id=1, source_target_pairs={{0,4},{4,0},{8,12},{12,8},{16,20},{20,16},{24,28},{28,24},{1,5},{5... | collective-permute-start | bytes 786440 | tf_op jit(solution)/shard_map/ppermute | solution.py:352
  115.6 2.2 %collective-permute-start.27 = (bf16[2,512,128]{2,1,0:T(8,128)(2,1)S(1)}, bf16[2,512,128]{2,1,0:T(8,128)(2,1)S(1)}, u32[]{:S(2)}, u32[]{:S(2)}) collective-permute-start(bf16[2,512,128]{2,1,0:T(8,128)(2,1)S(1)} %gate.11), channel_id=1, source_target_pairs={{8,16},{12,20},{16,8},{20,12},{9,17},{13,21},{17,9},{21,13},{10,18... | collective-permute-start | bytes 786440 | tf_op jit(solution)/shard_map/ppermute | solution.py:347
  117.8 2.1 %collect.1 = (f32[512,512]{1,0:T(8,128)}, f32[512,512]{1,0:T(8,128)}) custom-call(s32[3]{0:T(128)S(1)} %pad_add_fusion.place.refs_4_, f32[512,256]{1,0:T(8,128)S(1)} %get-tuple-element.58.refs_4_.refs_0_, f32[512,256]{1,0:T(8,128)S(1)} %get-tuple-element.59.refs_2_.refs_1_, f32[512,256]{1,0:T(8,128)S(1)} %get-tuple-element.66.refs_2_, ...), custom_call_target="tpu_custom_call" | custom-call | flops 2000000000 | bytes 7000000 | tf_op jit(solution)/shard_map/collect/pallas_call | solution.py:522
  119.9 1.0 weigh.8.kept
  120.9 2.9 %collective-permute-done.27.near = bf16[2,512,128]{2,1,0:T(8,128)(2,1)S(1)} collective-permute-done((bf16[2,512,128]{2,1,0:T(8,128)(2,1)S(1)}, bf16[2,512,128]{2,1,0:T(8,128)(2,1)S(1)}, u32[]{:S(2)}, u32[]{:S(2)}) %collective-permute-start.27) | collective-permute-done | bytes 262176 | tf_op jit(solution)/shard_map/ppermute | solution.py:347
  123.8 1.5 %finish.1 = (bf16[512,512]{1,0:T(8,128)(2,1)}, bf16[512,512]{1,0:T(8,128)(2,1)}, f32[512,512]{1,0:T(8,128)}, f32[512,512]{1,0:T(8,128)}) custom-call(s32[3]{0:T(128)S(1)} %pad_add_fusion.place.refs_4_, f32[512,256]{1,0:T(8,128)S(1)} %weigh.8.kept, ...), custom_call_target="tpu_custom_call", output_to_operand_aliasing={{0}: (5, {}), {1}: (6, {}), {2}: (7, {}), {3}: (8, {})} | custom-call | flops 1000000000 | bytes 3500000 | tf_op jit(solution)/shard_map/finish/pallas_call | solution.py:531
  (22 shorter events, 0.0 us)
Async XLA Ops:
  3.0 15.3 %collective-permute-start.1 = (bf16[272,1024]{1,0:T(8,128)(2,1)S(1)}, bf16[272,1024]{1,0:T(8,128)(2,1)S(1)}, u32[]{:S(2)}, u32[]{:S(2)}) collective-permute-start(bf16[272,1024]{1,0:T(8,128)(2,1)S(1)} %get-tuple-element.37.refs_0_), channel_id=1, source_target_pairs={{0,2},{1,3},{2,0},{3,1},{4,6},{5,7},{6,4},{7,5},{8,10},{9,11},{10,... | collective-permute-start | bytes 1671176 | tf_op jit(solution)/shard_map/ppermute | solution.py:355
  3.6 11.2 %collective-permute-start.2 = (bf16[1040,128]{1,0:T(8,128)(2,1)S(1)}, bf16[1040,128]{1,0:T(8,128)(2,1)S(1)}, u32[]{:S(2)}, u32[]{:S(2)}) collective-permute-start(bf16[1040,128]{1,0:T(8,128)(2,1)S(1)} %get-tuple-element.39), channel_id=1, source_target_pairs={{0,8},{4,12},{8,0},{12,4},{16,24},{20,28},{24,16},{28,20},{1,9},{5... | collective-permute-start | bytes 798728 | tf_op jit(solution)/shard_map/ppermute | solution.py:344
  3.6 14.7 %collective-permute-start.3 = (bf16[1040,128]{1,0:T(8,128)(2,1)S(1)}, bf16[1040,128]{1,0:T(8,128)(2,1)S(1)}, u32[]{:S(2)}, u32[]{:S(2)}) collective-permute-start(bf16[1040,128]{1,0:T(8,128)(2,1)S(1)} %get-tuple-element.40), channel_id=1, source_target_pairs={{0,16},{4,20},{8,24},{12,28},{16,0},{20,4},{24,8},{28,12},{1,17},{... | collective-permute-start | bytes 798728 | tf_op jit(solution)/shard_map/ppermute | solution.py:344
  6.6 12.4 %collective-permute-start = (bf16[272,1024]{1,0:T(8,128)(2,1)S(1)}, bf16[272,1024]{1,0:T(8,128)(2,1)S(1)}, u32[]{:S(2)}, u32[]{:S(2)}) collective-permute-start(bf16[272,1024]{1,0:T(8,128)(2,1)S(1)} %get-tuple-element.37.refs_0_), channel_id=1, source_target_pairs={{0,1},{1,0},{2,3},{3,2},{4,5},{5,4},{6,7},{7,6},{8,9},{9,8},{10,11... | collective-permute-start | bytes 1671176 | tf_op jit(solution)/shard_map/ppermute | solution.py:355
  18.3 2.0 %collective-permute-start.4 = (bf16[272,1024]{1,0:T(8,128)(2,1)S(1)}, bf16[272,1024]{1,0:T(8,128)(2,1)S(1)}, u32[]{:S(2)}, u32[]{:S(2)}) collective-permute-start(bf16[272,1024]{1,0:T(8,128)(2,1)S(1)} %get-tuple-element.41.refs_2_), channel_id=1, source_target_pairs={{0,1},{1,0},{2,3},{3,2},{4,5},{5,4},{6,7},{7,6},{8,9},{9,8},{10,11... | collective-permute-start | bytes 1671176 | tf_op jit(solution)/shard_map/ppermute | solution.py:355
  18.3 27.3 %collective-permute-start.12 = (bf16[1040,128]{1,0:T(8,128)(2,1)S(1)}, bf16[1040,128]{1,0:T(8,128)(2,1)S(1)}, u32[]{:S(2)}, u32[]{:S(2)}) collective-permute-start(bf16[1040,128]{1,0:T(8,128)(2,1)S(1)} %get-tuple-element.52), channel_id=1, source_target_pairs={{0,24},{4,28},{8,16},{12,20},{16,8},{20,12},{24,0},{28,4},{1,25},{... | collective-permute-start | bytes 798728 | tf_op jit(solution)/shard_map/ppermute | solution.py:344
  27.3 6.5 %collective-permute-start.5 = (bf16[256,256]{1,0:T(8,128)(2,1)S(1)}, bf16[256,256]{1,0:T(8,128)(2,1)S(1)}, u32[]{:S(2)}, u32[]{:S(2)}) collective-permute-start(bf16[256,256]{1,0:T(8,128)(2,1)S(1)} %get-tuple-element.44), channel_id=1, source_target_pairs={{0,8},{4,12},{8,0},{12,4},{16,24},{20,28},{24,16},{28,20},{1,9},{5... | collective-permute-start | bytes 393224 | tf_op jit(solution)/shard_map/ppermute | solution.py:344
  29.6 10.3 %collective-permute-start.6 = (bf16[256,256]{1,0:T(8,128)(2,1)S(1)}, bf16[256,256]{1,0:T(8,128)(2,1)S(1)}, u32[]{:S(2)}, u32[]{:S(2)}) collective-permute-start(bf16[256,256]{1,0:T(8,128)(2,1)S(1)} %get-tuple-element.45), channel_id=1, source_target_pairs={{0,16},{4,20},{8,24},{12,28},{16,0},{20,4},{24,8},{28,12},{1,17},{... | collective-permute-start | bytes 393224 | tf_op jit(solution)/shard_map/ppermute | solution.py:344
  30.1 14.0 %collective-permute-start.7 = (bf16[256,256]{1,0:T(8,128)(2,1)S(1)}, bf16[256,256]{1,0:T(8,128)(2,1)S(1)}, u32[]{:S(2)}, u32[]{:S(2)}) collective-permute-start(bf16[256,256]{1,0:T(8,128)(2,1)S(1)} %get-tuple-element.46), channel_id=1, source_target_pairs={{0,24},{4,28},{8,16},{12,20},{16,8},{20,12},{24,0},{28,4},{1,25},{... | collective-permute-start | bytes 393224 | tf_op jit(solution)/shard_map/ppermute | solution.py:344
  31.1 16.4 %collective-permute-start.13 = (bf16[256,256]{1,0:T(8,128)(2,1)S(1)}, bf16[256,256]{1,0:T(8,128)(2,1)S(1)}, u32[]{:S(2)}, u32[]{:S(2)}) collective-permute-start(bf16[256,256]{1,0:T(8,128)(2,1)S(1)} %get-tuple-element.43.refs_1_.refs_4_), channel_id=1, source_target_pairs={{0,4},{4,0},{8,12},{12,8},{16,20},{20,16},{24,28},{28,24},{1,5},{5... | collective-permute-start | bytes 393224 | tf_op jit(solution)/shard_map/ppermute | solution.py:352
  33.9 13.6 %collective-permute-start.14 = (bf16[256,256]{1,0:T(8,128)(2,1)S(1)}, bf16[256,256]{1,0:T(8,128)(2,1)S(1)}, u32[]{:S(2)}, u32[]{:S(2)}) collective-permute-start(bf16[256,256]{1,0:T(8,128)(2,1)S(1)} %collective-permute-done.5.refs_2_.refs_5_), channel_id=1, source_target_pairs={{0,4},{4,0},{8,12},{12,8},{16,20},{20,16},{24,28},{28,24},{1,5},{5... | collective-permute-start | bytes 393224 | tf_op jit(solution)/shard_map/ppermute | solution.py:352
  39.9 7.6 %collective-permute-start.15 = (bf16[256,256]{1,0:T(8,128)(2,1)S(1)}, bf16[256,256]{1,0:T(8,128)(2,1)S(1)}, u32[]{:S(2)}, u32[]{:S(2)}) collective-permute-start(bf16[256,256]{1,0:T(8,128)(2,1)S(1)} %collective-permute-done.6.refs_3_.refs_6_), channel_id=1, source_target_pairs={{0,4},{4,0},{8,12},{12,8},{16,20},{20,16},{24,28},{28,24},{1,5},{5... | collective-permute-start | bytes 393224 | tf_op jit(solution)/shard_map/ppermute | solution.py:352
  44.0 5.1 %collective-permute-start.16 = (bf16[256,256]{1,0:T(8,128)(2,1)S(1)}, bf16[256,256]{1,0:T(8,128)(2,1)S(1)}, u32[]{:S(2)}, u32[]{:S(2)}) collective-permute-start(bf16[256,256]{1,0:T(8,128)(2,1)S(1)} %collective-permute-done.7.refs_4_.refs_7_), channel_id=1, source_target_pairs={{0,4},{4,0},{8,12},{12,8},{16,20},{20,16},{24,28},{28,24},{1,5},{5... | collective-permute-start | bytes 393224 | tf_op jit(solution)/shard_map/ppermute | solution.py:352
  45.6 16.7 %collective-permute-start.8 = (bf16[256,1024]{1,0:T(8,128)(2,1)S(1)}, bf16[256,1024]{1,0:T(8,128)(2,1)S(1)}, u32[]{:S(2)}, u32[]{:S(2)}) collective-permute-start(bf16[256,1024]{1,0:T(8,128)(2,1)S(1)} %gate.7), channel_id=1, source_target_pairs={{0,0},{1,25},{2,10},{3,19},{4,4},{5,29},{6,14},{7,23},{8,8},{9,17}... | collective-permute-start | bytes 1572872 | tf_op jit(solution)/shard_map/ppermute | solution.py:407
  56.9 15.9 %collective-permute-start.17 = (bf16[4,256,256]{2,1,0:T(8,128)(2,1)S(1)}, bf16[4,256,256]{2,1,0:T(8,128)(2,1)S(1)}, u32[]{:S(2)}, u32[]{:S(2)}) collective-permute-start(bf16[4,256,256]{2,1,0:T(8,128)(2,1)S(1)} %get-tuple-element.55), channel_id=1, source_target_pairs={{0,4},{4,0},{8,12},{12,8},{16,20},{20,16},{24,28},{28,24},{1,5},{5... | collective-permute-start | bytes 1572872 | tf_op jit(solution)/shard_map/ppermute | solution.py:352
  58.5 11.4 %collective-permute-start.18 = (bf16[2,512,128]{2,1,0:T(8,128)(2,1)S(1)}, bf16[2,512,128]{2,1,0:T(8,128)(2,1)S(1)}, u32[]{:S(2)}, u32[]{:S(2)}) collective-permute-start(bf16[2,512,128]{2,1,0:T(8,128)(2,1)S(1)} %get-tuple-element.56), channel_id=1, source_target_pairs={{0,8},{4,12},{8,0},{12,4},{16,24},{20,28},{24,16},{28,20},{1,9},{5... | collective-permute-start | bytes 786440 | tf_op jit(solution)/shard_map/ppermute | solution.py:344
  60.0 12.8 %collective-permute-start.19 = (bf16[2,512,128]{2,1,0:T(8,128)(2,1)S(1)}, bf16[2,512,128]{2,1,0:T(8,128)(2,1)S(1)}, u32[]{:S(2)}, u32[]{:S(2)}) collective-permute-start(bf16[2,512,128]{2,1,0:T(8,128)(2,1)S(1)} %get-tuple-element.57), channel_id=1, source_target_pairs={{0,16},{4,20},{8,24},{12,28},{16,0},{20,4},{24,8},{28,12},{1,17},{... | collective-permute-start | bytes 786440 | tf_op jit(solution)/shard_map/ppermute | solution.py:344
  62.2 13.6 %collective-permute-start.10 = (bf16[256,1024]{1,0:T(8,128)(2,1)S(1)}, bf16[256,1024]{1,0:T(8,128)(2,1)S(1)}, u32[]{:S(2)}, u32[]{:S(2)}) collective-permute-start(bf16[256,1024]{1,0:T(8,128)(2,1)S(1)} %collective-permute-done.8.refs_0_.refs_2_), channel_id=1, source_target_pairs={{0,2},{1,3},{2,0},{3,1},{4,6},{5,7},{6,4},{7,5},{8,10},{9,11},{10,... | collective-permute-start | bytes 1572872 | tf_op jit(solution)/shard_map/ppermute | solution.py:355
  72.9 13.2 %collective-permute-start.20 = (bf16[4,256,256]{2,1,0:T(8,128)(2,1)S(1)}, bf16[4,256,256]{2,1,0:T(8,128)(2,1)S(1)}, u32[]{:S(2)}, u32[]{:S(2)}) collective-permute-start(bf16[4,256,256]{2,1,0:T(8,128)(2,1)S(1)} %sum.1.refs_5_), channel_id=1, source_target_pairs={{0,8},{4,12},{8,0},{12,4},{16,24},{20,28},{24,16},{28,20},{1,9},{5... | collective-permute-start | bytes 1572872 | tf_op jit(solution)/shard_map/ppermute | solution.py:344
  73.0 15.4 %collective-permute-start.30 = (bf16[4,256,256]{2,1,0:T(8,128)(2,1)S(1)}, bf16[4,256,256]{2,1,0:T(8,128)(2,1)S(1)}, u32[]{:S(2)}, u32[]{:S(2)}) collective-permute-start(bf16[4,256,256]{2,1,0:T(8,128)(2,1)S(1)} %sum.1.refs_5_), channel_id=1, source_target_pairs={{8,16},{12,20},{16,8},{20,12},{9,17},{13,21},{17,9},{21,13},{10,18... | collective-permute-start | bytes 1572872 | tf_op jit(solution)/shard_map/ppermute | solution.py:347
  75.7 15.3 %collective-permute-start.9 = (bf16[256,1024]{1,0:T(8,128)(2,1)S(1)}, bf16[256,1024]{1,0:T(8,128)(2,1)S(1)}, u32[]{:S(2)}, u32[]{:S(2)}) collective-permute-start(bf16[256,1024]{1,0:T(8,128)(2,1)S(1)} %collective-permute-done.8.refs_0_.refs_2_), channel_id=1, source_target_pairs={{0,1},{1,0},{2,3},{3,2},{4,5},{5,4},{6,7},{7,6},{8,9},{9,8},{10,11... | collective-permute-start | bytes 1572872 | tf_op jit(solution)/shard_map/ppermute | solution.py:355
  75.8 15.2 %collective-permute-start.11 = (bf16[256,1024]{1,0:T(8,128)(2,1)S(1)}, bf16[256,1024]{1,0:T(8,128)(2,1)S(1)}, u32[]{:S(2)}, u32[]{:S(2)}) collective-permute-start(bf16[256,1024]{1,0:T(8,128)(2,1)S(1)} %collective-permute-done.10.refs_2_), channel_id=1, source_target_pairs={{0,1},{1,0},{2,3},{3,2},{4,5},{5,4},{6,7},{7,6},{8,9},{9,8},{10,11... | collective-permute-start | bytes 1572872 | tf_op jit(solution)/shard_map/ppermute | solution.py:355
  86.1 14.1 %collective-permute-start.22 = (bf16[4,256,256]{2,1,0:T(8,128)(2,1)S(1)}, bf16[4,256,256]{2,1,0:T(8,128)(2,1)S(1)}, u32[]{:S(2)}, u32[]{:S(2)}) collective-permute-start(bf16[4,256,256]{2,1,0:T(8,128)(2,1)S(1)} %collective-permute-done.20.refs_1_.refs_5_), channel_id=1, source_target_pairs={{8,16},{12,20},{16,8},{20,12},{9,17},{13,21},{17,9},{21,13},{10,18... | collective-permute-start | bytes 1572872 | tf_op jit(solution)/shard_map/ppermute | solution.py:347
  88.4 17.1 %collective-permute-start.31 = (bf16[4,256,256]{2,1,0:T(8,128)(2,1)S(1)}, bf16[4,256,256]{2,1,0:T(8,128)(2,1)S(1)}, u32[]{:S(2)}, u32[]{:S(2)}) collective-permute-start(bf16[4,256,256]{2,1,0:T(8,128)(2,1)S(1)} %collective-permute-done.30.refs_5_), channel_id=1, source_target_pairs={{16,24},{20,28},{8,0},{12,4},{17,25},{21,29},{9,1},{13,5},{18,26},... | collective-permute-start | bytes 1572872 | tf_op jit(solution)/shard_map/ppermute | solution.py:347
  89.7 13.6 %collective-permute-start.21 = (bf16[2,528,128]{2,1,0:T(8,128)(2,1)S(1)}, bf16[2,528,128]{2,1,0:T(8,128)(2,1)S(1)}, u32[]{:S(2)}, u32[]{:S(2)}) collective-permute-start(bf16[2,528,128]{2,1,0:T(8,128)(2,1)S(1)} %gate.8), channel_id=1, source_target_pairs={{0,8},{4,12},{24,16},{28,20},{1,9},{5,13},{25,17},{29,21},{2,10},{... | collective-permute-start | bytes 811016 | tf_op jit(solution)/shard_map/ppermute | solution.py:347
  92.9 12.6 %collective-permute-start.29 = (bf16[512,256]{1,0:T(8,128)(2,1)S(1)}, bf16[512,256]{1,0:T(8,128)(2,1)S(1)}, u32[]{:S(2)}, u32[]{:S(2)}) collective-permute-start(bf16[512,256]{1,0:T(8,128)(2,1)S(1)} %get-tuple-element.65), channel_id=1, source_target_pairs={{0,4},{4,0},{8,12},{12,8},{16,20},{20,16},{24,28},{28,24},{1,5},{5... | collective-permute-start | bytes 786440 | tf_op jit(solution)/shard_map/ppermute | solution.py:352
  100.1 13.1 %collective-permute-start.25 = (bf16[4,256,256]{2,1,0:T(8,128)(2,1)S(1)}, bf16[4,256,256]{2,1,0:T(8,128)(2,1)S(1)}, u32[]{:S(2)}, u32[]{:S(2)}) collective-permute-start(bf16[4,256,256]{2,1,0:T(8,128)(2,1)S(1)} %collective-permute-done.22.refs_1_.refs_5_), channel_id=1, source_target_pairs={{16,24},{20,28},{8,0},{12,4},{17,25},{21,29},{9,1},{13,5},{18,26},... | collective-permute-start | bytes 1572872 | tf_op jit(solution)/shard_map/ppermute | solution.py:347
  102.7 9.2 %collective-permute-start.24 = (bf16[512,256]{1,0:T(8,128)(2,1)S(1)}, bf16[512,256]{1,0:T(8,128)(2,1)S(1)}, u32[]{:S(2)}, u32[]{:S(2)}) collective-permute-start(bf16[512,256]{1,0:T(8,128)(2,1)S(1)} %get-tuple-element.60), channel_id=1, source_target_pairs={{0,4},{4,0},{8,12},{12,8},{16,20},{20,16},{24,28},{28,24},{1,5},{5... | collective-permute-start | bytes 786440 | tf_op jit(solution)/shard_map/ppermute | solution.py:352
  103.3 8.7 %collective-permute-start.23 = (bf16[2,528,128]{2,1,0:T(8,128)(2,1)S(1)}, bf16[2,528,128]{2,1,0:T(8,128)(2,1)S(1)}, u32[]{:S(2)}, u32[]{:S(2)}) collective-permute-start(bf16[2,528,128]{2,1,0:T(8,128)(2,1)S(1)} %gate.9), channel_id=1, source_target_pairs={{8,16},{12,20},{16,8},{20,12},{9,17},{13,21},{17,9},{21,13},{10,18... | collective-permute-start | bytes 811016 | tf_op jit(solution)/shard_map/ppermute | solution.py:347
  106.8 11.0 %collective-permute-start.32 = (bf16[512,256]{1,0:T(8,128)(2,1)S(1)}, bf16[512,256]{1,0:T(8,128)(2,1)S(1)}, u32[]{:S(2)}, u32[]{:S(2)}) collective-permute-start(bf16[512,256]{1,0:T(8,128)(2,1)S(1)} %get-tuple-element.67), channel_id=1, source_target_pairs={{0,4},{4,0},{8,12},{12,8},{16,20},{20,16},{24,28},{28,24},{1,5},{5... | collective-permute-start | bytes 786440 | tf_op jit(solution)/shard_map/ppermute | solution.py:352
  112.0 8.9 %collective-permute-start.28 = (bf16[2,528,128]{2,1,0:T(8,128)(2,1)S(1)}, bf16[2,528,128]{2,1,0:T(8,128)(2,1)S(1)}, u32[]{:S(2)}, u32[]{:S(2)}) collective-permute-start(bf16[2,528,128]{2,1,0:T(8,128)(2,1)S(1)} %gate.10.refs_4_), channel_id=1, source_target_pairs={{16,24},{20,28},{8,0},{12,4},{17,25},{21,29},{9,1},{13,5},{18,26},... | collective-permute-start | bytes 811016 | tf_op jit(solution)/shard_map/ppermute | solution.py:347
  114.3 6.6 %collective-permute-start.26 = (bf16[512,256]{1,0:T(8,128)(2,1)S(1)}, bf16[512,256]{1,0:T(8,128)(2,1)S(1)}, u32[]{:S(2)}, u32[]{:S(2)}) collective-permute-start(bf16[512,256]{1,0:T(8,128)(2,1)S(1)} %weigh.7.refs_4_.refs_1_), channel_id=1, source_target_pairs={{0,4},{4,0},{8,12},{12,8},{16,20},{20,16},{24,28},{28,24},{1,5},{5... | collective-permute-start | bytes 786440 | tf_op jit(solution)/shard_map/ppermute | solution.py:352
  115.6 8.3 %collective-permute-start.27 = (bf16[2,512,128]{2,1,0:T(8,128)(2,1)S(1)}, bf16[2,512,128]{2,1,0:T(8,128)(2,1)S(1)}, u32[]{:S(2)}, u32[]{:S(2)}) collective-permute-start(bf16[2,512,128]{2,1,0:T(8,128)(2,1)S(1)} %gate.11), channel_id=1, source_target_pairs={{8,16},{12,20},{16,8},{20,12},{9,17},{13,21},{17,9},{21,13},{10,18... | collective-permute-start | bytes 786440 | tf_op jit(solution)/shard_map/ppermute | solution.py:347

commit v3 on v2

--- a/solution.py
+++ b/solution.py
@@ -498,13 +498,11 @@
         received.append(across(other))
         token = received[-2] if len(received) > 1 else own
         if len(kept) == 2:
-            (passing,) = gate([passing], [onward, own])
+            (passing,) = gate([passing], [onward])
             passing = hop(passing, middle)
-    (passing,) = gate([passing], [received[1]])
+    passing, late = gate([passing, given[-1]], [received[1]])
     (other,) = weigh(row_grads[-1], (False,), passing)
-    far = hop(passing, outward)
-    (late,) = gate([given[-1]], [other])
-    near = hop(late, middle)
+    far, near = hop(passing, outward), hop(late, middle)
     received.append(across(other))
     (own,) = weigh(row_grads[-1], (True,), other)
     kept.append(own)

time: 126 us -> 125 us (level)
    ppermute x8, waiting for transfers between devices: 9.59 us -> 6.68 us  [hop(): lax.ppermute(x, 'dp', [(2 * i + y, 2 * j + y) for i, j in pairs for y in...]
    ppermute x9, waiting for transfers between devices: 3.52 us -> 5.27 us  [across(): return lax.ppermute(x, 'dp', [(i, i ^ 1) for i in range(peers)])]
where the time goes in v3:
time: 125 us; the launch traced here: 124 us
  waiting for transfers between devices  55 us (44%)
  starting transfers between devices  39.3 us (31%)
  Pallas kernels  28.9 us (23%)
    ppermute x9, waiting for transfers between devices, along(): return lax.ppermute(x, 'dp', [(i, i ^ 2 * r) for i in range(peers)])  40.3 us
    ppermute x8, starting transfers between devices, hop(): lax.ppermute(x, 'dp', [(2 * i + y, 2 * j + y) for i, j in pairs for y in...  14.4 us
    ppermute x9, starting transfers between devices, across(): return lax.ppermute(x, 'dp', [(i, i ^ 1) for i in range(peers)])  11.9 us
    ppermute x9, starting transfers between devices, along(): return lax.ppermute(x, 'dp', [(i, i ^ 2 * r) for i in range(peers)])  9.87 us
    pallas_call x1, Pallas kernels, chained(): pl.pallas_call(functools.partial(attend_kernel, chain, spans, stored, len...  7.81 us
    pallas_call x1, Pallas kernels, chained(): pl.pallas_call(functools.partial(project_kernel, chain, features), out_sh...  7.09 us
    ppermute x8, waiting for transfers between devices, hop(): lax.ppermute(x, 'dp', [(2 * i + y, 2 * j + y) for i, j in pairs for y in...  6.68 us
    pallas_call x5, Pallas kernels, weigh(): pl.pallas_call(functools.partial(weigh_kernel, chain, wants), out_shape=[...  5.8 us
  transfers between devices with their start and end apart: 33, of which 14 were waited for; matrix products, arithmetic and copies ran while one was open for 0% of the time, Pallas kernels for 20%

profile of v3, /device:TPU:10, one launch (start us, length us, event | category | flops | bytes accessed | tf_op | source)
XLA Modules:
  0.0 124.1 jit_solution(3549077752770669867)
XLA Ops:
  0.6 0.1 pad_add_fusion.place.refs_4_
  0.7 2.3 %pack.1 = (bf16[1040,128]{1,0:T(8,128)(2,1)S(1)}, bf16[1040,128]{1,0:T(8,128)(2,1)S(1)}, bf16[1040,128]{1,0:T(8,128)(2,1)S(1)}, bf16[1040,128]{1,0:T(8,128)(2,1)S(1)}, bf16[272,1024]{1,0:T(8,128)(2,1)S(1)}) custom-call(s32[3]{0:T(128)S(1)} %pad_add_fusion.place.refs_4_, s32[2,8]{1,0:T(2,128)} %bitcast.7, s32[2,8]{1,0:T(2,128)} %bitcast.8, ...), custom_call_target="tpu_custom_call" | custom-call | flops 1000000000 | bytes 3500000 | tf_op jit(solution)/shard_map/pack/pallas_call | solution.py:357
  3.0 0.6 collective-permute-start.1
  3.6 0.0 collective-permute-start.2
  3.6 3.0 %collective-permute-start.3 = (bf16[1040,128]{1,0:T(8,128)(2,1)S(1)}, bf16[1040,128]{1,0:T(8,128)(2,1)S(1)}, u32[]{:S(2)}, u32[]{:S(2)}) collective-permute-start(bf16[1040,128]{1,0:T(8,128)(2,1)S(1)} %get-tuple-element.42), channel_id=1, source_target_pairs={{0,16},{4,20},{8,24},{12,28},{16,0},{20,4},{24,8},{28,12},{1,17},{... | collective-permute-start | bytes 798728 | tf_op jit(solution)/shard_map/ppermute | solution.py:344
  6.6 8.2 %collective-permute-done.2.refs_2_.refs_1_ = bf16[1040,128]{1,0:T(8,128)(2,1)S(1)} collective-permute-done((bf16[1040,128]{1,0:T(8,128)(2,1)S(1)}, bf16[1040,128]{1,0:T(8,128)(2,1)S(1)}, u32[]{:S(2)}, u32[]{:S(2)}) %collective-permute-start.2) | collective-permute-done | bytes 266272 | tf_op jit(solution)/shard_map/ppermute | solution.py:344
  14.8 3.4 %collective-permute-done.3.refs_3_.refs_2_ = bf16[1040,128]{1,0:T(8,128)(2,1)S(1)} collective-permute-done((bf16[1040,128]{1,0:T(8,128)(2,1)S(1)}, bf16[1040,128]{1,0:T(8,128)(2,1)S(1)}, u32[]{:S(2)}, u32[]{:S(2)}) %collective-permute-start.3) | collective-permute-done | bytes 266272 | tf_op jit(solution)/shard_map/ppermute | solution.py:344
  18.3 0.0 collective-permute-start.4
  18.3 0.7 collective-permute-start.12
  19.0 1.2 collective-permute-done.4.refs_3_
  20.2 7.1 %project.1 = (bf16[256,256]{1,0:T(8,128)(2,1)S(1)}, bf16[256,256]{1,0:T(8,128)(2,1)S(1)}, bf16[256,256]{1,0:T(8,128)(2,1)S(1)}, bf16[256,256]{1,0:T(8,128)(2,1)S(1)}, bf16[256,1024]{1,0:T(8,128)(2,1)S(1)}) custom-call(s32[3]{0:T(128)S(1)} %pad_add_fusion.place.refs_4_, bf16[4096,512]{1,0:T(8,128)(2,1)} %w_key.1, bf16[4096,512]{1,0:T(8,128)(2,1)} %w_value.1, ...), custom_call_target="tpu_custom_call" | custom-call | flops 6000000000 | bytes 21000000 | tf_op jit(solution)/shard_map/project/pallas_call | solution.py:387
  27.3 2.2 %collective-permute-start.5 = (bf16[256,256]{1,0:T(8,128)(2,1)S(1)}, bf16[256,256]{1,0:T(8,128)(2,1)S(1)}, u32[]{:S(2)}, u32[]{:S(2)}) collective-permute-start(bf16[256,256]{1,0:T(8,128)(2,1)S(1)} %get-tuple-element.46), channel_id=1, source_target_pairs={{0,8},{4,12},{8,0},{12,4},{16,24},{20,28},{24,16},{28,20},{1,9},{5... | collective-permute-start | bytes 393224 | tf_op jit(solution)/shard_map/ppermute | solution.py:344
  29.6 0.5 collective-permute-start.6
  30.1 1.0 collective-permute-start.7
  31.1 1.5 %collective-permute-start.13 = (bf16[256,256]{1,0:T(8,128)(2,1)S(1)}, bf16[256,256]{1,0:T(8,128)(2,1)S(1)}, u32[]{:S(2)}, u32[]{:S(2)}) collective-permute-start(bf16[256,256]{1,0:T(8,128)(2,1)S(1)} %get-tuple-element.45.refs_1_.refs_4_), channel_id=1, source_target_pairs={{0,4},{4,0},{8,12},{12,8},{16,20},{20,16},{24,28},{28,24},{1,5},{5... | collective-permute-start | bytes 393224 | tf_op jit(solution)/shard_map/ppermute | solution.py:352
  32.6 1.2 collective-permute-done.5.refs_2_.refs_5_
  33.9 1.5 %collective-permute-start.14 = (bf16[256,256]{1,0:T(8,128)(2,1)S(1)}, bf16[256,256]{1,0:T(8,128)(2,1)S(1)}, u32[]{:S(2)}, u32[]{:S(2)}) collective-permute-start(bf16[256,256]{1,0:T(8,128)(2,1)S(1)} %collective-permute-done.5.refs_2_.refs_5_), channel_id=1, source_target_pairs={{0,4},{4,0},{8,12},{12,8},{16,20},{20,16},{24,28},{28,24},{1,5},{5... | collective-permute-start | bytes 393224 | tf_op jit(solution)/shard_map/ppermute | solution.py:352
  35.4 4.5 %collective-permute-done.6.refs_3_.refs_6_ = bf16[256,256]{1,0:T(8,128)(2,1)S(1)} collective-permute-done((bf16[256,256]{1,0:T(8,128)(2,1)S(1)}, bf16[256,256]{1,0:T(8,128)(2,1)S(1)}, u32[]{:S(2)}, u32[]{:S(2)}) %collective-permute-start.6) | collective-permute-done | bytes 131104 | tf_op jit(solution)/shard_map/ppermute | solution.py:344
  39.9 1.5 %collective-permute-start.15 = (bf16[256,256]{1,0:T(8,128)(2,1)S(1)}, bf16[256,256]{1,0:T(8,128)(2,1)S(1)}, u32[]{:S(2)}, u32[]{:S(2)}) collective-permute-start(bf16[256,256]{1,0:T(8,128)(2,1)S(1)} %collective-permute-done.6.refs_3_.refs_6_), channel_id=1, source_target_pairs={{0,4},{4,0},{8,12},{12,8},{16,20},{20,16},{24,28},{28,24},{1,5},{5... | collective-permute-start | bytes 393224 | tf_op jit(solution)/shard_map/ppermute | solution.py:352
  41.4 2.7 %collective-permute-done.7.refs_4_.refs_7_ = bf16[256,256]{1,0:T(8,128)(2,1)S(1)} collective-permute-done((bf16[256,256]{1,0:T(8,128)(2,1)S(1)}, bf16[256,256]{1,0:T(8,128)(2,1)S(1)}, u32[]{:S(2)}, u32[]{:S(2)}) %collective-permute-start.7) | collective-permute-done | bytes 131104 | tf_op jit(solution)/shard_map/ppermute | solution.py:344
  44.0 1.5 %collective-permute-start.16 = (bf16[256,256]{1,0:T(8,128)(2,1)S(1)}, bf16[256,256]{1,0:T(8,128)(2,1)S(1)}, u32[]{:S(2)}, u32[]{:S(2)}) collective-permute-start(bf16[256,256]{1,0:T(8,128)(2,1)S(1)} %collective-permute-done.7.refs_4_.refs_7_), channel_id=1, source_target_pairs={{0,4},{4,0},{8,12},{12,8},{16,20},{20,16},{24,28},{28,24},{1,5},{5... | collective-permute-start | bytes 393224 | tf_op jit(solution)/shard_map/ppermute | solution.py:352
  45.6 0.0 collective-permute-done.12.refs_3_
  45.6 1.9 %collective-permute-start.8 = (bf16[256,1024]{1,0:T(8,128)(2,1)S(1)}, bf16[256,1024]{1,0:T(8,128)(2,1)S(1)}, u32[]{:S(2)}, u32[]{:S(2)}) collective-permute-start(bf16[256,1024]{1,0:T(8,128)(2,1)S(1)} %gate.6), channel_id=1, source_target_pairs={{0,0},{1,25},{2,10},{3,19},{4,4},{5,29},{6,14},{7,23},{8,8},{9,17}... | collective-permute-start | bytes 1572872 | tf_op jit(solution)/shard_map/ppermute | solution.py:407
  47.5 0.0 collective-permute-done.15.refs_10_
  47.5 1.6 %collective-permute-done.16.refs_11_ = bf16[256,256]{1,0:T(8,128)(2,1)S(1)} collective-permute-done((bf16[256,256]{1,0:T(8,128)(2,1)S(1)}, bf16[256,256]{1,0:T(8,128)(2,1)S(1)}, u32[]{:S(2)}, u32[]{:S(2)}) %collective-permute-start.16) | collective-permute-done | bytes 131104 | tf_op jit(solution)/shard_map/ppermute | solution.py:352
  49.1 7.8 %attend.1 = (bf16[2,512,128]{2,1,0:T(8,128)(2,1)S(1)}, bf16[2,512,128]{2,1,0:T(8,128)(2,1)S(1)}, bf16[2,512,128]{2,1,0:T(8,128)(2,1)S(1)}, bf16[2,512,128]{2,1,0...) custom-call(s32[3]{0:T(128)S(1)} %pad_add_fusion.place.refs_4_, ...), custom_call_target="tpu_custom_call" | custom-call | flops 14000000000 | bytes 49000000 | tf_op jit(solution)/shard_map/attend/pallas_call | solution.py:418
  56.9 1.6 %collective-permute-start.17 = (bf16[4,256,256]{2,1,0:T(8,128)(2,1)S(1)}, bf16[4,256,256]{2,1,0:T(8,128)(2,1)S(1)}, u32[]{:S(2)}, u32[]{:S(2)}) collective-permute-start(bf16[4,256,256]{2,1,0:T(8,128)(2,1)S(1)} %get-tuple-element.57), channel_id=1, source_target_pairs={{0,4},{4,0},{8,12},{12,8},{16,20},{20,16},{24,28},{28,24},{1,5},{5... | collective-permute-start | bytes 1572872 | tf_op jit(solution)/shard_map/ppermute | solution.py:352
  58.5 1.5 %collective-permute-start.18 = (bf16[2,512,128]{2,1,0:T(8,128)(2,1)S(1)}, bf16[2,512,128]{2,1,0:T(8,128)(2,1)S(1)}, u32[]{:S(2)}, u32[]{:S(2)}) collective-permute-start(bf16[2,512,128]{2,1,0:T(8,128)(2,1)S(1)} %get-tuple-element.58), channel_id=1, source_target_pairs={{0,8},{4,12},{8,0},{12,4},{16,24},{20,28},{24,16},{28,20},{1,9},{5... | collective-permute-start | bytes 786440 | tf_op jit(solution)/shard_map/ppermute | solution.py:344
  60.0 0.8 collective-permute-start.19
  60.8 1.5 %collective-permute-done.8.refs_0_.refs_2_ = bf16[256,1024]{1,0:T(8,128)(2,1)S(1)} collective-permute-done((bf16[256,1024]{1,0:T(8,128)(2,1)S(1)}, bf16[256,1024]{1,0:T(8,128)(2,1)S(1)}, u32[]{:S(2)}, u32[]{:S(2)}) %collective-permute-start.8) | collective-permute-done | bytes 524320 | tf_op jit(solution)/shard_map/ppermute | solution.py:407
  62.2 0.0 collective-permute-start.10
  62.2 7.7 %collective-permute-done.18.refs_0_.refs_1_ = bf16[2,512,128]{2,1,0:T(8,128)(2,1)S(1)} collective-permute-done((bf16[2,512,128]{2,1,0:T(8,128)(2,1)S(1)}, bf16[2,512,128]{2,1,0:T(8,128)(2,1)S(1)}, u32[]{:S(2)}, u32[]{:S(2)}) %collective-permute-start.18) | collective-permute-done | bytes 262176 | tf_op jit(solution)/shard_map/ppermute | solution.py:344
  69.9 2.9 %collective-permute-done.19.refs_1_.refs_2_ = bf16[2,512,128]{2,1,0:T(8,128)(2,1)S(1)} collective-permute-done((bf16[2,512,128]{2,1,0:T(8,128)(2,1)S(1)}, bf16[2,512,128]{2,1,0:T(8,128)(2,1)S(1)}, u32[]{:S(2)}, u32[]{:S(2)}) %collective-permute-start.19) | collective-permute-done | bytes 262176 | tf_op jit(solution)/shard_map/ppermute | solution.py:344
  72.8 0.1 sum.1.refs_5_
  72.9 0.1 collective-permute-start.20
  73.0 2.7 %collective-permute-start.30 = (bf16[4,256,256]{2,1,0:T(8,128)(2,1)S(1)}, bf16[4,256,256]{2,1,0:T(8,128)(2,1)S(1)}, u32[]{:S(2)}, u32[]{:S(2)}) collective-permute-start(bf16[4,256,256]{2,1,0:T(8,128)(2,1)S(1)} %sum.1.refs_5_), channel_id=1, source_target_pairs={{8,16},{12,20},{16,8},{20,12},{9,17},{13,21},{17,9},{21,13},{10,18... | collective-permute-start | bytes 1572872 | tf_op jit(solution)/shard_map/ppermute | solution.py:347
  75.7 0.1 collective-permute-start.9
  75.8 0.5 collective-permute-start.11
  76.3 9.8 %collective-permute-done.20.refs_1_.refs_5_ = bf16[4,256,256]{2,1,0:T(8,128)(2,1)S(1)} collective-permute-done((bf16[4,256,256]{2,1,0:T(8,128)(2,1)S(1)}, bf16[4,256,256]{2,1,0:T(8,128)(2,1)S(1)}, u32[]{:S(2)}, u32[]{:S(2)}) %collective-permute-start.20) | collective-permute-done | bytes 524320 | tf_op jit(solution)/shard_map/ppermute | solution.py:344
  86.1 2.3 %collective-permute-start.22 = (bf16[4,256,256]{2,1,0:T(8,128)(2,1)S(1)}, bf16[4,256,256]{2,1,0:T(8,128)(2,1)S(1)}, u32[]{:S(2)}, u32[]{:S(2)}) collective-permute-start(bf16[4,256,256]{2,1,0:T(8,128)(2,1)S(1)} %collective-permute-done.20.refs_1_.refs_5_), channel_id=1, source_target_pairs={{8,16},{12,20},{16,8},{20,12},{9,17},{13,21},{17,9},{21,13},{10,18... | collective-permute-start | bytes 1572872 | tf_op jit(solution)/shard_map/ppermute | solution.py:347
  88.4 1.3 %collective-permute-start.31 = (bf16[4,256,256]{2,1,0:T(8,128)(2,1)S(1)}, bf16[4,256,256]{2,1,0:T(8,128)(2,1)S(1)}, u32[]{:S(2)}, u32[]{:S(2)}) collective-permute-start(bf16[4,256,256]{2,1,0:T(8,128)(2,1)S(1)} %collective-permute-done.30.refs_5_), channel_id=1, source_target_pairs={{16,24},{20,28},{8,0},{12,4},{17,25},{21,29},{9,1},{13,5},{18,26},... | collective-permute-start | bytes 1572872 | tf_op jit(solution)/shard_map/ppermute | solution.py:347
  89.7 1.3 %collective-permute-start.21 = (bf16[2,528,128]{2,1,0:T(8,128)(2,1)S(1)}, bf16[2,528,128]{2,1,0:T(8,128)(2,1)S(1)}, u32[]{:S(2)}, u32[]{:S(2)}) collective-permute-start(bf16[2,528,128]{2,1,0:T(8,128)(2,1)S(1)} %gate.7), channel_id=1, source_target_pairs={{0,8},{4,12},{24,16},{28,20},{1,9},{5,13},{25,17},{29,21},{2,10},{... | collective-permute-start | bytes 811016 | tf_op jit(solution)/shard_map/ppermute | solution.py:347
  91.0 0.6 turn.1
  91.6 1.3 %weigh.5 = (f32[512,256]{1,0:T(8,128)S(1)}, bf16[512,256]{1,0:T(8,128)(2,1)S(1)}) custom-call(s32[3]{0:T(128)S(1)} %pad_add_fusion.place.refs_4_, bf16[2,512,256]{2,1,0:T(8,128)(2,1)S(1)} %get-tuple-element.49.refs_0_, bf16[2,512,256]{2,1,0:T(8,128)(2,1)S(1)} %get-tuple-element.50.refs_1_, bf16[2,512,256]{2,1,0:T(8,128)(2,1)S(1)} %get-tuple-element.51.refs_2_, ...), custom_call_target="tpu_custom_call" | custom-call | flops 2000000000 | bytes 7000000 | tf_op jit(solution)/shard_map/weigh/pallas_call | solution.py:481
  92.9 0.6 collective-permute-start.29
  93.5 6.7 %collective-permute-done.22.refs_1_.refs_5_ = bf16[4,256,256]{2,1,0:T(8,128)(2,1)S(1)} collective-permute-done((bf16[4,256,256]{2,1,0:T(8,128)(2,1)S(1)}, bf16[4,256,256]{2,1,0:T(8,128)(2,1)S(1)}, u32[]{:S(2)}, u32[]{:S(2)}) %collective-permute-start.22) | collective-permute-done | bytes 524320 | tf_op jit(solution)/shard_map/ppermute | solution.py:347
  100.1 1.3 %collective-permute-start.25 = (bf16[4,256,256]{2,1,0:T(8,128)(2,1)S(1)}, bf16[4,256,256]{2,1,0:T(8,128)(2,1)S(1)}, u32[]{:S(2)}, u32[]{:S(2)}) collective-permute-start(bf16[4,256,256]{2,1,0:T(8,128)(2,1)S(1)} %collective-permute-done.22.refs_1_.refs_5_), channel_id=1, source_target_pairs={{16,24},{20,28},{8,0},{12,4},{17,25},{21,29},{9,1},{13,5},{18,26},... | collective-permute-start | bytes 1572872 | tf_op jit(solution)/shard_map/ppermute | solution.py:347
  101.5 1.3 %weigh.6 = (f32[512,256]{1,0:T(8,128)S(1)}, bf16[512,256]{1,0:T(8,128)(2,1)S(1)}) custom-call(s32[3]{0:T(128)S(1)} %pad_add_fusion.place.refs_4_, bf16[2,512,256]{2,1,0:T(8,128)(2,1)S(1)} %get-tuple-element.49.refs_0_, bf16[2,512,256]{2,1,0:T(8,128)(2,1)S(1)} %get-tuple-element.50.refs_1_, bf16[2,512,256]{2,1,0:T(8,128)(2,1)S(1)} %get-tuple-element.51.refs_2_, ...), custom_call_target="tpu_custom_call" | custom-call | flops 2000000000 | bytes 7000000 | tf_op jit(solution)/shard_map/weigh/pallas_call | solution.py:481
  102.7 0.6 collective-permute-start.24
  103.3 2.2 %collective-permute-start.23 = (bf16[2,528,128]{2,1,0:T(8,128)(2,1)S(1)}, bf16[2,528,128]{2,1,0:T(8,128)(2,1)S(1)}, u32[]{:S(2)}, u32[]{:S(2)}) collective-permute-start(bf16[2,528,128]{2,1,0:T(8,128)(2,1)S(1)} %gate.8), channel_id=1, source_target_pairs={{8,16},{12,20},{16,8},{20,12},{9,17},{13,21},{17,9},{21,13},{10,18... | collective-permute-start | bytes 811016 | tf_op jit(solution)/shard_map/ppermute | solution.py:347
  105.5 1.3 %weigh.9 = (f32[512,256]{1,0:T(8,128)S(1)}, bf16[512,256]{1,0:T(8,128)(2,1)S(1)}) custom-call(s32[3]{0:T(128)S(1)} %pad_add_fusion.place.refs_4_, bf16[2,512,256]{2,1,0:T(8,128)(2,1)S(1)} %get-tuple-element.49.refs_0_, bf16[2,512,256]{2,1,0:T(8,128)(2,1)S(1)} %get-tuple-element.50.refs_1_, bf16[2,512,256]{2,1,0:T(8,128)(2,1)S(1)} %get-tuple-element.51.refs_2_, ...), custom_call_target="tpu_custom_call" | custom-call | flops 2000000000 | bytes 7000000 | tf_op jit(solution)/shard_map/weigh/pallas_call | solution.py:481
  106.8 1.6 %collective-permute-start.32 = (bf16[512,256]{1,0:T(8,128)(2,1)S(1)}, bf16[512,256]{1,0:T(8,128)(2,1)S(1)}, u32[]{:S(2)}, u32[]{:S(2)}) collective-permute-start(bf16[512,256]{1,0:T(8,128)(2,1)S(1)} %get-tuple-element.71), channel_id=1, source_target_pairs={{0,4},{4,0},{8,12},{12,8},{16,20},{20,16},{24,28},{28,24},{1,5},{5... | collective-permute-start | bytes 786440 | tf_op jit(solution)/shard_map/ppermute | solution.py:352
  108.4 1.6 %unpack.1 = (bf16[512,512]{1,0:T(8,128)(2,1)}, bf16[512,512]{1,0:T(8,128)(2,1)}) custom-call(s32[3]{0:T(128)S(1)} %pad_add_fusion.place.refs_4_, bf16[2,512,128]{2,1,0:T(8,128)(2,1)S(1)} %get-tuple-element.65.refs_0_, bf16[2,512,128]{2,1,0:T(8,128)(2,1)S(1)} %collective-permute-done.18.refs_0_.refs_1_, ...), custom_call_target="tpu_custom_call" | custom-call | flops 2000000000 | bytes 7000000 | tf_op jit(solution)/shard_map/unpack/pallas_call | solution.py:510
  110.0 1.9 %collective-permute-done.24.refs_2_.refs_4_ = bf16[512,256]{1,0:T(8,128)(2,1)S(1)} collective-permute-done((bf16[512,256]{1,0:T(8,128)(2,1)S(1)}, bf16[512,256]{1,0:T(8,128)(2,1)S(1)}, u32[]{:S(2)}, u32[]{:S(2)}) %collective-permute-start.24) | collective-permute-done | bytes 262176 | tf_op jit(solution)/shard_map/ppermute | solution.py:352
  112.0 0.0 collective-permute-done.23.refs_0_
  112.0 1.9 %collective-permute-start.27 = (bf16[2,512,128]{2,1,0:T(8,128)(2,1)S(1)}, bf16[2,512,128]{2,1,0:T(8,128)(2,1)S(1)}, u32[]{:S(2)}, u32[]{:S(2)}) collective-permute-start(bf16[2,512,128]{2,1,0:T(8,128)(2,1)S(1)} %get-tuple-element.64), channel_id=1, source_target_pairs={{8,16},{12,20},{16,8},{20,12},{9,17},{13,21},{17,9},{21,13},{10,18... | collective-permute-start | bytes 786440 | tf_op jit(solution)/shard_map/ppermute | solution.py:347
  113.9 1.3 %collective-permute-start.28 = (bf16[2,528,128]{2,1,0:T(8,128)(2,1)S(1)}, bf16[2,528,128]{2,1,0:T(8,128)(2,1)S(1)}, u32[]{:S(2)}, u32[]{:S(2)}) collective-permute-start(bf16[2,528,128]{2,1,0:T(8,128)(2,1)S(1)} %get-tuple-element.63.refs_4_), channel_id=1, source_target_pairs={{16,24},{20,28},{8,0},{12,4},{17,25},{21,29},{9,1},{13,5},{18,26},... | collective-permute-start | bytes 811016 | tf_op jit(solution)/shard_map/ppermute | solution.py:347
  115.2 1.0 weigh.7.refs_4_
  116.2 1.6 %collective-permute-start.26 = (bf16[512,256]{1,0:T(8,128)(2,1)S(1)}, bf16[512,256]{1,0:T(8,128)(2,1)S(1)}, u32[]{:S(2)}, u32[]{:S(2)}) collective-permute-start(bf16[512,256]{1,0:T(8,128)(2,1)S(1)} %weigh.7.refs_4_), channel_id=1, source_target_pairs={{0,4},{4,0},{8,12},{12,8},{16,20},{20,16},{24,28},{28,24},{1,5},{5... | collective-permute-start | bytes 786440 | tf_op jit(solution)/shard_map/ppermute | solution.py:352
  117.8 2.1 %collect.1 = (f32[512,512]{1,0:T(8,128)}, f32[512,512]{1,0:T(8,128)}) custom-call(s32[3]{0:T(128)S(1)} %pad_add_fusion.place.refs_4_, f32[512,256]{1,0:T(8,128)S(1)} %get-tuple-element.61.refs_4_.refs_0_, f32[512,256]{1,0:T(8,128)S(1)} %get-tuple-element.68.refs_1_, f32[512,256]{1,0:T(8,128)S(1)} %get-tuple-element.70.refs_2_, ...), custom_call_target="tpu_custom_call" | custom-call | flops 2000000000 | bytes 7000000 | tf_op jit(solution)/shard_map/collect/pallas_call | solution.py:520
  119.9 1.0 weigh.8.kept
  120.9 0.0 collective-permute-done.28.far
  120.9 1.7 %collective-permute-done.26.received = bf16[512,256]{1,0:T(8,128)(2,1)S(1)} collective-permute-done((bf16[512,256]{1,0:T(8,128)(2,1)S(1)}, bf16[512,256]{1,0:T(8,128)(2,1)S(1)}, u32[]{:S(2)}, u32[]{:S(2)}) %collective-permute-start.26) | collective-permute-done | bytes 262176 | tf_op jit(solution)/shard_map/ppermute | solution.py:352
  122.6 1.5 %finish.1 = (bf16[512,512]{1,0:T(8,128)(2,1)}, bf16[512,512]{1,0:T(8,128)(2,1)}, f32[512,512]{1,0:T(8,128)}, f32[512,512]{1,0:T(8,128)}) custom-call(s32[3]{0:T(128)S(1)} %pad_add_fusion.place.refs_4_, f32[512,256]{1,0:T(8,128)S(1)} %weigh.8.kept, ...), custom_call_target="tpu_custom_call", output_to_operand_aliasing={{0}: (5, {}), {1}: (6, {}), {2}: (7, {}), {3}: (8, {})} | custom-call | flops 1000000000 | bytes 3500000 | tf_op jit(solution)/shard_map/finish/pallas_call | solution.py:529
  (21 shorter events, 0.0 us)
Async XLA Ops:
  3.0 15.3 %collective-permute-start.1 = (bf16[272,1024]{1,0:T(8,128)(2,1)S(1)}, bf16[272,1024]{1,0:T(8,128)(2,1)S(1)}, u32[]{:S(2)}, u32[]{:S(2)}) collective-permute-start(bf16[272,1024]{1,0:T(8,128)(2,1)S(1)} %get-tuple-element.39.refs_0_), channel_id=1, source_target_pairs={{0,2},{1,3},{2,0},{3,1},{4,6},{5,7},{6,4},{7,5},{8,10},{9,11},{10,... | collective-permute-start | bytes 1671176 | tf_op jit(solution)/shard_map/ppermute | solution.py:355
  3.6 11.2 %collective-permute-start.2 = (bf16[1040,128]{1,0:T(8,128)(2,1)S(1)}, bf16[1040,128]{1,0:T(8,128)(2,1)S(1)}, u32[]{:S(2)}, u32[]{:S(2)}) collective-permute-start(bf16[1040,128]{1,0:T(8,128)(2,1)S(1)} %get-tuple-element.41), channel_id=1, source_target_pairs={{0,8},{4,12},{8,0},{12,4},{16,24},{20,28},{24,16},{28,20},{1,9},{5... | collective-permute-start | bytes 798728 | tf_op jit(solution)/shard_map/ppermute | solution.py:344
  3.6 14.7 %collective-permute-start.3 = (bf16[1040,128]{1,0:T(8,128)(2,1)S(1)}, bf16[1040,128]{1,0:T(8,128)(2,1)S(1)}, u32[]{:S(2)}, u32[]{:S(2)}) collective-permute-start(bf16[1040,128]{1,0:T(8,128)(2,1)S(1)} %get-tuple-element.42), channel_id=1, source_target_pairs={{0,16},{4,20},{8,24},{12,28},{16,0},{20,4},{24,8},{28,12},{1,17},{... | collective-permute-start | bytes 798728 | tf_op jit(solution)/shard_map/ppermute | solution.py:344
  6.6 12.4 %collective-permute-start = (bf16[272,1024]{1,0:T(8,128)(2,1)S(1)}, bf16[272,1024]{1,0:T(8,128)(2,1)S(1)}, u32[]{:S(2)}, u32[]{:S(2)}) collective-permute-start(bf16[272,1024]{1,0:T(8,128)(2,1)S(1)} %get-tuple-element.39.refs_0_), channel_id=1, source_target_pairs={{0,1},{1,0},{2,3},{3,2},{4,5},{5,4},{6,7},{7,6},{8,9},{9,8},{10,11... | collective-permute-start | bytes 1671176 | tf_op jit(solution)/shard_map/ppermute | solution.py:355
  18.3 2.0 %collective-permute-start.4 = (bf16[272,1024]{1,0:T(8,128)(2,1)S(1)}, bf16[272,1024]{1,0:T(8,128)(2,1)S(1)}, u32[]{:S(2)}, u32[]{:S(2)}) collective-permute-start(bf16[272,1024]{1,0:T(8,128)(2,1)S(1)} %get-tuple-element.43.refs_2_), channel_id=1, source_target_pairs={{0,1},{1,0},{2,3},{3,2},{4,5},{5,4},{6,7},{7,6},{8,9},{9,8},{10,11... | collective-permute-start | bytes 1671176 | tf_op jit(solution)/shard_map/ppermute | solution.py:355
  18.3 27.3 %collective-permute-start.12 = (bf16[1040,128]{1,0:T(8,128)(2,1)S(1)}, bf16[1040,128]{1,0:T(8,128)(2,1)S(1)}, u32[]{:S(2)}, u32[]{:S(2)}) collective-permute-start(bf16[1040,128]{1,0:T(8,128)(2,1)S(1)} %get-tuple-element.54), channel_id=1, source_target_pairs={{0,24},{4,28},{8,16},{12,20},{16,8},{20,12},{24,0},{28,4},{1,25},{... | collective-permute-start | bytes 798728 | tf_op jit(solution)/shard_map/ppermute | solution.py:344
  27.3 6.5 %collective-permute-start.5 = (bf16[256,256]{1,0:T(8,128)(2,1)S(1)}, bf16[256,256]{1,0:T(8,128)(2,1)S(1)}, u32[]{:S(2)}, u32[]{:S(2)}) collective-permute-start(bf16[256,256]{1,0:T(8,128)(2,1)S(1)} %get-tuple-element.46), channel_id=1, source_target_pairs={{0,8},{4,12},{8,0},{12,4},{16,24},{20,28},{24,16},{28,20},{1,9},{5... | collective-permute-start | bytes 393224 | tf_op jit(solution)/shard_map/ppermute | solution.py:344
  29.6 10.3 %collective-permute-start.6 = (bf16[256,256]{1,0:T(8,128)(2,1)S(1)}, bf16[256,256]{1,0:T(8,128)(2,1)S(1)}, u32[]{:S(2)}, u32[]{:S(2)}) collective-permute-start(bf16[256,256]{1,0:T(8,128)(2,1)S(1)} %get-tuple-element.47), channel_id=1, source_target_pairs={{0,16},{4,20},{8,24},{12,28},{16,0},{20,4},{24,8},{28,12},{1,17},{... | collective-permute-start | bytes 393224 | tf_op jit(solution)/shard_map/ppermute | solution.py:344
  30.1 14.0 %collective-permute-start.7 = (bf16[256,256]{1,0:T(8,128)(2,1)S(1)}, bf16[256,256]{1,0:T(8,128)(2,1)S(1)}, u32[]{:S(2)}, u32[]{:S(2)}) collective-permute-start(bf16[256,256]{1,0:T(8,128)(2,1)S(1)} %get-tuple-element.48), channel_id=1, source_target_pairs={{0,24},{4,28},{8,16},{12,20},{16,8},{20,12},{24,0},{28,4},{1,25},{... | collective-permute-start | bytes 393224 | tf_op jit(solution)/shard_map/ppermute | solution.py:344
  31.1 16.4 %collective-permute-start.13 = (bf16[256,256]{1,0:T(8,128)(2,1)S(1)}, bf16[256,256]{1,0:T(8,128)(2,1)S(1)}, u32[]{:S(2)}, u32[]{:S(2)}) collective-permute-start(bf16[256,256]{1,0:T(8,128)(2,1)S(1)} %get-tuple-element.45.refs_1_.refs_4_), channel_id=1, source_target_pairs={{0,4},{4,0},{8,12},{12,8},{16,20},{20,16},{24,28},{28,24},{1,5},{5... | collective-permute-start | bytes 393224 | tf_op jit(solution)/shard_map/ppermute | solution.py:352
  33.9 13.6 %collective-permute-start.14 = (bf16[256,256]{1,0:T(8,128)(2,1)S(1)}, bf16[256,256]{1,0:T(8,128)(2,1)S(1)}, u32[]{:S(2)}, u32[]{:S(2)}) collective-permute-start(bf16[256,256]{1,0:T(8,128)(2,1)S(1)} %collective-permute-done.5.refs_2_.refs_5_), channel_id=1, source_target_pairs={{0,4},{4,0},{8,12},{12,8},{16,20},{20,16},{24,28},{28,24},{1,5},{5... | collective-permute-start | bytes 393224 | tf_op jit(solution)/shard_map/ppermute | solution.py:352
  39.9 7.6 %collective-permute-start.15 = (bf16[256,256]{1,0:T(8,128)(2,1)S(1)}, bf16[256,256]{1,0:T(8,128)(2,1)S(1)}, u32[]{:S(2)}, u32[]{:S(2)}) collective-permute-start(bf16[256,256]{1,0:T(8,128)(2,1)S(1)} %collective-permute-done.6.refs_3_.refs_6_), channel_id=1, source_target_pairs={{0,4},{4,0},{8,12},{12,8},{16,20},{20,16},{24,28},{28,24},{1,5},{5... | collective-permute-start | bytes 393224 | tf_op jit(solution)/shard_map/ppermute | solution.py:352
  44.0 5.1 %collective-permute-start.16 = (bf16[256,256]{1,0:T(8,128)(2,1)S(1)}, bf16[256,256]{1,0:T(8,128)(2,1)S(1)}, u32[]{:S(2)}, u32[]{:S(2)}) collective-permute-start(bf16[256,256]{1,0:T(8,128)(2,1)S(1)} %collective-permute-done.7.refs_4_.refs_7_), channel_id=1, source_target_pairs={{0,4},{4,0},{8,12},{12,8},{16,20},{20,16},{24,28},{28,24},{1,5},{5... | collective-permute-start | bytes 393224 | tf_op jit(solution)/shard_map/ppermute | solution.py:352
  45.6 16.7 %collective-permute-start.8 = (bf16[256,1024]{1,0:T(8,128)(2,1)S(1)}, bf16[256,1024]{1,0:T(8,128)(2,1)S(1)}, u32[]{:S(2)}, u32[]{:S(2)}) collective-permute-start(bf16[256,1024]{1,0:T(8,128)(2,1)S(1)} %gate.6), channel_id=1, source_target_pairs={{0,0},{1,25},{2,10},{3,19},{4,4},{5,29},{6,14},{7,23},{8,8},{9,17}... | collective-permute-start | bytes 1572872 | tf_op jit(solution)/shard_map/ppermute | solution.py:407
  56.9 15.9 %collective-permute-start.17 = (bf16[4,256,256]{2,1,0:T(8,128)(2,1)S(1)}, bf16[4,256,256]{2,1,0:T(8,128)(2,1)S(1)}, u32[]{:S(2)}, u32[]{:S(2)}) collective-permute-start(bf16[4,256,256]{2,1,0:T(8,128)(2,1)S(1)} %get-tuple-element.57), channel_id=1, source_target_pairs={{0,4},{4,0},{8,12},{12,8},{16,20},{20,16},{24,28},{28,24},{1,5},{5... | collective-permute-start | bytes 1572872 | tf_op jit(solution)/shard_map/ppermute | solution.py:352
  58.5 11.4 %collective-permute-start.18 = (bf16[2,512,128]{2,1,0:T(8,128)(2,1)S(1)}, bf16[2,512,128]{2,1,0:T(8,128)(2,1)S(1)}, u32[]{:S(2)}, u32[]{:S(2)}) collective-permute-start(bf16[2,512,128]{2,1,0:T(8,128)(2,1)S(1)} %get-tuple-element.58), channel_id=1, source_target_pairs={{0,8},{4,12},{8,0},{12,4},{16,24},{20,28},{24,16},{28,20},{1,9},{5... | collective-permute-start | bytes 786440 | tf_op jit(solution)/shard_map/ppermute | solution.py:344
  60.0 12.8 %collective-permute-start.19 = (bf16[2,512,128]{2,1,0:T(8,128)(2,1)S(1)}, bf16[2,512,128]{2,1,0:T(8,128)(2,1)S(1)}, u32[]{:S(2)}, u32[]{:S(2)}) collective-permute-start(bf16[2,512,128]{2,1,0:T(8,128)(2,1)S(1)} %get-tuple-element.59), channel_id=1, source_target_pairs={{0,16},{4,20},{8,24},{12,28},{16,0},{20,4},{24,8},{28,12},{1,17},{... | collective-permute-start | bytes 786440 | tf_op jit(solution)/shard_map/ppermute | solution.py:344
  62.2 13.6 %collective-permute-start.10 = (bf16[256,1024]{1,0:T(8,128)(2,1)S(1)}, bf16[256,1024]{1,0:T(8,128)(2,1)S(1)}, u32[]{:S(2)}, u32[]{:S(2)}) collective-permute-start(bf16[256,1024]{1,0:T(8,128)(2,1)S(1)} %collective-permute-done.8.refs_0_.refs_2_), channel_id=1, source_target_pairs={{0,2},{1,3},{2,0},{3,1},{4,6},{5,7},{6,4},{7,5},{8,10},{9,11},{10,... | collective-permute-start | bytes 1572872 | tf_op jit(solution)/shard_map/ppermute | solution.py:355
  72.9 13.2 %collective-permute-start.20 = (bf16[4,256,256]{2,1,0:T(8,128)(2,1)S(1)}, bf16[4,256,256]{2,1,0:T(8,128)(2,1)S(1)}, u32[]{:S(2)}, u32[]{:S(2)}) collective-permute-start(bf16[4,256,256]{2,1,0:T(8,128)(2,1)S(1)} %sum.1.refs_5_), channel_id=1, source_target_pairs={{0,8},{4,12},{8,0},{12,4},{16,24},{20,28},{24,16},{28,20},{1,9},{5... | collective-permute-start | bytes 1572872 | tf_op jit(solution)/shard_map/ppermute | solution.py:344
  73.0 15.4 %collective-permute-start.30 = (bf16[4,256,256]{2,1,0:T(8,128)(2,1)S(1)}, bf16[4,256,256]{2,1,0:T(8,128)(2,1)S(1)}, u32[]{:S(2)}, u32[]{:S(2)}) collective-permute-start(bf16[4,256,256]{2,1,0:T(8,128)(2,1)S(1)} %sum.1.refs_5_), channel_id=1, source_target_pairs={{8,16},{12,20},{16,8},{20,12},{9,17},{13,21},{17,9},{21,13},{10,18... | collective-permute-start | bytes 1572872 | tf_op jit(solution)/shard_map/ppermute | solution.py:347
  75.7 15.3 %collective-permute-start.9 = (bf16[256,1024]{1,0:T(8,128)(2,1)S(1)}, bf16[256,1024]{1,0:T(8,128)(2,1)S(1)}, u32[]{:S(2)}, u32[]{:S(2)}) collective-permute-start(bf16[256,1024]{1,0:T(8,128)(2,1)S(1)} %collective-permute-done.8.refs_0_.refs_2_), channel_id=1, source_target_pairs={{0,1},{1,0},{2,3},{3,2},{4,5},{5,4},{6,7},{7,6},{8,9},{9,8},{10,11... | collective-permute-start | bytes 1572872 | tf_op jit(solution)/shard_map/ppermute | solution.py:355
  75.8 15.2 %collective-permute-start.11 = (bf16[256,1024]{1,0:T(8,128)(2,1)S(1)}, bf16[256,1024]{1,0:T(8,128)(2,1)S(1)}, u32[]{:S(2)}, u32[]{:S(2)}) collective-permute-start(bf16[256,1024]{1,0:T(8,128)(2,1)S(1)} %collective-permute-done.10.refs_2_), channel_id=1, source_target_pairs={{0,1},{1,0},{2,3},{3,2},{4,5},{5,4},{6,7},{7,6},{8,9},{9,8},{10,11... | collective-permute-start | bytes 1572872 | tf_op jit(solution)/shard_map/ppermute | solution.py:355
  86.1 14.1 %collective-permute-start.22 = (bf16[4,256,256]{2,1,0:T(8,128)(2,1)S(1)}, bf16[4,256,256]{2,1,0:T(8,128)(2,1)S(1)}, u32[]{:S(2)}, u32[]{:S(2)}) collective-permute-start(bf16[4,256,256]{2,1,0:T(8,128)(2,1)S(1)} %collective-permute-done.20.refs_1_.refs_5_), channel_id=1, source_target_pairs={{8,16},{12,20},{16,8},{20,12},{9,17},{13,21},{17,9},{21,13},{10,18... | collective-permute-start | bytes 1572872 | tf_op jit(solution)/shard_map/ppermute | solution.py:347
  88.4 17.1 %collective-permute-start.31 = (bf16[4,256,256]{2,1,0:T(8,128)(2,1)S(1)}, bf16[4,256,256]{2,1,0:T(8,128)(2,1)S(1)}, u32[]{:S(2)}, u32[]{:S(2)}) collective-permute-start(bf16[4,256,256]{2,1,0:T(8,128)(2,1)S(1)} %collective-permute-done.30.refs_5_), channel_id=1, source_target_pairs={{16,24},{20,28},{8,0},{12,4},{17,25},{21,29},{9,1},{13,5},{18,26},... | collective-permute-start | bytes 1572872 | tf_op jit(solution)/shard_map/ppermute | solution.py:347
  89.7 13.6 %collective-permute-start.21 = (bf16[2,528,128]{2,1,0:T(8,128)(2,1)S(1)}, bf16[2,528,128]{2,1,0:T(8,128)(2,1)S(1)}, u32[]{:S(2)}, u32[]{:S(2)}) collective-permute-start(bf16[2,528,128]{2,1,0:T(8,128)(2,1)S(1)} %gate.7), channel_id=1, source_target_pairs={{0,8},{4,12},{24,16},{28,20},{1,9},{5,13},{25,17},{29,21},{2,10},{... | collective-permute-start | bytes 811016 | tf_op jit(solution)/shard_map/ppermute | solution.py:347
  92.9 12.6 %collective-permute-start.29 = (bf16[512,256]{1,0:T(8,128)(2,1)S(1)}, bf16[512,256]{1,0:T(8,128)(2,1)S(1)}, u32[]{:S(2)}, u32[]{:S(2)}) collective-permute-start(bf16[512,256]{1,0:T(8,128)(2,1)S(1)} %get-tuple-element.69), channel_id=1, source_target_pairs={{0,4},{4,0},{8,12},{12,8},{16,20},{20,16},{24,28},{28,24},{1,5},{5... | collective-permute-start | bytes 786440 | tf_op jit(solution)/shard_map/ppermute | solution.py:352
  100.1 15.1 %collective-permute-start.25 = (bf16[4,256,256]{2,1,0:T(8,128)(2,1)S(1)}, bf16[4,256,256]{2,1,0:T(8,128)(2,1)S(1)}, u32[]{:S(2)}, u32[]{:S(2)}) collective-permute-start(bf16[4,256,256]{2,1,0:T(8,128)(2,1)S(1)} %collective-permute-done.22.refs_1_.refs_5_), channel_id=1, source_target_pairs={{16,24},{20,28},{8,0},{12,4},{17,25},{21,29},{9,1},{13,5},{18,26},... | collective-permute-start | bytes 1572872 | tf_op jit(solution)/shard_map/ppermute | solution.py:347
  102.7 9.2 %collective-permute-start.24 = (bf16[512,256]{1,0:T(8,128)(2,1)S(1)}, bf16[512,256]{1,0:T(8,128)(2,1)S(1)}, u32[]{:S(2)}, u32[]{:S(2)}) collective-permute-start(bf16[512,256]{1,0:T(8,128)(2,1)S(1)} %get-tuple-element.62), channel_id=1, source_target_pairs={{0,4},{4,0},{8,12},{12,8},{16,20},{20,16},{24,28},{28,24},{1,5},{5... | collective-permute-start | bytes 786440 | tf_op jit(solution)/shard_map/ppermute | solution.py:352
  103.3 8.7 %collective-permute-start.23 = (bf16[2,528,128]{2,1,0:T(8,128)(2,1)S(1)}, bf16[2,528,128]{2,1,0:T(8,128)(2,1)S(1)}, u32[]{:S(2)}, u32[]{:S(2)}) collective-permute-start(bf16[2,528,128]{2,1,0:T(8,128)(2,1)S(1)} %gate.8), channel_id=1, source_target_pairs={{8,16},{12,20},{16,8},{20,12},{9,17},{13,21},{17,9},{21,13},{10,18... | collective-permute-start | bytes 811016 | tf_op jit(solution)/shard_map/ppermute | solution.py:347
  106.8 11.0 %collective-permute-start.32 = (bf16[512,256]{1,0:T(8,128)(2,1)S(1)}, bf16[512,256]{1,0:T(8,128)(2,1)S(1)}, u32[]{:S(2)}, u32[]{:S(2)}) collective-permute-start(bf16[512,256]{1,0:T(8,128)(2,1)S(1)} %get-tuple-element.71), channel_id=1, source_target_pairs={{0,4},{4,0},{8,12},{12,8},{16,20},{20,16},{24,28},{28,24},{1,5},{5... | collective-permute-start | bytes 786440 | tf_op jit(solution)/shard_map/ppermute | solution.py:352
  112.0 8.9 %collective-permute-start.27 = (bf16[2,512,128]{2,1,0:T(8,128)(2,1)S(1)}, bf16[2,512,128]{2,1,0:T(8,128)(2,1)S(1)}, u32[]{:S(2)}, u32[]{:S(2)}) collective-permute-start(bf16[2,512,128]{2,1,0:T(8,128)(2,1)S(1)} %get-tuple-element.64), channel_id=1, source_target_pairs={{8,16},{12,20},{16,8},{20,12},{9,17},{13,21},{17,9},{21,13},{10,18... | collective-permute-start | bytes 786440 | tf_op jit(solution)/shard_map/ppermute | solution.py:347
  113.9 7.0 %collective-permute-start.28 = (bf16[2,528,128]{2,1,0:T(8,128)(2,1)S(1)}, bf16[2,528,128]{2,1,0:T(8,128)(2,1)S(1)}, u32[]{:S(2)}, u32[]{:S(2)}) collective-permute-start(bf16[2,528,128]{2,1,0:T(8,128)(2,1)S(1)} %get-tuple-element.63.refs_4_), channel_id=1, source_target_pairs={{16,24},{20,28},{8,0},{12,4},{17,25},{21,29},{9,1},{13,5},{18,26},... | collective-permute-start | bytes 811016 | tf_op jit(solution)/shard_map/ppermute | solution.py:347
  116.2 6.4 %collective-permute-start.26 = (bf16[512,256]{1,0:T(8,128)(2,1)S(1)}, bf16[512,256]{1,0:T(8,128)(2,1)S(1)}, u32[]{:S(2)}, u32[]{:S(2)}) collective-permute-start(bf16[512,256]{1,0:T(8,128)(2,1)S(1)} %weigh.7.refs_4_), channel_id=1, source_target_pairs={{0,4},{4,0},{8,12},{12,8},{16,20},{20,16},{24,28},{28,24},{1,5},{5... | collective-permute-start | bytes 786440 | tf_op jit(solution)/shard_map/ppermute | solution.py:352

commit v4 on v3

--- a/solution.py
+++ b/solution.py
@@ -498,11 +498,12 @@
         received.append(across(other))
         token = received[-2] if len(received) > 1 else own
         if len(kept) == 2:
-            (passing,) = gate([passing], [onward])
+            late, passing = gate([given[-1], passing], [onward, own])
+            returned.append(hop(late, middle))
             passing = hop(passing, middle)
-    passing, late = gate([passing, given[-1]], [received[1]])
+    (passing,) = gate([passing], [kept[2]])
     (other,) = weigh(row_grads[-1], (False,), passing)
-    far, near = hop(passing, outward), hop(late, middle)
+    far = hop(passing, outward)
     received.append(across(other))
     (own,) = weigh(row_grads[-1], (True,), other)
     kept.append(own)
@@ -543,7 +544,7 @@
         place,
         kept[-1],
         received[-1],
-        near,
+        returned[-1],
         far,
         attended,
         query_grad,

time: 125 us -> 124 us (level)
  waiting for transfers between devices: 55 us -> 53.5 us
    ppermute x8, starting transfers between devices: 14.4 us -> 16.1 us  [hop(): lax.ppermute(x, 'dp', [(2 * i + y, 2 * j + y) for i, j in pairs for y in...]
    ppermute x9, waiting for transfers between devices: 5.27 us -> 3.86 us  [across(): return lax.ppermute(x, 'dp', [(i, i ^ 1) for i in range(peers)])]
  transfers between devices with their start and end apart: 33 -> 33, of which waited for: 14 -> 13; matrix products, arithmetic and copies ran while one was open for 0% -> 0% of each run, Pallas kernels for 20% -> 20%
where the time goes in v4:
time: 124 us
  waiting for transfers between devices  53.5 us (43%)
  starting transfers between devices  40.5 us (33%)
  Pallas kernels  28.9 us (23%)
    ppermute x9, waiting for transfers between devices, along(): return lax.ppermute(x, 'dp', [(i, i ^ 2 * r) for i in range(peers)])  40.3 us
    ppermute x8, starting transfers between devices, hop(): lax.ppermute(x, 'dp', [(2 * i + y, 2 * j + y) for i, j in pairs for y in...  16.1 us
    ppermute x9, starting transfers between devices, across(): return lax.ppermute(x, 'dp', [(i, i ^ 1) for i in range(peers)])  11.4 us
    ppermute x9, starting transfers between devices, along(): return lax.ppermute(x, 'dp', [(i, i ^ 2 * r) for i in range(peers)])  9.87 us
    pallas_call x1, Pallas kernels, chained(): pl.pallas_call(functools.partial(attend_kernel, chain, spans, stored, len...  7.81 us
    pallas_call x1, Pallas kernels, chained(): pl.pallas_call(functools.partial(project_kernel, chain, features), out_sh...  7.09 us
    ppermute x8, waiting for transfers between devices, hop(): lax.ppermute(x, 'dp', [(2 * i + y, 2 * j + y) for i, j in pairs for y in...  6.68 us
    pallas_call x5, Pallas kernels, weigh(): pl.pallas_call(functools.partial(weigh_kernel, chain, wants), out_shape=[...  5.8 us
  transfers between devices with their start and end apart: 33, of which 13 were waited for; matrix products, arithmetic and copies ran while one was open for 0% of the time, Pallas kernels for 20%

profile of v4, /device:TPU:10, one launch (start us, length us, event | category | flops | bytes accessed | tf_op | source)
XLA Modules:
  0.0 123.9 jit_solution(14693175595404671595)
XLA Ops:
  0.6 0.1 pad_add_fusion.place.refs_4_
  0.7 2.3 %pack.1 = (bf16[1040,128]{1,0:T(8,128)(2,1)S(1)}, bf16[1040,128]{1,0:T(8,128)(2,1)S(1)}, bf16[1040,128]{1,0:T(8,128)(2,1)S(1)}, bf16[1040,128]{1,0:T(8,128)(2,1)S(1)}, bf16[272,1024]{1,0:T(8,128)(2,1)S(1)}) custom-call(s32[3]{0:T(128)S(1)} %pad_add_fusion.place.refs_4_, s32[2,8]{1,0:T(2,128)} %bitcast.7, s32[2,8]{1,0:T(2,128)} %bitcast.8, ...), custom_call_target="tpu_custom_call" | custom-call | flops 1000000000 | bytes 3500000 | tf_op jit(solution)/shard_map/pack/pallas_call | solution.py:357
  3.0 0.6 collective-permute-start.1
  3.6 3.0 %collective-permute-start.3 = (bf16[1040,128]{1,0:T(8,128)(2,1)S(1)}, bf16[1040,128]{1,0:T(8,128)(2,1)S(1)}, u32[]{:S(2)}, u32[]{:S(2)}) collective-permute-start(bf16[1040,128]{1,0:T(8,128)(2,1)S(1)} %get-tuple-element.42), channel_id=1, source_target_pairs={{0,16},{4,20},{8,24},{12,28},{16,0},{20,4},{24,8},{28,12},{1,17},{... | collective-permute-start | bytes 798728 | tf_op jit(solution)/shard_map/ppermute | solution.py:344
  6.6 0.0 collective-permute-start
  6.6 8.2 %collective-permute-done.2.refs_2_.refs_1_ = bf16[1040,128]{1,0:T(8,128)(2,1)S(1)} collective-permute-done((bf16[1040,128]{1,0:T(8,128)(2,1)S(1)}, bf16[1040,128]{1,0:T(8,128)(2,1)S(1)}, u32[]{:S(2)}, u32[]{:S(2)}) %collective-permute-start.2) | collective-permute-done | bytes 266272 | tf_op jit(solution)/shard_map/ppermute | solution.py:344
  14.8 3.4 %collective-permute-done.3.refs_3_.refs_2_ = bf16[1040,128]{1,0:T(8,128)(2,1)S(1)} collective-permute-done((bf16[1040,128]{1,0:T(8,128)(2,1)S(1)}, bf16[1040,128]{1,0:T(8,128)(2,1)S(1)}, u32[]{:S(2)}, u32[]{:S(2)}) %collective-permute-start.3) | collective-permute-done | bytes 266272 | tf_op jit(solution)/shard_map/ppermute | solution.py:344
  18.3 0.0 collective-permute-done.1.refs_0_
  18.3 0.7 collective-permute-start.12
  19.0 0.0 collective-permute-done.refs_1_
  19.0 1.2 collective-permute-done.4.refs_3_
  20.2 7.1 %project.1 = (bf16[256,256]{1,0:T(8,128)(2,1)S(1)}, bf16[256,256]{1,0:T(8,128)(2,1)S(1)}, bf16[256,256]{1,0:T(8,128)(2,1)S(1)}, bf16[256,256]{1,0:T(8,128)(2,1)S(1)}, bf16[256,1024]{1,0:T(8,128)(2,1)S(1)}) custom-call(s32[3]{0:T(128)S(1)} %pad_add_fusion.place.refs_4_, bf16[4096,512]{1,0:T(8,128)(2,1)} %w_key.1, bf16[4096,512]{1,0:T(8,128)(2,1)} %w_value.1, ...), custom_call_target="tpu_custom_call" | custom-call | flops 6000000000 | bytes 21000000 | tf_op jit(solution)/shard_map/project/pallas_call | solution.py:387
  27.3 2.2 %collective-permute-start.5 = (bf16[256,256]{1,0:T(8,128)(2,1)S(1)}, bf16[256,256]{1,0:T(8,128)(2,1)S(1)}, u32[]{:S(2)}, u32[]{:S(2)}) collective-permute-start(bf16[256,256]{1,0:T(8,128)(2,1)S(1)} %get-tuple-element.46), channel_id=1, source_target_pairs={{0,8},{4,12},{8,0},{12,4},{16,24},{20,28},{24,16},{28,20},{1,9},{5... | collective-permute-start | bytes 393224 | tf_op jit(solution)/shard_map/ppermute | solution.py:344
  29.6 0.5 collective-permute-start.6
  30.1 1.0 collective-permute-start.7
  31.1 1.5 %collective-permute-start.13 = (bf16[256,256]{1,0:T(8,128)(2,1)S(1)}, bf16[256,256]{1,0:T(8,128)(2,1)S(1)}, u32[]{:S(2)}, u32[]{:S(2)}) collective-permute-start(bf16[256,256]{1,0:T(8,128)(2,1)S(1)} %get-tuple-element.45.refs_1_.refs_4_), channel_id=1, source_target_pairs={{0,4},{4,0},{8,12},{12,8},{16,20},{20,16},{24,28},{28,24},{1,5},{5... | collective-permute-start | bytes 393224 | tf_op jit(solution)/shard_map/ppermute | solution.py:352
  32.6 1.2 collective-permute-done.5.refs_2_.refs_5_
  33.9 1.5 %collective-permute-start.14 = (bf16[256,256]{1,0:T(8,128)(2,1)S(1)}, bf16[256,256]{1,0:T(8,128)(2,1)S(1)}, u32[]{:S(2)}, u32[]{:S(2)}) collective-permute-start(bf16[256,256]{1,0:T(8,128)(2,1)S(1)} %collective-permute-done.5.refs_2_.refs_5_), channel_id=1, source_target_pairs={{0,4},{4,0},{8,12},{12,8},{16,20},{20,16},{24,28},{28,24},{1,5},{5... | collective-permute-start | bytes 393224 | tf_op jit(solution)/shard_map/ppermute | solution.py:352
  35.4 4.5 %collective-permute-done.6.refs_3_.refs_6_ = bf16[256,256]{1,0:T(8,128)(2,1)S(1)} collective-permute-done((bf16[256,256]{1,0:T(8,128)(2,1)S(1)}, bf16[256,256]{1,0:T(8,128)(2,1)S(1)}, u32[]{:S(2)}, u32[]{:S(2)}) %collective-permute-start.6) | collective-permute-done | bytes 131104 | tf_op jit(solution)/shard_map/ppermute | solution.py:344
  39.9 1.5 %collective-permute-start.15 = (bf16[256,256]{1,0:T(8,128)(2,1)S(1)}, bf16[256,256]{1,0:T(8,128)(2,1)S(1)}, u32[]{:S(2)}, u32[]{:S(2)}) collective-permute-start(bf16[256,256]{1,0:T(8,128)(2,1)S(1)} %collective-permute-done.6.refs_3_.refs_6_), channel_id=1, source_target_pairs={{0,4},{4,0},{8,12},{12,8},{16,20},{20,16},{24,28},{28,24},{1,5},{5... | collective-permute-start | bytes 393224 | tf_op jit(solution)/shard_map/ppermute | solution.py:352
  41.4 2.7 %collective-permute-done.7.refs_4_.refs_7_ = bf16[256,256]{1,0:T(8,128)(2,1)S(1)} collective-permute-done((bf16[256,256]{1,0:T(8,128)(2,1)S(1)}, bf16[256,256]{1,0:T(8,128)(2,1)S(1)}, u32[]{:S(2)}, u32[]{:S(2)}) %collective-permute-start.7) | collective-permute-done | bytes 131104 | tf_op jit(solution)/shard_map/ppermute | solution.py:344
  44.0 1.5 %collective-permute-start.16 = (bf16[256,256]{1,0:T(8,128)(2,1)S(1)}, bf16[256,256]{1,0:T(8,128)(2,1)S(1)}, u32[]{:S(2)}, u32[]{:S(2)}) collective-permute-start(bf16[256,256]{1,0:T(8,128)(2,1)S(1)} %collective-permute-done.7.refs_4_.refs_7_), channel_id=1, source_target_pairs={{0,4},{4,0},{8,12},{12,8},{16,20},{20,16},{24,28},{28,24},{1,5},{5... | collective-permute-start | bytes 393224 | tf_op jit(solution)/shard_map/ppermute | solution.py:352
  45.6 0.0 collective-permute-done.12.refs_3_
  45.6 1.9 %collective-permute-start.8 = (bf16[256,1024]{1,0:T(8,128)(2,1)S(1)}, bf16[256,1024]{1,0:T(8,128)(2,1)S(1)}, u32[]{:S(2)}, u32[]{:S(2)}) collective-permute-start(bf16[256,1024]{1,0:T(8,128)(2,1)S(1)} %gate.6), channel_id=1, source_target_pairs={{0,0},{1,25},{2,10},{3,19},{4,4},{5,29},{6,14},{7,23},{8,8},{9,17}... | collective-permute-start | bytes 1572872 | tf_op jit(solution)/shard_map/ppermute | solution.py:407
  47.5 0.0 collective-permute-done.13.refs_8_
  47.5 0.0 collective-permute-done.15.refs_10_
  47.5 1.6 %collective-permute-done.16.refs_11_ = bf16[256,256]{1,0:T(8,128)(2,1)S(1)} collective-permute-done((bf16[256,256]{1,0:T(8,128)(2,1)S(1)}, bf16[256,256]{1,0:T(8,128)(2,1)S(1)}, u32[]{:S(2)}, u32[]{:S(2)}) %collective-permute-start.16) | collective-permute-done | bytes 131104 | tf_op jit(solution)/shard_map/ppermute | solution.py:352
  49.1 7.8 %attend.1 = (bf16[2,512,128]{2,1,0:T(8,128)(2,1)S(1)}, bf16[2,512,128]{2,1,0:T(8,128)(2,1)S(1)}, bf16[2,512,128]{2,1,0:T(8,128)(2,1)S(1)}, bf16[2,512,128]{2,1,0...) custom-call(s32[3]{0:T(128)S(1)} %pad_add_fusion.place.refs_4_, ...), custom_call_target="tpu_custom_call" | custom-call | flops 14000000000 | bytes 49000000 | tf_op jit(solution)/shard_map/attend/pallas_call | solution.py:418
  56.9 1.6 %collective-permute-start.17 = (bf16[4,256,256]{2,1,0:T(8,128)(2,1)S(1)}, bf16[4,256,256]{2,1,0:T(8,128)(2,1)S(1)}, u32[]{:S(2)}, u32[]{:S(2)}) collective-permute-start(bf16[4,256,256]{2,1,0:T(8,128)(2,1)S(1)} %get-tuple-element.58), channel_id=1, source_target_pairs={{0,4},{4,0},{8,12},{12,8},{16,20},{20,16},{24,28},{28,24},{1,5},{5... | collective-permute-start | bytes 1572872 | tf_op jit(solution)/shard_map/ppermute | solution.py:352
  58.5 1.5 %collective-permute-start.18 = (bf16[2,512,128]{2,1,0:T(8,128)(2,1)S(1)}, bf16[2,512,128]{2,1,0:T(8,128)(2,1)S(1)}, u32[]{:S(2)}, u32[]{:S(2)}) collective-permute-start(bf16[2,512,128]{2,1,0:T(8,128)(2,1)S(1)} %get-tuple-element.59), channel_id=1, source_target_pairs={{0,8},{4,12},{8,0},{12,4},{16,24},{20,28},{24,16},{28,20},{1,9},{5... | collective-permute-start | bytes 786440 | tf_op jit(solution)/shard_map/ppermute | solution.py:344
  60.0 0.8 collective-permute-start.19
  60.8 1.5 %collective-permute-done.8.refs_0_.refs_2_ = bf16[256,1024]{1,0:T(8,128)(2,1)S(1)} collective-permute-done((bf16[256,1024]{1,0:T(8,128)(2,1)S(1)}, bf16[256,1024]{1,0:T(8,128)(2,1)S(1)}, u32[]{:S(2)}, u32[]{:S(2)}) %collective-permute-start.8) | collective-permute-done | bytes 524320 | tf_op jit(solution)/shard_map/ppermute | solution.py:407
  62.2 7.7 %collective-permute-done.18.refs_0_.refs_1_ = bf16[2,512,128]{2,1,0:T(8,128)(2,1)S(1)} collective-permute-done((bf16[2,512,128]{2,1,0:T(8,128)(2,1)S(1)}, bf16[2,512,128]{2,1,0:T(8,128)(2,1)S(1)}, u32[]{:S(2)}, u32[]{:S(2)}) %collective-permute-start.18) | collective-permute-done | bytes 262176 | tf_op jit(solution)/shard_map/ppermute | solution.py:344
  69.9 2.9 %collective-permute-done.19.refs_1_.refs_2_ = bf16[2,512,128]{2,1,0:T(8,128)(2,1)S(1)} collective-permute-done((bf16[2,512,128]{2,1,0:T(8,128)(2,1)S(1)}, bf16[2,512,128]{2,1,0:T(8,128)(2,1)S(1)}, u32[]{:S(2)}, u32[]{:S(2)}) %collective-permute-start.19) | collective-permute-done | bytes 262176 | tf_op jit(solution)/shard_map/ppermute | solution.py:344
  72.8 0.0 collective-permute-done.17.received
  72.8 0.1 sum.1.refs_5_
  72.9 0.1 collective-permute-start.20
  73.0 2.7 %collective-permute-start.25 = (bf16[4,256,256]{2,1,0:T(8,128)(2,1)S(1)}, bf16[4,256,256]{2,1,0:T(8,128)(2,1)S(1)}, u32[]{:S(2)}, u32[]{:S(2)}) collective-permute-start(bf16[4,256,256]{2,1,0:T(8,128)(2,1)S(1)} %sum.1.refs_5_), channel_id=1, source_target_pairs={{8,16},{12,20},{16,8},{20,12},{9,17},{13,21},{17,9},{21,13},{10,18... | collective-permute-start | bytes 1572872 | tf_op jit(solution)/shard_map/ppermute | solution.py:347
  75.7 0.1 collective-permute-start.9
  75.8 0.0 collective-permute-done.10.refs_2_
  75.8 0.5 collective-permute-start.11
  76.3 9.8 %collective-permute-done.20.refs_1_.refs_5_ = bf16[4,256,256]{2,1,0:T(8,128)(2,1)S(1)} collective-permute-done((bf16[4,256,256]{2,1,0:T(8,128)(2,1)S(1)}, bf16[4,256,256]{2,1,0:T(8,128)(2,1)S(1)}, u32[]{:S(2)}, u32[]{:S(2)}) %collective-permute-start.20) | collective-permute-done | bytes 524320 | tf_op jit(solution)/shard_map/ppermute | solution.py:344
  86.1 2.3 %collective-permute-start.22 = (bf16[4,256,256]{2,1,0:T(8,128)(2,1)S(1)}, bf16[4,256,256]{2,1,0:T(8,128)(2,1)S(1)}, u32[]{:S(2)}, u32[]{:S(2)}) collective-permute-start(bf16[4,256,256]{2,1,0:T(8,128)(2,1)S(1)} %collective-permute-done.20.refs_1_.refs_5_), channel_id=1, source_target_pairs={{8,16},{12,20},{16,8},{20,12},{9,17},{13,21},{17,9},{21,13},{10,18... | collective-permute-start | bytes 1572872 | tf_op jit(solution)/shard_map/ppermute | solution.py:347
  88.4 1.3 %collective-permute-start.26 = (bf16[4,256,256]{2,1,0:T(8,128)(2,1)S(1)}, bf16[4,256,256]{2,1,0:T(8,128)(2,1)S(1)}, u32[]{:S(2)}, u32[]{:S(2)}) collective-permute-start(bf16[4,256,256]{2,1,0:T(8,128)(2,1)S(1)} %collective-permute-done.25.refs_5_), channel_id=1, source_target_pairs={{16,24},{20,28},{8,0},{12,4},{17,25},{21,29},{9,1},{13,5},{18,26},... | collective-permute-start | bytes 1572872 | tf_op jit(solution)/shard_map/ppermute | solution.py:347
  89.7 1.3 %collective-permute-start.21 = (bf16[2,528,128]{2,1,0:T(8,128)(2,1)S(1)}, bf16[2,528,128]{2,1,0:T(8,128)(2,1)S(1)}, u32[]{:S(2)}, u32[]{:S(2)}) collective-permute-start(bf16[2,528,128]{2,1,0:T(8,128)(2,1)S(1)} %gate.7), channel_id=1, source_target_pairs={{0,8},{4,12},{24,16},{28,20},{1,9},{5,13},{25,17},{29,21},{2,10},{... | collective-permute-start | bytes 811016 | tf_op jit(solution)/shard_map/ppermute | solution.py:347
  91.0 0.6 turn.1
  91.6 1.3 %weigh.5 = (f32[512,256]{1,0:T(8,128)S(1)}, bf16[512,256]{1,0:T(8,128)(2,1)S(1)}) custom-call(s32[3]{0:T(128)S(1)} %pad_add_fusion.place.refs_4_, bf16[2,512,256]{2,1,0:T(8,128)(2,1)S(1)} %get-tuple-element.49.refs_0_, bf16[2,512,256]{2,1,0:T(8,128)(2,1)S(1)} %get-tuple-element.50.refs_1_, bf16[2,512,256]{2,1,0:T(8,128)(2,1)S(1)} %get-tuple-element.51.refs_2_, ...), custom_call_target="tpu_custom_call" | custom-call | flops 2000000000 | bytes 7000000 | tf_op jit(solution)/shard_map/weigh/pallas_call | solution.py:481
  92.9 0.6 collective-permute-start.24
  93.5 6.7 %collective-permute-done.22.refs_2_.refs_5_ = bf16[4,256,256]{2,1,0:T(8,128)(2,1)S(1)} collective-permute-done((bf16[4,256,256]{2,1,0:T(8,128)(2,1)S(1)}, bf16[4,256,256]{2,1,0:T(8,128)(2,1)S(1)}, u32[]{:S(2)}, u32[]{:S(2)}) %collective-permute-start.22) | collective-permute-done | bytes 524320 | tf_op jit(solution)/shard_map/ppermute | solution.py:347
  100.1 1.3 %collective-permute-start.27 = (bf16[4,256,256]{2,1,0:T(8,128)(2,1)S(1)}, bf16[4,256,256]{2,1,0:T(8,128)(2,1)S(1)}, u32[]{:S(2)}, u32[]{:S(2)}) collective-permute-start(bf16[4,256,256]{2,1,0:T(8,128)(2,1)S(1)} %collective-permute-done.22.refs_2_.refs_5_), channel_id=1, source_target_pairs={{16,24},{20,28},{8,0},{12,4},{17,25},{21,29},{9,1},{13,5},{18,26},... | collective-permute-start | bytes 1572872 | tf_op jit(solution)/shard_map/ppermute | solution.py:347
  101.5 1.3 %weigh.6 = (f32[512,256]{1,0:T(8,128)S(1)}, bf16[512,256]{1,0:T(8,128)(2,1)S(1)}) custom-call(s32[3]{0:T(128)S(1)} %pad_add_fusion.place.refs_4_, bf16[2,512,256]{2,1,0:T(8,128)(2,1)S(1)} %get-tuple-element.49.refs_0_, bf16[2,512,256]{2,1,0:T(8,128)(2,1)S(1)} %get-tuple-element.50.refs_1_, bf16[2,512,256]{2,1,0:T(8,128)(2,1)S(1)} %get-tuple-element.51.refs_2_, ...), custom_call_target="tpu_custom_call" | custom-call | flops 2000000000 | bytes 7000000 | tf_op jit(solution)/shard_map/weigh/pallas_call | solution.py:481
  102.7 0.6 collective-permute-start.31
  103.3 2.2 %collective-permute-start.23 = (bf16[2,528,128]{2,1,0:T(8,128)(2,1)S(1)}, bf16[2,528,128]{2,1,0:T(8,128)(2,1)S(1)}, u32[]{:S(2)}, u32[]{:S(2)}) collective-permute-start(bf16[2,528,128]{2,1,0:T(8,128)(2,1)S(1)} %get-tuple-element.63), channel_id=1, source_target_pairs={{8,16},{12,20},{16,8},{20,12},{9,17},{13,21},{17,9},{21,13},{10,18... | collective-permute-start | bytes 811016 | tf_op jit(solution)/shard_map/ppermute | solution.py:347
  105.5 1.3 %weigh.7 = (f32[512,256]{1,0:T(8,128)S(1)}, bf16[512,256]{1,0:T(8,128)(2,1)S(1)}) custom-call(s32[3]{0:T(128)S(1)} %pad_add_fusion.place.refs_4_, bf16[2,512,256]{2,1,0:T(8,128)(2,1)S(1)} %get-tuple-element.49.refs_0_, bf16[2,512,256]{2,1,0:T(8,128)(2,1)S(1)} %get-tuple-element.50.refs_1_, bf16[2,512,256]{2,1,0:T(8,128)(2,1)S(1)} %get-tuple-element.51.refs_2_, ...), custom_call_target="tpu_custom_call" | custom-call | flops 2000000000 | bytes 7000000 | tf_op jit(solution)/shard_map/weigh/pallas_call | solution.py:481
  106.8 1.6 %collective-permute-start.32 = (bf16[512,256]{1,0:T(8,128)(2,1)S(1)}, bf16[512,256]{1,0:T(8,128)(2,1)S(1)}, u32[]{:S(2)}, u32[]{:S(2)}) collective-permute-start(bf16[512,256]{1,0:T(8,128)(2,1)S(1)} %get-tuple-element.71), channel_id=1, source_target_pairs={{0,4},{4,0},{8,12},{12,8},{16,20},{20,16},{24,28},{28,24},{1,5},{5... | collective-permute-start | bytes 786440 | tf_op jit(solution)/shard_map/ppermute | solution.py:352
  108.4 1.6 %unpack.1 = (bf16[512,512]{1,0:T(8,128)(2,1)}, bf16[512,512]{1,0:T(8,128)(2,1)}) custom-call(s32[3]{0:T(128)S(1)} %pad_add_fusion.place.refs_4_, bf16[2,512,128]{2,1,0:T(8,128)(2,1)S(1)} %get-tuple-element.67.refs_0_, bf16[2,512,128]{2,1,0:T(8,128)(2,1)S(1)} %collective-permute-done.18.refs_0_.refs_1_, ...), custom_call_target="tpu_custom_call" | custom-call | flops 2000000000 | bytes 7000000 | tf_op jit(solution)/shard_map/unpack/pallas_call | solution.py:511
  110.0 3.6 %collective-permute-start.29 = (bf16[2,512,128]{2,1,0:T(8,128)(2,1)S(1)}, bf16[2,512,128]{2,1,0:T(8,128)(2,1)S(1)}, u32[]{:S(2)}, u32[]{:S(2)}) collective-permute-start(bf16[2,512,128]{2,1,0:T(8,128)(2,1)S(1)} %get-tuple-element.66), channel_id=1, source_target_pairs={{8,16},{12,20},{16,8},{20,12},{9,17},{13,21},{17,9},{21,13},{10,18... | collective-permute-start | bytes 786440 | tf_op jit(solution)/shard_map/ppermute | solution.py:347
  113.7 1.3 %collective-permute-start.30 = (bf16[2,528,128]{2,1,0:T(8,128)(2,1)S(1)}, bf16[2,528,128]{2,1,0:T(8,128)(2,1)S(1)}, u32[]{:S(2)}, u32[]{:S(2)}) collective-permute-start(bf16[2,528,128]{2,1,0:T(8,128)(2,1)S(1)} %gate.9.refs_4_), channel_id=1, source_target_pairs={{16,24},{20,28},{8,0},{12,4},{17,25},{21,29},{9,1},{13,5},{18,26},... | collective-permute-start | bytes 811016 | tf_op jit(solution)/shard_map/ppermute | solution.py:347
  115.0 1.0 weigh.8.refs_4_
  116.0 1.0 collective-permute-start.28
  117.1 2.1 %collect.1 = (f32[512,512]{1,0:T(8,128)}, f32[512,512]{1,0:T(8,128)}) custom-call(s32[3]{0:T(128)S(1)} %pad_add_fusion.place.refs_4_, f32[512,256]{1,0:T(8,128)S(1)} %get-tuple-element.61.refs_4_.refs_0_, f32[512,256]{1,0:T(8,128)S(1)} %get-tuple-element.62.refs_3_.refs_1_, f32[512,256]{1,0:T(8,128)S(1)} %get-tuple-element.65.refs_1_.refs_2_, ...), custom_call_target="tpu_custom_call" | custom-call | flops 2000000000 | bytes 7000000 | tf_op jit(solution)/shard_map/collect/pallas_call | solution.py:521
  119.2 1.0 weigh.9.kept
  120.2 2.3 %collective-permute-done.28.received = bf16[512,256]{1,0:T(8,128)(2,1)S(1)} collective-permute-done((bf16[512,256]{1,0:T(8,128)(2,1)S(1)}, bf16[512,256]{1,0:T(8,128)(2,1)S(1)}, u32[]{:S(2)}, u32[]{:S(2)}) %collective-permute-start.28) | collective-permute-done | bytes 262176 | tf_op jit(solution)/shard_map/ppermute | solution.py:352
  122.5 1.5 %finish.1 = (bf16[512,512]{1,0:T(8,128)(2,1)}, bf16[512,512]{1,0:T(8,128)(2,1)}, f32[512,512]{1,0:T(8,128)}, f32[512,512]{1,0:T(8,128)}) custom-call(s32[3]{0:T(128)S(1)} %pad_add_fusion.place.refs_4_, f32[512,256]{1,0:T(8,128)S(1)} %weigh.9.kept, ...), custom_call_target="tpu_custom_call", output_to_operand_aliasing={{0}: (5, {}), {1}: (6, {}), {2}: (7, {}), {3}: (8, {})} | custom-call | flops 1000000000 | bytes 3500000 | tf_op jit(solution)/shard_map/finish/pallas_call | solution.py:530
  (21 shorter events, 0.0 us)
Async XLA Ops:
  3.0 15.3 %collective-permute-start.1 = (bf16[272,1024]{1,0:T(8,128)(2,1)S(1)}, bf16[272,1024]{1,0:T(8,128)(2,1)S(1)}, u32[]{:S(2)}, u32[]{:S(2)}) collective-permute-start(bf16[272,1024]{1,0:T(8,128)(2,1)S(1)} %get-tuple-element.39.refs_0_), channel_id=1, source_target_pairs={{0,2},{1,3},{2,0},{3,1},{4,6},{5,7},{6,4},{7,5},{8,10},{9,11},{10,... | collective-permute-start | bytes 1671176 | tf_op jit(solution)/shard_map/ppermute | solution.py:355
  3.6 11.2 %collective-permute-start.2 = (bf16[1040,128]{1,0:T(8,128)(2,1)S(1)}, bf16[1040,128]{1,0:T(8,128)(2,1)S(1)}, u32[]{:S(2)}, u32[]{:S(2)}) collective-permute-start(bf16[1040,128]{1,0:T(8,128)(2,1)S(1)} %get-tuple-element.41), channel_id=1, source_target_pairs={{0,8},{4,12},{8,0},{12,4},{16,24},{20,28},{24,16},{28,20},{1,9},{5... | collective-permute-start | bytes 798728 | tf_op jit(solution)/shard_map/ppermute | solution.py:344
  3.6 14.7 %collective-permute-start.3 = (bf16[1040,128]{1,0:T(8,128)(2,1)S(1)}, bf16[1040,128]{1,0:T(8,128)(2,1)S(1)}, u32[]{:S(2)}, u32[]{:S(2)}) collective-permute-start(bf16[1040,128]{1,0:T(8,128)(2,1)S(1)} %get-tuple-element.42), channel_id=1, source_target_pairs={{0,16},{4,20},{8,24},{12,28},{16,0},{20,4},{24,8},{28,12},{1,17},{... | collective-permute-start | bytes 798728 | tf_op jit(solution)/shard_map/ppermute | solution.py:344
  6.6 12.4 %collective-permute-start = (bf16[272,1024]{1,0:T(8,128)(2,1)S(1)}, bf16[272,1024]{1,0:T(8,128)(2,1)S(1)}, u32[]{:S(2)}, u32[]{:S(2)}) collective-permute-start(bf16[272,1024]{1,0:T(8,128)(2,1)S(1)} %get-tuple-element.39.refs_0_), channel_id=1, source_target_pairs={{0,1},{1,0},{2,3},{3,2},{4,5},{5,4},{6,7},{7,6},{8,9},{9,8},{10,11... | collective-permute-start | bytes 1671176 | tf_op jit(solution)/shard_map/ppermute | solution.py:355
  18.3 2.0 %collective-permute-start.4 = (bf16[272,1024]{1,0:T(8,128)(2,1)S(1)}, bf16[272,1024]{1,0:T(8,128)(2,1)S(1)}, u32[]{:S(2)}, u32[]{:S(2)}) collective-permute-start(bf16[272,1024]{1,0:T(8,128)(2,1)S(1)} %get-tuple-element.43.refs_2_), channel_id=1, source_target_pairs={{0,1},{1,0},{2,3},{3,2},{4,5},{5,4},{6,7},{7,6},{8,9},{9,8},{10,11... | collective-permute-start | bytes 1671176 | tf_op jit(solution)/shard_map/ppermute | solution.py:355
  18.3 27.3 %collective-permute-start.12 = (bf16[1040,128]{1,0:T(8,128)(2,1)S(1)}, bf16[1040,128]{1,0:T(8,128)(2,1)S(1)}, u32[]{:S(2)}, u32[]{:S(2)}) collective-permute-start(bf16[1040,128]{1,0:T(8,128)(2,1)S(1)} %get-tuple-element.54), channel_id=1, source_target_pairs={{0,24},{4,28},{8,16},{12,20},{16,8},{20,12},{24,0},{28,4},{1,25},{... | collective-permute-start | bytes 798728 | tf_op jit(solution)/shard_map/ppermute | solution.py:344
  27.3 6.5 %collective-permute-start.5 = (bf16[256,256]{1,0:T(8,128)(2,1)S(1)}, bf16[256,256]{1,0:T(8,128)(2,1)S(1)}, u32[]{:S(2)}, u32[]{:S(2)}) collective-permute-start(bf16[256,256]{1,0:T(8,128)(2,1)S(1)} %get-tuple-element.46), channel_id=1, source_target_pairs={{0,8},{4,12},{8,0},{12,4},{16,24},{20,28},{24,16},{28,20},{1,9},{5... | collective-permute-start | bytes 393224 | tf_op jit(solution)/shard_map/ppermute | solution.py:344
  29.6 10.3 %collective-permute-start.6 = (bf16[256,256]{1,0:T(8,128)(2,1)S(1)}, bf16[256,256]{1,0:T(8,128)(2,1)S(1)}, u32[]{:S(2)}, u32[]{:S(2)}) collective-permute-start(bf16[256,256]{1,0:T(8,128)(2,1)S(1)} %get-tuple-element.47), channel_id=1, source_target_pairs={{0,16},{4,20},{8,24},{12,28},{16,0},{20,4},{24,8},{28,12},{1,17},{... | collective-permute-start | bytes 393224 | tf_op jit(solution)/shard_map/ppermute | solution.py:344
  30.1 14.0 %collective-permute-start.7 = (bf16[256,256]{1,0:T(8,128)(2,1)S(1)}, bf16[256,256]{1,0:T(8,128)(2,1)S(1)}, u32[]{:S(2)}, u32[]{:S(2)}) collective-permute-start(bf16[256,256]{1,0:T(8,128)(2,1)S(1)} %get-tuple-element.48), channel_id=1, source_target_pairs={{0,24},{4,28},{8,16},{12,20},{16,8},{20,12},{24,0},{28,4},{1,25},{... | collective-permute-start | bytes 393224 | tf_op jit(solution)/shard_map/ppermute | solution.py:344
  31.1 16.4 %collective-permute-start.13 = (bf16[256,256]{1,0:T(8,128)(2,1)S(1)}, bf16[256,256]{1,0:T(8,128)(2,1)S(1)}, u32[]{:S(2)}, u32[]{:S(2)}) collective-permute-start(bf16[256,256]{1,0:T(8,128)(2,1)S(1)} %get-tuple-element.45.refs_1_.refs_4_), channel_id=1, source_target_pairs={{0,4},{4,0},{8,12},{12,8},{16,20},{20,16},{24,28},{28,24},{1,5},{5... | collective-permute-start | bytes 393224 | tf_op jit(solution)/shard_map/ppermute | solution.py:352
  33.9 13.6 %collective-permute-start.14 = (bf16[256,256]{1,0:T(8,128)(2,1)S(1)}, bf16[256,256]{1,0:T(8,128)(2,1)S(1)}, u32[]{:S(2)}, u32[]{:S(2)}) collective-permute-start(bf16[256,256]{1,0:T(8,128)(2,1)S(1)} %collective-permute-done.5.refs_2_.refs_5_), channel_id=1, source_target_pairs={{0,4},{4,0},{8,12},{12,8},{16,20},{20,16},{24,28},{28,24},{1,5},{5... | collective-permute-start | bytes 393224 | tf_op jit(solution)/shard_map/ppermute | solution.py:352
  39.9 7.6 %collective-permute-start.15 = (bf16[256,256]{1,0:T(8,128)(2,1)S(1)}, bf16[256,256]{1,0:T(8,128)(2,1)S(1)}, u32[]{:S(2)}, u32[]{:S(2)}) collective-permute-start(bf16[256,256]{1,0:T(8,128)(2,1)S(1)} %collective-permute-done.6.refs_3_.refs_6_), channel_id=1, source_target_pairs={{0,4},{4,0},{8,12},{12,8},{16,20},{20,16},{24,28},{28,24},{1,5},{5... | collective-permute-start | bytes 393224 | tf_op jit(solution)/shard_map/ppermute | solution.py:352
  44.0 5.1 %collective-permute-start.16 = (bf16[256,256]{1,0:T(8,128)(2,1)S(1)}, bf16[256,256]{1,0:T(8,128)(2,1)S(1)}, u32[]{:S(2)}, u32[]{:S(2)}) collective-permute-start(bf16[256,256]{1,0:T(8,128)(2,1)S(1)} %collective-permute-done.7.refs_4_.refs_7_), channel_id=1, source_target_pairs={{0,4},{4,0},{8,12},{12,8},{16,20},{20,16},{24,28},{28,24},{1,5},{5... | collective-permute-start | bytes 393224 | tf_op jit(solution)/shard_map/ppermute | solution.py:352
  45.6 16.7 %collective-permute-start.8 = (bf16[256,1024]{1,0:T(8,128)(2,1)S(1)}, bf16[256,1024]{1,0:T(8,128)(2,1)S(1)}, u32[]{:S(2)}, u32[]{:S(2)}) collective-permute-start(bf16[256,1024]{1,0:T(8,128)(2,1)S(1)} %gate.6), channel_id=1, source_target_pairs={{0,0},{1,25},{2,10},{3,19},{4,4},{5,29},{6,14},{7,23},{8,8},{9,17}... | collective-permute-start | bytes 1572872 | tf_op jit(solution)/shard_map/ppermute | solution.py:407
  56.9 15.9 %collective-permute-start.17 = (bf16[4,256,256]{2,1,0:T(8,128)(2,1)S(1)}, bf16[4,256,256]{2,1,0:T(8,128)(2,1)S(1)}, u32[]{:S(2)}, u32[]{:S(2)}) collective-permute-start(bf16[4,256,256]{2,1,0:T(8,128)(2,1)S(1)} %get-tuple-element.58), channel_id=1, source_target_pairs={{0,4},{4,0},{8,12},{12,8},{16,20},{20,16},{24,28},{28,24},{1,5},{5... | collective-permute-start | bytes 1572872 | tf_op jit(solution)/shard_map/ppermute | solution.py:352
  58.5 11.4 %collective-permute-start.18 = (bf16[2,512,128]{2,1,0:T(8,128)(2,1)S(1)}, bf16[2,512,128]{2,1,0:T(8,128)(2,1)S(1)}, u32[]{:S(2)}, u32[]{:S(2)}) collective-permute-start(bf16[2,512,128]{2,1,0:T(8,128)(2,1)S(1)} %get-tuple-element.59), channel_id=1, source_target_pairs={{0,8},{4,12},{8,0},{12,4},{16,24},{20,28},{24,16},{28,20},{1,9},{5... | collective-permute-start | bytes 786440 | tf_op jit(solution)/shard_map/ppermute | solution.py:344
  60.0 12.8 %collective-permute-start.19 = (bf16[2,512,128]{2,1,0:T(8,128)(2,1)S(1)}, bf16[2,512,128]{2,1,0:T(8,128)(2,1)S(1)}, u32[]{:S(2)}, u32[]{:S(2)}) collective-permute-start(bf16[2,512,128]{2,1,0:T(8,128)(2,1)S(1)} %get-tuple-element.60), channel_id=1, source_target_pairs={{0,16},{4,20},{8,24},{12,28},{16,0},{20,4},{24,8},{28,12},{1,17},{... | collective-permute-start | bytes 786440 | tf_op jit(solution)/shard_map/ppermute | solution.py:344
  62.2 13.6 %collective-permute-start.10 = (bf16[256,1024]{1,0:T(8,128)(2,1)S(1)}, bf16[256,1024]{1,0:T(8,128)(2,1)S(1)}, u32[]{:S(2)}, u32[]{:S(2)}) collective-permute-start(bf16[256,1024]{1,0:T(8,128)(2,1)S(1)} %collective-permute-done.8.refs_0_.refs_2_), channel_id=1, source_target_pairs={{0,2},{1,3},{2,0},{3,1},{4,6},{5,7},{6,4},{7,5},{8,10},{9,11},{10,... | collective-permute-start | bytes 1572872 | tf_op jit(solution)/shard_map/ppermute | solution.py:355
  72.9 13.2 %collective-permute-start.20 = (bf16[4,256,256]{2,1,0:T(8,128)(2,1)S(1)}, bf16[4,256,256]{2,1,0:T(8,128)(2,1)S(1)}, u32[]{:S(2)}, u32[]{:S(2)}) collective-permute-start(bf16[4,256,256]{2,1,0:T(8,128)(2,1)S(1)} %sum.1.refs_5_), channel_id=1, source_target_pairs={{0,8},{4,12},{8,0},{12,4},{16,24},{20,28},{24,16},{28,20},{1,9},{5... | collective-permute-start | bytes 1572872 | tf_op jit(solution)/shard_map/ppermute | solution.py:344
  73.0 15.4 %collective-permute-start.25 = (bf16[4,256,256]{2,1,0:T(8,128)(2,1)S(1)}, bf16[4,256,256]{2,1,0:T(8,128)(2,1)S(1)}, u32[]{:S(2)}, u32[]{:S(2)}) collective-permute-start(bf16[4,256,256]{2,1,0:T(8,128)(2,1)S(1)} %sum.1.refs_5_), channel_id=1, source_target_pairs={{8,16},{12,20},{16,8},{20,12},{9,17},{13,21},{17,9},{21,13},{10,18... | collective-permute-start | bytes 1572872 | tf_op jit(solution)/shard_map/ppermute | solution.py:347
  75.7 15.3 %collective-permute-start.9 = (bf16[256,1024]{1,0:T(8,128)(2,1)S(1)}, bf16[256,1024]{1,0:T(8,128)(2,1)S(1)}, u32[]{:S(2)}, u32[]{:S(2)}) collective-permute-start(bf16[256,1024]{1,0:T(8,128)(2,1)S(1)} %collective-permute-done.8.refs_0_.refs_2_), channel_id=1, source_target_pairs={{0,1},{1,0},{2,3},{3,2},{4,5},{5,4},{6,7},{7,6},{8,9},{9,8},{10,11... | collective-permute-start | bytes 1572872 | tf_op jit(solution)/shard_map/ppermute | solution.py:355
  75.8 15.2 %collective-permute-start.11 = (bf16[256,1024]{1,0:T(8,128)(2,1)S(1)}, bf16[256,1024]{1,0:T(8,128)(2,1)S(1)}, u32[]{:S(2)}, u32[]{:S(2)}) collective-permute-start(bf16[256,1024]{1,0:T(8,128)(2,1)S(1)} %collective-permute-done.10.refs_2_), channel_id=1, source_target_pairs={{0,1},{1,0},{2,3},{3,2},{4,5},{5,4},{6,7},{7,6},{8,9},{9,8},{10,11... | collective-permute-start | bytes 1572872 | tf_op jit(solution)/shard_map/ppermute | solution.py:355
  86.1 14.1 %collective-permute-start.22 = (bf16[4,256,256]{2,1,0:T(8,128)(2,1)S(1)}, bf16[4,256,256]{2,1,0:T(8,128)(2,1)S(1)}, u32[]{:S(2)}, u32[]{:S(2)}) collective-permute-start(bf16[4,256,256]{2,1,0:T(8,128)(2,1)S(1)} %collective-permute-done.20.refs_1_.refs_5_), channel_id=1, source_target_pairs={{8,16},{12,20},{16,8},{20,12},{9,17},{13,21},{17,9},{21,13},{10,18... | collective-permute-start | bytes 1572872 | tf_op jit(solution)/shard_map/ppermute | solution.py:347
  88.4 17.1 %collective-permute-start.26 = (bf16[4,256,256]{2,1,0:T(8,128)(2,1)S(1)}, bf16[4,256,256]{2,1,0:T(8,128)(2,1)S(1)}, u32[]{:S(2)}, u32[]{:S(2)}) collective-permute-start(bf16[4,256,256]{2,1,0:T(8,128)(2,1)S(1)} %collective-permute-done.25.refs_5_), channel_id=1, source_target_pairs={{16,24},{20,28},{8,0},{12,4},{17,25},{21,29},{9,1},{13,5},{18,26},... | collective-permute-start | bytes 1572872 | tf_op jit(solution)/shard_map/ppermute | solution.py:347
  89.7 13.6 %collective-permute-start.21 = (bf16[2,528,128]{2,1,0:T(8,128)(2,1)S(1)}, bf16[2,528,128]{2,1,0:T(8,128)(2,1)S(1)}, u32[]{:S(2)}, u32[]{:S(2)}) collective-permute-start(bf16[2,528,128]{2,1,0:T(8,128)(2,1)S(1)} %gate.7), channel_id=1, source_target_pairs={{0,8},{4,12},{24,16},{28,20},{1,9},{5,13},{25,17},{29,21},{2,10},{... | collective-permute-start | bytes 811016 | tf_op jit(solution)/shard_map/ppermute | solution.py:347
  92.9 12.6 %collective-permute-start.24 = (bf16[512,256]{1,0:T(8,128)(2,1)S(1)}, bf16[512,256]{1,0:T(8,128)(2,1)S(1)}, u32[]{:S(2)}, u32[]{:S(2)}) collective-permute-start(bf16[512,256]{1,0:T(8,128)(2,1)S(1)} %get-tuple-element.64), channel_id=1, source_target_pairs={{0,4},{4,0},{8,12},{12,8},{16,20},{20,16},{24,28},{28,24},{1,5},{5... | collective-permute-start | bytes 786440 | tf_op jit(solution)/shard_map/ppermute | solution.py:352
  100.1 14.9 %collective-permute-start.27 = (bf16[4,256,256]{2,1,0:T(8,128)(2,1)S(1)}, bf16[4,256,256]{2,1,0:T(8,128)(2,1)S(1)}, u32[]{:S(2)}, u32[]{:S(2)}) collective-permute-start(bf16[4,256,256]{2,1,0:T(8,128)(2,1)S(1)} %collective-permute-done.22.refs_2_.refs_5_), channel_id=1, source_target_pairs={{16,24},{20,28},{8,0},{12,4},{17,25},{21,29},{9,1},{13,5},{18,26},... | collective-permute-start | bytes 1572872 | tf_op jit(solution)/shard_map/ppermute | solution.py:347
  102.7 14.3 %collective-permute-start.31 = (bf16[512,256]{1,0:T(8,128)(2,1)S(1)}, bf16[512,256]{1,0:T(8,128)(2,1)S(1)}, u32[]{:S(2)}, u32[]{:S(2)}) collective-permute-start(bf16[512,256]{1,0:T(8,128)(2,1)S(1)} %get-tuple-element.70), channel_id=1, source_target_pairs={{0,4},{4,0},{8,12},{12,8},{16,20},{20,16},{24,28},{28,24},{1,5},{5... | collective-permute-start | bytes 786440 | tf_op jit(solution)/shard_map/ppermute | solution.py:352
  103.3 10.4 %collective-permute-start.23 = (bf16[2,528,128]{2,1,0:T(8,128)(2,1)S(1)}, bf16[2,528,128]{2,1,0:T(8,128)(2,1)S(1)}, u32[]{:S(2)}, u32[]{:S(2)}) collective-permute-start(bf16[2,528,128]{2,1,0:T(8,128)(2,1)S(1)} %get-tuple-element.63), channel_id=1, source_target_pairs={{8,16},{12,20},{16,8},{20,12},{9,17},{13,21},{17,9},{21,13},{10,18... | collective-permute-start | bytes 811016 | tf_op jit(solution)/shard_map/ppermute | solution.py:347
  106.8 10.3 %collective-permute-start.32 = (bf16[512,256]{1,0:T(8,128)(2,1)S(1)}, bf16[512,256]{1,0:T(8,128)(2,1)S(1)}, u32[]{:S(2)}, u32[]{:S(2)}) collective-permute-start(bf16[512,256]{1,0:T(8,128)(2,1)S(1)} %get-tuple-element.71), channel_id=1, source_target_pairs={{0,4},{4,0},{8,12},{12,8},{16,20},{20,16},{24,28},{28,24},{1,5},{5... | collective-permute-start | bytes 786440 | tf_op jit(solution)/shard_map/ppermute | solution.py:352
  110.0 10.2 %collective-permute-start.29 = (bf16[2,512,128]{2,1,0:T(8,128)(2,1)S(1)}, bf16[2,512,128]{2,1,0:T(8,128)(2,1)S(1)}, u32[]{:S(2)}, u32[]{:S(2)}) collective-permute-start(bf16[2,512,128]{2,1,0:T(8,128)(2,1)S(1)} %get-tuple-element.66), channel_id=1, source_target_pairs={{8,16},{12,20},{16,8},{20,12},{9,17},{13,21},{17,9},{21,13},{10,18... | collective-permute-start | bytes 786440 | tf_op jit(solution)/shard_map/ppermute | solution.py:347
  113.7 6.5 %collective-permute-start.30 = (bf16[2,528,128]{2,1,0:T(8,128)(2,1)S(1)}, bf16[2,528,128]{2,1,0:T(8,128)(2,1)S(1)}, u32[]{:S(2)}, u32[]{:S(2)}) collective-permute-start(bf16[2,528,128]{2,1,0:T(8,128)(2,1)S(1)} %gate.9.refs_4_), channel_id=1, source_target_pairs={{16,24},{20,28},{8,0},{12,4},{17,25},{21,29},{9,1},{13,5},{18,26},... | collective-permute-start | bytes 811016 | tf_op jit(solution)/shard_map/ppermute | solution.py:347
  116.0 6.4 %collective-permute-start.28 = (bf16[512,256]{1,0:T(8,128)(2,1)S(1)}, bf16[512,256]{1,0:T(8,128)(2,1)S(1)}, u32[]{:S(2)}, u32[]{:S(2)}) collective-permute-start(bf16[512,256]{1,0:T(8,128)(2,1)S(1)} %weigh.8.refs_4_), channel_id=1, source_target_pairs={{0,4},{4,0},{8,12},{12,8},{16,20},{20,16},{24,28},{28,24},{1,5},{5... | collective-permute-start | bytes 786440 | tf_op jit(solution)/shard_map/ppermute | solution.py:352

commit v5 on v1

--- a/solution.py
+++ b/solution.py
@@ -28,13 +28,14 @@
     return pl.ds(pl.multiple_of(head * HEAD, HEAD), HEAD)
 
 
-def pack_kernel(chain, slots, place, owner, store_row, queries, out_grad, store, gain, *refs):
+def pack_kernel(chain, slots, owner, store_row, queries, out_grad, store, gain, *refs):
     packed, (bundle, sems, sem) = refs[:chain], refs[chain:]
     tokens, rows = queries.shape[0], store.shape[0]
     named, spans = owner.shape
+    member = lax.axis_index("dp") // 2
     copies = [pltpu.make_async_copy(store, bundle.at[pl.ds(0, rows), :], sem)] + [
         pltpu.make_async_copy(
-            source.at[:, column(place[0] ^ r)],
+            source.at[:, column(member ^ r)],
             packed[r].at[pl.ds(side * tokens, tokens), :],
             sems.at[r, side],
         )
@@ -357,14 +358,13 @@
             jax.ShapeDtypeStruct((2 * tokens + spans * neighbours_per, HEAD), queries.dtype)
         ] * chain
         + [jax.ShapeDtypeStruct((rows + TILE, width), store.dtype)],
-        in_specs=[SMEM] * 3 + [HBM] * 3 + [VMEM],
+        in_specs=[SMEM] * 2 + [HBM] * 3 + [VMEM],
         out_specs=[VMEM] * (chain + 1),
         scratch_shapes=[pltpu.SemaphoreType.DMA((chain, 2)), pltpu.SemaphoreType.DMA],
         compiler_params=params(8),
         cost_estimate=estimate(1),
         name="pack",
     )(
-        place,
         held(owner.T),
         held(store_row.T),
         held(queries),

time: 124 us -> 124 us (level)
  no operation moved by 1% of the time
where the time goes in v5:
time: 124 us; the launch traced here: 123 us
  waiting for transfers between devices  53.1 us (43%)
  starting transfers between devices  39.8 us (32%)
  Pallas kernels  28.8 us (23%)
    ppermute x9, waiting for transfers between devices, along(): return lax.ppermute(x, 'dp', [(i, i ^ 2 * r) for i in range(peers)])  40.7 us
    ppermute x8, starting transfers between devices, hop(): lax.ppermute(x, 'dp', [(2 * i + y, 2 * j + y) for i, j in pairs for y in...  15.9 us
    ppermute x9, starting transfers between devices, across(): return lax.ppermute(x, 'dp', [(i, i ^ 1) for i in range(peers)])  11 us
    ppermute x9, starting transfers between devices, along(): return lax.ppermute(x, 'dp', [(i, i ^ 2 * r) for i in range(peers)])  9.83 us
    pallas_call x1, Pallas kernels, chained(): pl.pallas_call(functools.partial(attend_kernel, chain, spans, stored, len...  7.83 us
    pallas_call x1, Pallas kernels, chained(): pl.pallas_call(functools.partial(project_kernel, chain, features), out_sh...  7.09 us
    ppermute x8, waiting for transfers between devices, hop(): lax.ppermute(x, 'dp', [(2 * i + y, 2 * j + y) for i, j in pairs for y in...  6.89 us
    pallas_call x5, Pallas kernels, weigh(): pl.pallas_call(functools.partial(weigh_kernel, chain, wants), out_shape=[...  5.8 us
  transfers between devices with their start and end apart: 33, of which 13 were waited for; matrix products, arithmetic and copies ran while one was open for 0% of the time, Pallas kernels for 21%

profile of v5, /device:TPU:10, one launch (start us, length us, event | category | flops | bytes accessed | tf_op | source)
XLA Modules:
  0.0 122.7 jit_solution(3044625511400849657)
XLA Ops:
  0.6 2.2 %pack.1 = (bf16[1040,128]{1,0:T(8,128)(2,1)S(1)}, bf16[1040,128]{1,0:T(8,128)(2,1)S(1)}, bf16[1040,128]{1,0:T(8,128)(2,1)S(1)}, bf16[1040,128]{1,0:T(8,128)(2,1)S(1)}, bf16[272,1024]{1,0:T(8,128)(2,1)S(1)}) custom-call(s32[2,8]{1,0:T(2,128)} %bitcast.7, s32[2,8]{1,0:T(2,128)} %bitcast.8, bf16[512,512]{1,0:T(8,128)(2,1)} %queries.1, ...), custom_call_target="tpu_custom_call" | custom-call | flops 1000000000 | bytes 3500000 | tf_op jit(solution)/shard_map/pack/pallas_call | solution.py:355
  2.8 0.6 collective-permute-start.1
  3.4 0.0 collective-permute-start.2
  3.4 3.0 %collective-permute-start.3 = (bf16[1040,128]{1,0:T(8,128)(2,1)S(1)}, bf16[1040,128]{1,0:T(8,128)(2,1)S(1)}, u32[]{:S(2)}, u32[]{:S(2)}) collective-permute-start(bf16[1040,128]{1,0:T(8,128)(2,1)S(1)} %get-tuple-element.42), channel_id=1, source_target_pairs={{0,16},{4,20},{8,24},{12,28},{16,0},{20,4},{24,8},{28,12},{1,17},{... | collective-permute-start | bytes 798728 | tf_op jit(solution)/shard_map/ppermute | solution.py:342
  6.4 8.2 %collective-permute-done.2.refs_2_.refs_1_ = bf16[1040,128]{1,0:T(8,128)(2,1)S(1)} collective-permute-done((bf16[1040,128]{1,0:T(8,128)(2,1)S(1)}, bf16[1040,128]{1,0:T(8,128)(2,1)S(1)}, u32[]{:S(2)}, u32[]{:S(2)}) %collective-permute-start.2) | collective-permute-done | bytes 266272 | tf_op jit(solution)/shard_map/ppermute | solution.py:342
  14.7 3.4 %collective-permute-done.3.refs_3_.refs_2_ = bf16[1040,128]{1,0:T(8,128)(2,1)S(1)} collective-permute-done((bf16[1040,128]{1,0:T(8,128)(2,1)S(1)}, bf16[1040,128]{1,0:T(8,128)(2,1)S(1)}, u32[]{:S(2)}, u32[]{:S(2)}) %collective-permute-start.3) | collective-permute-done | bytes 266272 | tf_op jit(solution)/shard_map/ppermute | solution.py:342
  18.1 0.0 collective-permute-start.4
  18.1 0.1 pad_add_fusion.place.refs_4_
  18.2 0.7 collective-permute-start.12
  18.9 0.0 collective-permute-done.refs_1_
  18.9 1.1 collective-permute-done.4.refs_3_
  20.0 7.1 %project.1 = (bf16[256,256]{1,0:T(8,128)(2,1)S(1)}, bf16[256,256]{1,0:T(8,128)(2,1)S(1)}, bf16[256,256]{1,0:T(8,128)(2,1)S(1)}, bf16[256,256]{1,0:T(8,128)(2,1)S(1)}, bf16[256,1024]{1,0:T(8,128)(2,1)S(1)}) custom-call(s32[3]{0:T(128)S(1)} %pad_add_fusion.place.refs_4_, bf16[4096,512]{1,0:T(8,128)(2,1)} %w_key.1, bf16[4096,512]{1,0:T(8,128)(2,1)} %w_value.1, ...), custom_call_target="tpu_custom_call" | custom-call | flops 6000000000 | bytes 21000000 | tf_op jit(solution)/shard_map/project/pallas_call | solution.py:384
  27.1 2.2 %collective-permute-start.5 = (bf16[256,256]{1,0:T(8,128)(2,1)S(1)}, bf16[256,256]{1,0:T(8,128)(2,1)S(1)}, u32[]{:S(2)}, u32[]{:S(2)}) collective-permute-start(bf16[256,256]{1,0:T(8,128)(2,1)S(1)} %get-tuple-element.46), channel_id=1, source_target_pairs={{0,8},{4,12},{8,0},{12,4},{16,24},{20,28},{24,16},{28,20},{1,9},{5... | collective-permute-start | bytes 393224 | tf_op jit(solution)/shard_map/ppermute | solution.py:342
  29.4 0.5 collective-permute-start.6
  29.9 1.1 collective-permute-start.7
  30.9 1.5 %collective-permute-start.13 = (bf16[256,256]{1,0:T(8,128)(2,1)S(1)}, bf16[256,256]{1,0:T(8,128)(2,1)S(1)}, u32[]{:S(2)}, u32[]{:S(2)}) collective-permute-start(bf16[256,256]{1,0:T(8,128)(2,1)S(1)} %get-tuple-element.45.refs_1_.refs_4_), channel_id=1, source_target_pairs={{0,4},{4,0},{8,12},{12,8},{16,20},{20,16},{24,28},{28,24},{1,5},{5... | collective-permute-start | bytes 393224 | tf_op jit(solution)/shard_map/ppermute | solution.py:350
  32.5 1.2 collective-permute-done.5.refs_2_.refs_5_
  33.7 1.5 %collective-permute-start.14 = (bf16[256,256]{1,0:T(8,128)(2,1)S(1)}, bf16[256,256]{1,0:T(8,128)(2,1)S(1)}, u32[]{:S(2)}, u32[]{:S(2)}) collective-permute-start(bf16[256,256]{1,0:T(8,128)(2,1)S(1)} %collective-permute-done.5.refs_2_.refs_5_), channel_id=1, source_target_pairs={{0,4},{4,0},{8,12},{12,8},{16,20},{20,16},{24,28},{28,24},{1,5},{5... | collective-permute-start | bytes 393224 | tf_op jit(solution)/shard_map/ppermute | solution.py:350
  35.2 4.6 %collective-permute-done.6.refs_3_.refs_6_ = bf16[256,256]{1,0:T(8,128)(2,1)S(1)} collective-permute-done((bf16[256,256]{1,0:T(8,128)(2,1)S(1)}, bf16[256,256]{1,0:T(8,128)(2,1)S(1)}, u32[]{:S(2)}, u32[]{:S(2)}) %collective-permute-start.6) | collective-permute-done | bytes 131104 | tf_op jit(solution)/shard_map/ppermute | solution.py:342
  39.7 1.5 %collective-permute-start.15 = (bf16[256,256]{1,0:T(8,128)(2,1)S(1)}, bf16[256,256]{1,0:T(8,128)(2,1)S(1)}, u32[]{:S(2)}, u32[]{:S(2)}) collective-permute-start(bf16[256,256]{1,0:T(8,128)(2,1)S(1)} %collective-permute-done.6.refs_3_.refs_6_), channel_id=1, source_target_pairs={{0,4},{4,0},{8,12},{12,8},{16,20},{20,16},{24,28},{28,24},{1,5},{5... | collective-permute-start | bytes 393224 | tf_op jit(solution)/shard_map/ppermute | solution.py:350
  41.3 2.7 %collective-permute-done.7.refs_4_.refs_7_ = bf16[256,256]{1,0:T(8,128)(2,1)S(1)} collective-permute-done((bf16[256,256]{1,0:T(8,128)(2,1)S(1)}, bf16[256,256]{1,0:T(8,128)(2,1)S(1)}, u32[]{:S(2)}, u32[]{:S(2)}) %collective-permute-start.7) | collective-permute-done | bytes 131104 | tf_op jit(solution)/shard_map/ppermute | solution.py:342
  43.9 1.5 %collective-permute-start.16 = (bf16[256,256]{1,0:T(8,128)(2,1)S(1)}, bf16[256,256]{1,0:T(8,128)(2,1)S(1)}, u32[]{:S(2)}, u32[]{:S(2)}) collective-permute-start(bf16[256,256]{1,0:T(8,128)(2,1)S(1)} %collective-permute-done.7.refs_4_.refs_7_), channel_id=1, source_target_pairs={{0,4},{4,0},{8,12},{12,8},{16,20},{20,16},{24,28},{28,24},{1,5},{5... | collective-permute-start | bytes 393224 | tf_op jit(solution)/shard_map/ppermute | solution.py:350
  45.4 1.9 %collective-permute-start.8 = (bf16[256,1024]{1,0:T(8,128)(2,1)S(1)}, bf16[256,1024]{1,0:T(8,128)(2,1)S(1)}, u32[]{:S(2)}, u32[]{:S(2)}) collective-permute-start(bf16[256,1024]{1,0:T(8,128)(2,1)S(1)} %gate.6), channel_id=1, source_target_pairs={{0,0},{1,25},{2,10},{3,19},{4,4},{5,29},{6,14},{7,23},{8,8},{9,17}... | collective-permute-start | bytes 1572872 | tf_op jit(solution)/shard_map/ppermute | solution.py:404
  47.4 0.0 collective-permute-done.13.refs_8_
  47.4 0.0 collective-permute-done.14.refs_9_
  47.4 1.7 %collective-permute-done.16.refs_11_ = bf16[256,256]{1,0:T(8,128)(2,1)S(1)} collective-permute-done((bf16[256,256]{1,0:T(8,128)(2,1)S(1)}, bf16[256,256]{1,0:T(8,128)(2,1)S(1)}, u32[]{:S(2)}, u32[]{:S(2)}) %collective-permute-start.16) | collective-permute-done | bytes 131104 | tf_op jit(solution)/shard_map/ppermute | solution.py:350
  49.0 7.8 %attend.1 = (bf16[2,512,128]{2,1,0:T(8,128)(2,1)S(1)}, bf16[2,512,128]{2,1,0:T(8,128)(2,1)S(1)}, bf16[2,512,128]{2,1,0:T(8,128)(2,1)S(1)}, bf16[2,512,128]{2,1,0...) custom-call(s32[3]{0:T(128)S(1)} %pad_add_fusion.place.refs_4_, ...), custom_call_target="tpu_custom_call" | custom-call | flops 14000000000 | bytes 49000000 | tf_op jit(solution)/shard_map/attend/pallas_call | solution.py:415
  56.9 1.6 %collective-permute-start.17 = (bf16[4,256,256]{2,1,0:T(8,128)(2,1)S(1)}, bf16[4,256,256]{2,1,0:T(8,128)(2,1)S(1)}, u32[]{:S(2)}, u32[]{:S(2)}) collective-permute-start(bf16[4,256,256]{2,1,0:T(8,128)(2,1)S(1)} %get-tuple-element.56), channel_id=1, source_target_pairs={{0,4},{4,0},{8,12},{12,8},{16,20},{20,16},{24,28},{28,24},{1,5},{5... | collective-permute-start | bytes 1572872 | tf_op jit(solution)/shard_map/ppermute | solution.py:350
  58.5 1.5 %collective-permute-start.18 = (bf16[2,512,128]{2,1,0:T(8,128)(2,1)S(1)}, bf16[2,512,128]{2,1,0:T(8,128)(2,1)S(1)}, u32[]{:S(2)}, u32[]{:S(2)}) collective-permute-start(bf16[2,512,128]{2,1,0:T(8,128)(2,1)S(1)} %get-tuple-element.57), channel_id=1, source_target_pairs={{0,8},{4,12},{8,0},{12,4},{16,24},{20,28},{24,16},{28,20},{1,9},{5... | collective-permute-start | bytes 786440 | tf_op jit(solution)/shard_map/ppermute | solution.py:342
  59.9 0.7 collective-permute-start.19
  60.7 1.3 %collective-permute-done.8.refs_0_.refs_2_ = bf16[256,1024]{1,0:T(8,128)(2,1)S(1)} collective-permute-done((bf16[256,1024]{1,0:T(8,128)(2,1)S(1)}, bf16[256,1024]{1,0:T(8,128)(2,1)S(1)}, u32[]{:S(2)}, u32[]{:S(2)}) %collective-permute-start.8) | collective-permute-done | bytes 524320 | tf_op jit(solution)/shard_map/ppermute | solution.py:404
  61.9 0.0 collective-permute-start.10
  61.9 7.9 %collective-permute-done.18.refs_0_.refs_1_ = bf16[2,512,128]{2,1,0:T(8,128)(2,1)S(1)} collective-permute-done((bf16[2,512,128]{2,1,0:T(8,128)(2,1)S(1)}, bf16[2,512,128]{2,1,0:T(8,128)(2,1)S(1)}, u32[]{:S(2)}, u32[]{:S(2)}) %collective-permute-start.18) | collective-permute-done | bytes 262176 | tf_op jit(solution)/shard_map/ppermute | solution.py:342
  69.8 2.9 %collective-permute-done.19.refs_1_.refs_2_ = bf16[2,512,128]{2,1,0:T(8,128)(2,1)S(1)} collective-permute-done((bf16[2,512,128]{2,1,0:T(8,128)(2,1)S(1)}, bf16[2,512,128]{2,1,0:T(8,128)(2,1)S(1)}, u32[]{:S(2)}, u32[]{:S(2)}) %collective-permute-start.19) | collective-permute-done | bytes 262176 | tf_op jit(solution)/shard_map/ppermute | solution.py:342
  72.7 0.0 collective-permute-done.17.received
  72.7 0.1 sum.1.refs_5_
  72.8 0.1 collective-permute-start.20
  72.9 2.7 %collective-permute-start.30 = (bf16[4,256,256]{2,1,0:T(8,128)(2,1)S(1)}, bf16[4,256,256]{2,1,0:T(8,128)(2,1)S(1)}, u32[]{:S(2)}, u32[]{:S(2)}) collective-permute-start(bf16[4,256,256]{2,1,0:T(8,128)(2,1)S(1)} %sum.1.refs_5_), channel_id=1, source_target_pairs={{8,16},{12,20},{16,8},{20,12},{9,17},{13,21},{17,9},{21,13},{10,18... | collective-permute-start | bytes 1572872 | tf_op jit(solution)/shard_map/ppermute | solution.py:345
  75.7 0.1 collective-permute-start.9
  75.8 0.0 collective-permute-done.10.refs_2_
  75.8 0.5 collective-permute-start.11
  76.3 9.8 %collective-permute-done.20.refs_5_.refs_1_ = bf16[4,256,256]{2,1,0:T(8,128)(2,1)S(1)} collective-permute-done((bf16[4,256,256]{2,1,0:T(8,128)(2,1)S(1)}, bf16[4,256,256]{2,1,0:T(8,128)(2,1)S(1)}, u32[]{:S(2)}, u32[]{:S(2)}) %collective-permute-start.20) | collective-permute-done | bytes 524320 | tf_op jit(solution)/shard_map/ppermute | solution.py:342
  86.1 2.2 %collective-permute-start.22 = (bf16[4,256,256]{2,1,0:T(8,128)(2,1)S(1)}, bf16[4,256,256]{2,1,0:T(8,128)(2,1)S(1)}, u32[]{:S(2)}, u32[]{:S(2)}) collective-permute-start(bf16[4,256,256]{2,1,0:T(8,128)(2,1)S(1)} %collective-permute-done.20.refs_5_.refs_1_), channel_id=1, source_target_pairs={{8,16},{12,20},{16,8},{20,12},{9,17},{13,21},{17,9},{21,13},{10,18... | collective-permute-start | bytes 1572872 | tf_op jit(solution)/shard_map/ppermute | solution.py:345
  88.3 1.3 %collective-permute-start.31 = (bf16[4,256,256]{2,1,0:T(8,128)(2,1)S(1)}, bf16[4,256,256]{2,1,0:T(8,128)(2,1)S(1)}, u32[]{:S(2)}, u32[]{:S(2)}) collective-permute-start(bf16[4,256,256]{2,1,0:T(8,128)(2,1)S(1)} %collective-permute-done.30.refs_5_), channel_id=1, source_target_pairs={{16,24},{20,28},{8,0},{12,4},{17,25},{21,29},{9,1},{13,5},{18,26},... | collective-permute-start | bytes 1572872 | tf_op jit(solution)/shard_map/ppermute | solution.py:345
  89.6 1.3 %collective-permute-start.25 = (bf16[2,512,128]{2,1,0:T(8,128)(2,1)S(1)}, bf16[2,512,128]{2,1,0:T(8,128)(2,1)S(1)}, u32[]{:S(2)}, u32[]{:S(2)}) collective-permute-start(bf16[2,512,128]{2,1,0:T(8,128)(2,1)S(1)} %gate.7), channel_id=1, source_target_pairs={{0,8},{4,12},{24,16},{28,20},{1,9},{5,13},{25,17},{29,21},{2,10},{... | collective-permute-start | bytes 786440 | tf_op jit(solution)/shard_map/ppermute | solution.py:345
  90.9 0.6 turn.1
  91.5 1.3 %weigh.5 = (f32[512,256]{1,0:T(8,128)S(1)}, bf16[512,256]{1,0:T(8,128)(2,1)S(1)}) custom-call(s32[3]{0:T(128)S(1)} %pad_add_fusion.place.refs_4_, bf16[2,512,256]{2,1,0:T(8,128)(2,1)S(1)} %get-tuple-element.49.refs_0_, bf16[2,512,256]{2,1,0:T(8,128)(2,1)S(1)} %get-tuple-element.50.refs_1_, bf16[2,512,256]{2,1,0:T(8,128)(2,1)S(1)} %get-tuple-element.51.refs_2_, ...), custom_call_target="tpu_custom_call" | custom-call | flops 2000000000 | bytes 7000000 | tf_op jit(solution)/shard_map/weigh/pallas_call | solution.py:477
  92.8 0.6 collective-permute-start.29
  93.4 6.9 %collective-permute-done.22.refs_5_.refs_2_ = bf16[4,256,256]{2,1,0:T(8,128)(2,1)S(1)} collective-permute-done((bf16[4,256,256]{2,1,0:T(8,128)(2,1)S(1)}, bf16[4,256,256]{2,1,0:T(8,128)(2,1)S(1)}, u32[]{:S(2)}, u32[]{:S(2)}) %collective-permute-start.22) | collective-permute-done | bytes 524320 | tf_op jit(solution)/shard_map/ppermute | solution.py:345
  100.2 1.3 %collective-permute-start.23 = (bf16[4,256,256]{2,1,0:T(8,128)(2,1)S(1)}, bf16[4,256,256]{2,1,0:T(8,128)(2,1)S(1)}, u32[]{:S(2)}, u32[]{:S(2)}) collective-permute-start(bf16[4,256,256]{2,1,0:T(8,128)(2,1)S(1)} %collective-permute-done.22.refs_5_.refs_2_), channel_id=1, source_target_pairs={{16,24},{20,28},{8,0},{12,4},{17,25},{21,29},{9,1},{13,5},{18,26},... | collective-permute-start | bytes 1572872 | tf_op jit(solution)/shard_map/ppermute | solution.py:345
  101.6 1.3 %weigh.6 = (f32[512,256]{1,0:T(8,128)S(1)}, bf16[512,256]{1,0:T(8,128)(2,1)S(1)}) custom-call(s32[3]{0:T(128)S(1)} %pad_add_fusion.place.refs_4_, bf16[2,512,256]{2,1,0:T(8,128)(2,1)S(1)} %get-tuple-element.49.refs_0_, bf16[2,512,256]{2,1,0:T(8,128)(2,1)S(1)} %get-tuple-element.50.refs_1_, bf16[2,512,256]{2,1,0:T(8,128)(2,1)S(1)} %get-tuple-element.51.refs_2_, ...), custom_call_target="tpu_custom_call" | custom-call | flops 2000000000 | bytes 7000000 | tf_op jit(solution)/shard_map/weigh/pallas_call | solution.py:477
  102.8 0.6 collective-permute-start.21
  103.4 2.2 %collective-permute-start.27 = (bf16[2,512,128]{2,1,0:T(8,128)(2,1)S(1)}, bf16[2,512,128]{2,1,0:T(8,128)(2,1)S(1)}, u32[]{:S(2)}, u32[]{:S(2)}) collective-permute-start(bf16[2,512,128]{2,1,0:T(8,128)(2,1)S(1)} %get-tuple-element.65), channel_id=1, source_target_pairs={{8,16},{12,20},{16,8},{20,12},{9,17},{13,21},{17,9},{21,13},{10,18... | collective-permute-start | bytes 786440 | tf_op jit(solution)/shard_map/ppermute | solution.py:345
  105.6 1.3 %weigh.9 = (f32[512,256]{1,0:T(8,128)S(1)}, bf16[512,256]{1,0:T(8,128)(2,1)S(1)}) custom-call(s32[3]{0:T(128)S(1)} %pad_add_fusion.place.refs_4_, bf16[2,512,256]{2,1,0:T(8,128)(2,1)S(1)} %get-tuple-element.49.refs_0_, bf16[2,512,256]{2,1,0:T(8,128)(2,1)S(1)} %get-tuple-element.50.refs_1_, bf16[2,512,256]{2,1,0:T(8,128)(2,1)S(1)} %get-tuple-element.51.refs_2_, ...), custom_call_target="tpu_custom_call" | custom-call | flops 2000000000 | bytes 7000000 | tf_op jit(solution)/shard_map/weigh/pallas_call | solution.py:477
  106.9 1.6 %collective-permute-start.32 = (bf16[512,256]{1,0:T(8,128)(2,1)S(1)}, bf16[512,256]{1,0:T(8,128)(2,1)S(1)}, u32[]{:S(2)}, u32[]{:S(2)}) collective-permute-start(bf16[512,256]{1,0:T(8,128)(2,1)S(1)} %get-tuple-element.71), channel_id=1, source_target_pairs={{0,4},{4,0},{8,12},{12,8},{16,20},{20,16},{24,28},{28,24},{1,5},{5... | collective-permute-start | bytes 786440 | tf_op jit(solution)/shard_map/ppermute | solution.py:350
  108.5 1.6 %unpack.1 = (bf16[512,512]{1,0:T(8,128)(2,1)}, bf16[512,512]{1,0:T(8,128)(2,1)}) custom-call(s32[3]{0:T(128)S(1)} %pad_add_fusion.place.refs_4_, bf16[2,512,128]{2,1,0:T(8,128)(2,1)S(1)} %get-tuple-element.66.refs_0_, bf16[2,512,128]{2,1,0:T(8,128)(2,1)S(1)} %collective-permute-done.18.refs_0_.refs_1_, ...), custom_call_target="tpu_custom_call" | custom-call | flops 2000000000 | bytes 7000000 | tf_op jit(solution)/shard_map/unpack/pallas_call | solution.py:507
  110.1 3.6 %collective-permute-start.26 = (bf16[2,512,128]{2,1,0:T(8,128)(2,1)S(1)}, bf16[2,512,128]{2,1,0:T(8,128)(2,1)S(1)}, u32[]{:S(2)}, u32[]{:S(2)}) collective-permute-start(bf16[2,512,128]{2,1,0:T(8,128)(2,1)S(1)} %get-tuple-element.64), channel_id=1, source_target_pairs={{8,16},{12,20},{16,8},{20,12},{9,17},{13,21},{17,9},{21,13},{10,18... | collective-permute-start | bytes 786440 | tf_op jit(solution)/shard_map/ppermute | solution.py:345
  113.8 1.0 weigh.7.refs_4_.refs_1_
  114.8 0.6 collective-permute-start.24
  115.4 1.3 %collective-permute-start.28 = (bf16[2,512,128]{2,1,0:T(8,128)(2,1)S(1)}, bf16[2,512,128]{2,1,0:T(8,128)(2,1)S(1)}, u32[]{:S(2)}, u32[]{:S(2)}) collective-permute-start(bf16[2,512,128]{2,1,0:T(8,128)(2,1)S(1)} %gate.9), channel_id=1, source_target_pairs={{16,24},{20,28},{8,0},{12,4},{17,25},{21,29},{9,1},{13,5},{18,26},... | collective-permute-start | bytes 786440 | tf_op jit(solution)/shard_map/ppermute | solution.py:345
  116.7 2.1 %collect.1 = (f32[512,512]{1,0:T(8,128)}, f32[512,512]{1,0:T(8,128)}) custom-call(s32[3]{0:T(128)S(1)} %pad_add_fusion.place.refs_4_, f32[512,256]{1,0:T(8,128)S(1)} %get-tuple-element.59.refs_4_.refs_0_, f32[512,256]{1,0:T(8,128)S(1)} %get-tuple-element.63.refs_3_.refs_1_, f32[512,256]{1,0:T(8,128)S(1)} %get-tuple-element.70.refs_2_, ...), custom_call_target="tpu_custom_call" | custom-call | flops 2000000000 | bytes 7000000 | tf_op jit(solution)/shard_map/collect/pallas_call | solution.py:517
  118.8 1.0 weigh.8.kept
  119.8 1.4 %collective-permute-done.24.received = bf16[512,256]{1,0:T(8,128)(2,1)S(1)} collective-permute-done((bf16[512,256]{1,0:T(8,128)(2,1)S(1)}, bf16[512,256]{1,0:T(8,128)(2,1)S(1)}, u32[]{:S(2)}, u32[]{:S(2)}) %collective-permute-start.24) | collective-permute-done | bytes 262176 | tf_op jit(solution)/shard_map/ppermute | solution.py:350
  121.2 1.5 %finish.1 = (bf16[512,512]{1,0:T(8,128)(2,1)}, bf16[512,512]{1,0:T(8,128)(2,1)}, f32[512,512]{1,0:T(8,128)}, f32[512,512]{1,0:T(8,128)}) custom-call(s32[3]{0:T(128)S(1)} %pad_add_fusion.place.refs_4_, f32[512,256]{1,0:T(8,128)S(1)} %weigh.8.kept, ...), custom_call_target="tpu_custom_call", output_to_operand_aliasing={{0}: (5, {}), {1}: (6, {}), {2}: (7, {}), {3}: (8, {})} | custom-call | flops 1000000000 | bytes 3500000 | tf_op jit(solution)/shard_map/finish/pallas_call | solution.py:526
  (21 shorter events, 0.0 us)
Async XLA Ops:
  2.8 15.3 %collective-permute-start.1 = (bf16[272,1024]{1,0:T(8,128)(2,1)S(1)}, bf16[272,1024]{1,0:T(8,128)(2,1)S(1)}, u32[]{:S(2)}, u32[]{:S(2)}) collective-permute-start(bf16[272,1024]{1,0:T(8,128)(2,1)S(1)} %get-tuple-element.39.refs_0_), channel_id=1, source_target_pairs={{0,2},{1,3},{2,0},{3,1},{4,6},{5,7},{6,4},{7,5},{8,10},{9,11},{10,... | collective-permute-start | bytes 1671176 | tf_op jit(solution)/shard_map/ppermute | solution.py:353
  3.4 11.2 %collective-permute-start.2 = (bf16[1040,128]{1,0:T(8,128)(2,1)S(1)}, bf16[1040,128]{1,0:T(8,128)(2,1)S(1)}, u32[]{:S(2)}, u32[]{:S(2)}) collective-permute-start(bf16[1040,128]{1,0:T(8,128)(2,1)S(1)} %get-tuple-element.41), channel_id=1, source_target_pairs={{0,8},{4,12},{8,0},{12,4},{16,24},{20,28},{24,16},{28,20},{1,9},{5... | collective-permute-start | bytes 798728 | tf_op jit(solution)/shard_map/ppermute | solution.py:342
  3.4 14.7 %collective-permute-start.3 = (bf16[1040,128]{1,0:T(8,128)(2,1)S(1)}, bf16[1040,128]{1,0:T(8,128)(2,1)S(1)}, u32[]{:S(2)}, u32[]{:S(2)}) collective-permute-start(bf16[1040,128]{1,0:T(8,128)(2,1)S(1)} %get-tuple-element.42), channel_id=1, source_target_pairs={{0,16},{4,20},{8,24},{12,28},{16,0},{20,4},{24,8},{28,12},{1,17},{... | collective-permute-start | bytes 798728 | tf_op jit(solution)/shard_map/ppermute | solution.py:342
  6.4 12.5 %collective-permute-start = (bf16[272,1024]{1,0:T(8,128)(2,1)S(1)}, bf16[272,1024]{1,0:T(8,128)(2,1)S(1)}, u32[]{:S(2)}, u32[]{:S(2)}) collective-permute-start(bf16[272,1024]{1,0:T(8,128)(2,1)S(1)} %get-tuple-element.39.refs_0_), channel_id=1, source_target_pairs={{0,1},{1,0},{2,3},{3,2},{4,5},{5,4},{6,7},{7,6},{8,9},{9,8},{10,11... | collective-permute-start | bytes 1671176 | tf_op jit(solution)/shard_map/ppermute | solution.py:353
  18.1 2.0 %collective-permute-start.4 = (bf16[272,1024]{1,0:T(8,128)(2,1)S(1)}, bf16[272,1024]{1,0:T(8,128)(2,1)S(1)}, u32[]{:S(2)}, u32[]{:S(2)}) collective-permute-start(bf16[272,1024]{1,0:T(8,128)(2,1)S(1)} %get-tuple-element.43.refs_2_), channel_id=1, source_target_pairs={{0,1},{1,0},{2,3},{3,2},{4,5},{5,4},{6,7},{7,6},{8,9},{9,8},{10,11... | collective-permute-start | bytes 1671176 | tf_op jit(solution)/shard_map/ppermute | solution.py:353
  18.2 27.3 %collective-permute-start.12 = (bf16[1040,128]{1,0:T(8,128)(2,1)S(1)}, bf16[1040,128]{1,0:T(8,128)(2,1)S(1)}, u32[]{:S(2)}, u32[]{:S(2)}) collective-permute-start(bf16[1040,128]{1,0:T(8,128)(2,1)S(1)} %get-tuple-element.54), channel_id=1, source_target_pairs={{0,24},{4,28},{8,16},{12,20},{16,8},{20,12},{24,0},{28,4},{1,25},{... | collective-permute-start | bytes 798728 | tf_op jit(solution)/shard_map/ppermute | solution.py:342
  27.1 6.5 %collective-permute-start.5 = (bf16[256,256]{1,0:T(8,128)(2,1)S(1)}, bf16[256,256]{1,0:T(8,128)(2,1)S(1)}, u32[]{:S(2)}, u32[]{:S(2)}) collective-permute-start(bf16[256,256]{1,0:T(8,128)(2,1)S(1)} %get-tuple-element.46), channel_id=1, source_target_pairs={{0,8},{4,12},{8,0},{12,4},{16,24},{20,28},{24,16},{28,20},{1,9},{5... | collective-permute-start | bytes 393224 | tf_op jit(solution)/shard_map/ppermute | solution.py:342
  29.4 10.3 %collective-permute-start.6 = (bf16[256,256]{1,0:T(8,128)(2,1)S(1)}, bf16[256,256]{1,0:T(8,128)(2,1)S(1)}, u32[]{:S(2)}, u32[]{:S(2)}) collective-permute-start(bf16[256,256]{1,0:T(8,128)(2,1)S(1)} %get-tuple-element.47), channel_id=1, source_target_pairs={{0,16},{4,20},{8,24},{12,28},{16,0},{20,4},{24,8},{28,12},{1,17},{... | collective-permute-start | bytes 393224 | tf_op jit(solution)/shard_map/ppermute | solution.py:342
  29.9 14.0 %collective-permute-start.7 = (bf16[256,256]{1,0:T(8,128)(2,1)S(1)}, bf16[256,256]{1,0:T(8,128)(2,1)S(1)}, u32[]{:S(2)}, u32[]{:S(2)}) collective-permute-start(bf16[256,256]{1,0:T(8,128)(2,1)S(1)} %get-tuple-element.48), channel_id=1, source_target_pairs={{0,24},{4,28},{8,16},{12,20},{16,8},{20,12},{24,0},{28,4},{1,25},{... | collective-permute-start | bytes 393224 | tf_op jit(solution)/shard_map/ppermute | solution.py:342
  30.9 16.4 %collective-permute-start.13 = (bf16[256,256]{1,0:T(8,128)(2,1)S(1)}, bf16[256,256]{1,0:T(8,128)(2,1)S(1)}, u32[]{:S(2)}, u32[]{:S(2)}) collective-permute-start(bf16[256,256]{1,0:T(8,128)(2,1)S(1)} %get-tuple-element.45.refs_1_.refs_4_), channel_id=1, source_target_pairs={{0,4},{4,0},{8,12},{12,8},{16,20},{20,16},{24,28},{28,24},{1,5},{5... | collective-permute-start | bytes 393224 | tf_op jit(solution)/shard_map/ppermute | solution.py:350
  33.7 13.7 %collective-permute-start.14 = (bf16[256,256]{1,0:T(8,128)(2,1)S(1)}, bf16[256,256]{1,0:T(8,128)(2,1)S(1)}, u32[]{:S(2)}, u32[]{:S(2)}) collective-permute-start(bf16[256,256]{1,0:T(8,128)(2,1)S(1)} %collective-permute-done.5.refs_2_.refs_5_), channel_id=1, source_target_pairs={{0,4},{4,0},{8,12},{12,8},{16,20},{20,16},{24,28},{28,24},{1,5},{5... | collective-permute-start | bytes 393224 | tf_op jit(solution)/shard_map/ppermute | solution.py:350
  39.7 7.6 %collective-permute-start.15 = (bf16[256,256]{1,0:T(8,128)(2,1)S(1)}, bf16[256,256]{1,0:T(8,128)(2,1)S(1)}, u32[]{:S(2)}, u32[]{:S(2)}) collective-permute-start(bf16[256,256]{1,0:T(8,128)(2,1)S(1)} %collective-permute-done.6.refs_3_.refs_6_), channel_id=1, source_target_pairs={{0,4},{4,0},{8,12},{12,8},{16,20},{20,16},{24,28},{28,24},{1,5},{5... | collective-permute-start | bytes 393224 | tf_op jit(solution)/shard_map/ppermute | solution.py:350
  43.9 5.1 %collective-permute-start.16 = (bf16[256,256]{1,0:T(8,128)(2,1)S(1)}, bf16[256,256]{1,0:T(8,128)(2,1)S(1)}, u32[]{:S(2)}, u32[]{:S(2)}) collective-permute-start(bf16[256,256]{1,0:T(8,128)(2,1)S(1)} %collective-permute-done.7.refs_4_.refs_7_), channel_id=1, source_target_pairs={{0,4},{4,0},{8,12},{12,8},{16,20},{20,16},{24,28},{28,24},{1,5},{5... | collective-permute-start | bytes 393224 | tf_op jit(solution)/shard_map/ppermute | solution.py:350
  45.4 16.5 %collective-permute-start.8 = (bf16[256,1024]{1,0:T(8,128)(2,1)S(1)}, bf16[256,1024]{1,0:T(8,128)(2,1)S(1)}, u32[]{:S(2)}, u32[]{:S(2)}) collective-permute-start(bf16[256,1024]{1,0:T(8,128)(2,1)S(1)} %gate.6), channel_id=1, source_target_pairs={{0,0},{1,25},{2,10},{3,19},{4,4},{5,29},{6,14},{7,23},{8,8},{9,17}... | collective-permute-start | bytes 1572872 | tf_op jit(solution)/shard_map/ppermute | solution.py:404
  56.9 15.9 %collective-permute-start.17 = (bf16[4,256,256]{2,1,0:T(8,128)(2,1)S(1)}, bf16[4,256,256]{2,1,0:T(8,128)(2,1)S(1)}, u32[]{:S(2)}, u32[]{:S(2)}) collective-permute-start(bf16[4,256,256]{2,1,0:T(8,128)(2,1)S(1)} %get-tuple-element.56), channel_id=1, source_target_pairs={{0,4},{4,0},{8,12},{12,8},{16,20},{20,16},{24,28},{28,24},{1,5},{5... | collective-permute-start | bytes 1572872 | tf_op jit(solution)/shard_map/ppermute | solution.py:350
  58.5 11.3 %collective-permute-start.18 = (bf16[2,512,128]{2,1,0:T(8,128)(2,1)S(1)}, bf16[2,512,128]{2,1,0:T(8,128)(2,1)S(1)}, u32[]{:S(2)}, u32[]{:S(2)}) collective-permute-start(bf16[2,512,128]{2,1,0:T(8,128)(2,1)S(1)} %get-tuple-element.57), channel_id=1, source_target_pairs={{0,8},{4,12},{8,0},{12,4},{16,24},{20,28},{24,16},{28,20},{1,9},{5... | collective-permute-start | bytes 786440 | tf_op jit(solution)/shard_map/ppermute | solution.py:342
  59.9 12.8 %collective-permute-start.19 = (bf16[2,512,128]{2,1,0:T(8,128)(2,1)S(1)}, bf16[2,512,128]{2,1,0:T(8,128)(2,1)S(1)}, u32[]{:S(2)}, u32[]{:S(2)}) collective-permute-start(bf16[2,512,128]{2,1,0:T(8,128)(2,1)S(1)} %get-tuple-element.58), channel_id=1, source_target_pairs={{0,16},{4,20},{8,24},{12,28},{16,0},{20,4},{24,8},{28,12},{1,17},{... | collective-permute-start | bytes 786440 | tf_op jit(solution)/shard_map/ppermute | solution.py:342
  61.9 13.8 %collective-permute-start.10 = (bf16[256,1024]{1,0:T(8,128)(2,1)S(1)}, bf16[256,1024]{1,0:T(8,128)(2,1)S(1)}, u32[]{:S(2)}, u32[]{:S(2)}) collective-permute-start(bf16[256,1024]{1,0:T(8,128)(2,1)S(1)} %collective-permute-done.8.refs_0_.refs_2_), channel_id=1, source_target_pairs={{0,2},{1,3},{2,0},{3,1},{4,6},{5,7},{6,4},{7,5},{8,10},{9,11},{10,... | collective-permute-start | bytes 1572872 | tf_op jit(solution)/shard_map/ppermute | solution.py:353
  72.8 13.2 %collective-permute-start.20 = (bf16[4,256,256]{2,1,0:T(8,128)(2,1)S(1)}, bf16[4,256,256]{2,1,0:T(8,128)(2,1)S(1)}, u32[]{:S(2)}, u32[]{:S(2)}) collective-permute-start(bf16[4,256,256]{2,1,0:T(8,128)(2,1)S(1)} %sum.1.refs_5_), channel_id=1, source_target_pairs={{0,8},{4,12},{8,0},{12,4},{16,24},{20,28},{24,16},{28,20},{1,9},{5... | collective-permute-start | bytes 1572872 | tf_op jit(solution)/shard_map/ppermute | solution.py:342
  72.9 15.3 %collective-permute-start.30 = (bf16[4,256,256]{2,1,0:T(8,128)(2,1)S(1)}, bf16[4,256,256]{2,1,0:T(8,128)(2,1)S(1)}, u32[]{:S(2)}, u32[]{:S(2)}) collective-permute-start(bf16[4,256,256]{2,1,0:T(8,128)(2,1)S(1)} %sum.1.refs_5_), channel_id=1, source_target_pairs={{8,16},{12,20},{16,8},{20,12},{9,17},{13,21},{17,9},{21,13},{10,18... | collective-permute-start | bytes 1572872 | tf_op jit(solution)/shard_map/ppermute | solution.py:345
  75.7 15.2 %collective-permute-start.9 = (bf16[256,1024]{1,0:T(8,128)(2,1)S(1)}, bf16[256,1024]{1,0:T(8,128)(2,1)S(1)}, u32[]{:S(2)}, u32[]{:S(2)}) collective-permute-start(bf16[256,1024]{1,0:T(8,128)(2,1)S(1)} %collective-permute-done.8.refs_0_.refs_2_), channel_id=1, source_target_pairs={{0,1},{1,0},{2,3},{3,2},{4,5},{5,4},{6,7},{7,6},{8,9},{9,8},{10,11... | collective-permute-start | bytes 1572872 | tf_op jit(solution)/shard_map/ppermute | solution.py:353
  75.8 15.2 %collective-permute-start.11 = (bf16[256,1024]{1,0:T(8,128)(2,1)S(1)}, bf16[256,1024]{1,0:T(8,128)(2,1)S(1)}, u32[]{:S(2)}, u32[]{:S(2)}) collective-permute-start(bf16[256,1024]{1,0:T(8,128)(2,1)S(1)} %collective-permute-done.10.refs_2_), channel_id=1, source_target_pairs={{0,1},{1,0},{2,3},{3,2},{4,5},{5,4},{6,7},{7,6},{8,9},{9,8},{10,11... | collective-permute-start | bytes 1572872 | tf_op jit(solution)/shard_map/ppermute | solution.py:353
  86.1 14.1 %collective-permute-start.22 = (bf16[4,256,256]{2,1,0:T(8,128)(2,1)S(1)}, bf16[4,256,256]{2,1,0:T(8,128)(2,1)S(1)}, u32[]{:S(2)}, u32[]{:S(2)}) collective-permute-start(bf16[4,256,256]{2,1,0:T(8,128)(2,1)S(1)} %collective-permute-done.20.refs_5_.refs_1_), channel_id=1, source_target_pairs={{8,16},{12,20},{16,8},{20,12},{9,17},{13,21},{17,9},{21,13},{10,18... | collective-permute-start | bytes 1572872 | tf_op jit(solution)/shard_map/ppermute | solution.py:345
  88.3 17.3 %collective-permute-start.31 = (bf16[4,256,256]{2,1,0:T(8,128)(2,1)S(1)}, bf16[4,256,256]{2,1,0:T(8,128)(2,1)S(1)}, u32[]{:S(2)}, u32[]{:S(2)}) collective-permute-start(bf16[4,256,256]{2,1,0:T(8,128)(2,1)S(1)} %collective-permute-done.30.refs_5_), channel_id=1, source_target_pairs={{16,24},{20,28},{8,0},{12,4},{17,25},{21,29},{9,1},{13,5},{18,26},... | collective-permute-start | bytes 1572872 | tf_op jit(solution)/shard_map/ppermute | solution.py:345
  89.6 13.8 %collective-permute-start.25 = (bf16[2,512,128]{2,1,0:T(8,128)(2,1)S(1)}, bf16[2,512,128]{2,1,0:T(8,128)(2,1)S(1)}, u32[]{:S(2)}, u32[]{:S(2)}) collective-permute-start(bf16[2,512,128]{2,1,0:T(8,128)(2,1)S(1)} %gate.7), channel_id=1, source_target_pairs={{0,8},{4,12},{24,16},{28,20},{1,9},{5,13},{25,17},{29,21},{2,10},{... | collective-permute-start | bytes 786440 | tf_op jit(solution)/shard_map/ppermute | solution.py:345
  92.8 12.8 %collective-permute-start.29 = (bf16[512,256]{1,0:T(8,128)(2,1)S(1)}, bf16[512,256]{1,0:T(8,128)(2,1)S(1)}, u32[]{:S(2)}, u32[]{:S(2)}) collective-permute-start(bf16[512,256]{1,0:T(8,128)(2,1)S(1)} %get-tuple-element.69), channel_id=1, source_target_pairs={{0,4},{4,0},{8,12},{12,8},{16,20},{20,16},{24,28},{28,24},{1,5},{5... | collective-permute-start | bytes 786440 | tf_op jit(solution)/shard_map/ppermute | solution.py:350
  100.2 13.5 %collective-permute-start.23 = (bf16[4,256,256]{2,1,0:T(8,128)(2,1)S(1)}, bf16[4,256,256]{2,1,0:T(8,128)(2,1)S(1)}, u32[]{:S(2)}, u32[]{:S(2)}) collective-permute-start(bf16[4,256,256]{2,1,0:T(8,128)(2,1)S(1)} %collective-permute-done.22.refs_5_.refs_2_), channel_id=1, source_target_pairs={{16,24},{20,28},{8,0},{12,4},{17,25},{21,29},{9,1},{13,5},{18,26},... | collective-permute-start | bytes 1572872 | tf_op jit(solution)/shard_map/ppermute | solution.py:345
  102.8 10.9 %collective-permute-start.21 = (bf16[512,256]{1,0:T(8,128)(2,1)S(1)}, bf16[512,256]{1,0:T(8,128)(2,1)S(1)}, u32[]{:S(2)}, u32[]{:S(2)}) collective-permute-start(bf16[512,256]{1,0:T(8,128)(2,1)S(1)} %get-tuple-element.60), channel_id=1, source_target_pairs={{0,4},{4,0},{8,12},{12,8},{16,20},{20,16},{24,28},{28,24},{1,5},{5... | collective-permute-start | bytes 786440 | tf_op jit(solution)/shard_map/ppermute | solution.py:350
  103.4 12.0 %collective-permute-start.27 = (bf16[2,512,128]{2,1,0:T(8,128)(2,1)S(1)}, bf16[2,512,128]{2,1,0:T(8,128)(2,1)S(1)}, u32[]{:S(2)}, u32[]{:S(2)}) collective-permute-start(bf16[2,512,128]{2,1,0:T(8,128)(2,1)S(1)} %get-tuple-element.65), channel_id=1, source_target_pairs={{8,16},{12,20},{16,8},{20,12},{9,17},{13,21},{17,9},{21,13},{10,18... | collective-permute-start | bytes 786440 | tf_op jit(solution)/shard_map/ppermute | solution.py:345
  106.9 9.8 %collective-permute-start.32 = (bf16[512,256]{1,0:T(8,128)(2,1)S(1)}, bf16[512,256]{1,0:T(8,128)(2,1)S(1)}, u32[]{:S(2)}, u32[]{:S(2)}) collective-permute-start(bf16[512,256]{1,0:T(8,128)(2,1)S(1)} %get-tuple-element.71), channel_id=1, source_target_pairs={{0,4},{4,0},{8,12},{12,8},{16,20},{20,16},{24,28},{28,24},{1,5},{5... | collective-permute-start | bytes 786440 | tf_op jit(solution)/shard_map/ppermute | solution.py:350
  110.1 9.7 %collective-permute-start.26 = (bf16[2,512,128]{2,1,0:T(8,128)(2,1)S(1)}, bf16[2,512,128]{2,1,0:T(8,128)(2,1)S(1)}, u32[]{:S(2)}, u32[]{:S(2)}) collective-permute-start(bf16[2,512,128]{2,1,0:T(8,128)(2,1)S(1)} %get-tuple-element.64), channel_id=1, source_target_pairs={{8,16},{12,20},{16,8},{20,12},{9,17},{13,21},{17,9},{21,13},{10,18... | collective-permute-start | bytes 786440 | tf_op jit(solution)/shard_map/ppermute | solution.py:345
  114.8 6.4 %collective-permute-start.24 = (bf16[512,256]{1,0:T(8,128)(2,1)S(1)}, bf16[512,256]{1,0:T(8,128)(2,1)S(1)}, u32[]{:S(2)}, u32[]{:S(2)}) collective-permute-start(bf16[512,256]{1,0:T(8,128)(2,1)S(1)} %weigh.7.refs_4_.refs_1_), channel_id=1, source_target_pairs={{0,4},{4,0},{8,12},{12,8},{16,20},{20,16},{24,28},{28,24},{1,5},{5... | collective-permute-start | bytes 786440 | tf_op jit(solution)/shard_map/ppermute | solution.py:350
  115.4 5.9 %collective-permute-start.28 = (bf16[2,512,128]{2,1,0:T(8,128)(2,1)S(1)}, bf16[2,512,128]{2,1,0:T(8,128)(2,1)S(1)}, u32[]{:S(2)}, u32[]{:S(2)}) collective-permute-start(bf16[2,512,128]{2,1,0:T(8,128)(2,1)S(1)} %gate.9), channel_id=1, source_target_pairs={{16,24},{20,28},{8,0},{12,4},{17,25},{21,29},{9,1},{13,5},{18,26},... | collective-permute-start | bytes 786440 | tf_op jit(solution)/shard_map/ppermute | solution.py:345
